TPU v7x, 32 devices: a whole 2x2x4 slice. The times are simulated.
32 devices in a mesh: groups: 2 (over y), blk: 4 (over z), col: 4 (over x, core).
Axes of the slice: x: 2, y: 2, z: 4, core: 2. Of those that a mesh axis runs over, the one named last changes fastest.
Arguments:
- aic: float32 [256, 32768], P(('groups', 'blk'), 'col'), parts along dimension 0, may hold values from -0.03125 to 0.03125
- downwash: float32 [8, 8192, 384], P(('groups', 'col'), 'blk'), parts along dimension 0, may hold values from -6 to 6
- node_modes: float32 [6, 32, 192], P(None, 'blk'), may hold values from -0.4375 to 0.4375
- src_rows: int32 [4, 4, 4, 8], P('blk', 'col'), may hold values from 0 to 7
- dst_nodes: int32 [4, 4, 4, 8], P('blk', 'col'), may hold values from 0 to 7
- counts: int32 [4, 4, 4], P('blk', 'col'), may hold values from 0 to 8, as said below
- spline_weights: float32 [4, 4, 6, 4, 8], P('blk', 'col'), may hold values from -0.6 to 0.6
Outputs:
- gaf: float32 [384, 384], P('groups'), parts along dimension 0
There are 2 independent parts, one for each index of `groups`. A program takes and returns all parts, laid end to end along the dimension named above; an argument that names none is the same for every part. Nothing has to cross between parts.
Inputs may be any that keep to these rules, and one draw needn't show every extreme that they name: `counts`: slot s of a list is live when s < count; every source sub-block sends 8 live slots to its own owner, and one owner receives 8 live slots from every source sub-block. `src_rows`: rows within a sub-block of 8 rows. `dst_nodes`: nodes within an owner.
All inputs are finite; a program needn't handle non-finite values.
Results may differ from a plain program's by a relative error of at most 0.0003.
Values sent between devices are 32-bit elements; how exact they have to be, the bound alone decides.
No kernel may reach another device: no remote copies, remote signals or barrier semaphores. Data moves between devices by JAX's collectives and lax.ppermute only.
A program may use at most 64 MiB of HBM per device.

v0:
```python
import jax
import jax.numpy as jnp
from jax import lax
from jax.sharding import PartitionSpec as P


def shifted(value, axis, steps):
    count = lax.axis_size(axis)
    pairs = [(source, (source + steps) % count) for source in range(count)]
    return lax.ppermute(value, axis, pairs)


def shards(aic, downwash, node_modes, src_rows, dst_nodes, counts, spline_weights):
    cycle_size = lax.axis_size("blk")
    col_count = lax.axis_size("col")
    device = lax.axis_index("blk")
    own_block = downwash[0]
    panel_rows = own_block.shape[0]

    def product(shapes, source):
        columns = lax.dynamic_slice_in_dim(aic, source * panel_rows, panel_rows, 1)
        return jnp.dot(
            columns, shapes, precision=lax.Precision.HIGHEST, preferred_element_type=jnp.float32
        )

    halfway = cycle_size // 2

    def advance(offset, running):
        pressure, forward, behind = running
        forward = shifted(forward, "blk", 1)
        behind = shifted(behind, "blk", -1)
        pressure = pressure + product(forward, (device - offset) % cycle_size)
        pressure = pressure + product(behind, (device + offset) % cycle_size)
        return (pressure, forward, behind)

    pressure = product(own_block, device)
    pressure, forward, behind = lax.fori_loop(1, halfway, advance, (pressure, own_block, own_block))
    forward = shifted(forward, "blk", 1)
    pressure = pressure + product(forward, (device - halfway) % cycle_size)
    slots = src_rows.shape[-1]
    slot_index = jnp.arange(slots, dtype=jnp.int32)
    all_rows, all_nodes, all_counts = (
        lax.all_gather(src_rows, "col", axis=1, tiled=True),
        lax.all_gather(dst_nodes, "col", axis=1, tiled=True),
        lax.all_gather(counts, "col", axis=1, tiled=True),
    )
    weight_all = lax.all_gather(spline_weights, "col", axis=1, tiled=True)
    sub_rows = pressure.shape[0] // col_count
    offsets = jnp.arange(col_count, dtype=jnp.int32)[:, None, None] * sub_rows
    shifted_rows = all_rows[0] + offsets
    row_ids = jnp.transpose(shifted_rows, (1, 0, 2)).reshape(cycle_size, col_count * slots)
    node_ids = jnp.transpose(all_nodes[0], (1, 0, 2)).reshape(cycle_size, col_count * slots)
    live_sub = (slot_index[None, None, :] < all_counts[0][:, :, None]).astype(jnp.float32)
    live = jnp.transpose(live_sub, (1, 0, 2)).reshape(cycle_size, col_count * slots)
    weight_rows = jnp.transpose(weight_all[0], (1, 2, 0, 3)).reshape(
        6, cycle_size, col_count * slots
    )
    node_count = node_modes.shape[1]
    forces = pressure[row_ids.T]
    picks = (node_ids[None, :, :] == jnp.arange(node_count, dtype=jnp.int32)[:, None, None]).astype(
        jnp.float32
    )
    spread = weight_rows[:, None, :, :] * live[None, None, :, :] * picks[None, :, :, :]
    spread = spread.reshape(6 * node_count, cycle_size, row_ids.shape[1])
    arrived_forces, arrived_spread = (
        lax.all_to_all(forces, "blk", split_axis=1, concat_axis=1, tiled=True),
        lax.all_to_all(spread, "blk", split_axis=1, concat_axis=1, tiled=True),
    )
    loads = jnp.einsum(
        "jsc,csk->jk", arrived_spread, arrived_forces, precision=lax.Precision.HIGHEST
    )
    flat_modes = node_modes.reshape(6 * node_count, node_modes.shape[2])
    modal = jnp.einsum("jm,jk->mk", flat_modes, loads, precision=lax.Precision.HIGHEST)
    return lax.psum(modal, ("blk", "col"))


def solution(mesh):
    placed = (
        P(("groups", "blk"), "col"),
        P(("groups", "col"), "blk", None),
        P(None, "blk", None),
        P("blk", "col", None, None),
        P("blk", "col", None, None),
        P("blk", "col", None),
        P("blk", "col", None, None, None),
    )
    return jax.shard_map(
        shards, mesh=mesh, in_specs=placed, out_specs=P("groups", None), check_vma=False
    )
```

profile of v0, /device:TPU:0, one launch (start us, length us, event | category | flops | bytes accessed | tf_op | source)
XLA Modules:
  0.0 329.9 jit_solution(2935997758581484725)
XLA Ops:
  6.5 3.0 collective-permute-start
  9.6 2.0 collective-permute-start.1
  11.6 69.3 %collective-permute-done = f32[2048,384]{1,0:T(8,128)} collective-permute-done((f32[2048,384]{1,0:T(8,128)}, f32[2048,384]{1,0:T(8,128)}, u32[]{:S(2)}, u32[]{:S(2)}) %collective-permute-start) | collective-permute-done | bytes 3145760 | tf_op jit(solution)/shard_map/while/body/eval_jaxpr/ppermute | solution.py:10
  80.9 5.2 %all_gather.13 = s32[1,4,4]{2,0,1:T(1,128)S(1)} all-gather(s32[1,1,4]{2,0,1:T(1,128)} %bitcast.57), channel_id=1, replica_groups=mesh['groups'=2,'blk'=4,'col'=4] {'col'}, dimensions={1}, use_global_device_ids=true | all-gather | bytes 80 | tf_op jit(solution)/shard_map/all_gather | solution.py:45
  86.0 5.3 %all_gather.14 = s32[1,4,4,8]{3,2,0,1:T(4,128)S(1)} all-gather(s32[1,1,4,8]{3,2,0,1:T(4,128)} %bitcast.55), channel_id=1, replica_groups=mesh['groups'=2,'blk'=4,'col'=4] {'col'}, dimensions={1}, use_global_device_ids=true | all-gather | bytes 640 | tf_op jit(solution)/shard_map/all_gather | solution.py:44
  91.3 0.1 eq.24
  91.4 5.4 %all_gather.12 = f32[1,4,6,4,8]{4,3,2,0,1:T(4,128)S(1)} all-gather(f32[1,1,6,4,8]{4,3,2,0,1:T(4,128)} %bitcast.53), channel_id=1, replica_groups=mesh['groups'=2,'blk'=4,'col'=4] {'col'}, dimensions={1}, use_global_device_ids=true | all-gather | bytes 3840 | tf_op jit(solution)/shard_map/all_gather | solution.py:47
  96.9 0.1 broadcast_in_dim_reshape.2
  97.0 0.1 copy.31
  97.1 0.1 lt.72
  97.4 0.7 reshape.63
  98.2 69.1 %all-to-all-start = ((f32[4,1,1536]{2,1,0:T(1,128)}), f32[4,1,1536]{2,1,0:T(1,128)S(1)}, u32[]{:S(2)}, u32[]{:S(2)}) async-start(f32[4,1,1536]{2,1,0:T(1,128)} %reshape.63), calls=%async_computation | async-start | bytes 49152 | tf_op jit(solution)/shard_map/all_to_all | solution.py:67
  167.3 5.3 %all_gather.15 = s32[1,4,4,8]{3,2,0,1:T(4,128)S(1)} all-gather(s32[1,1,4,8]{3,2,0,1:T(4,128)} %bitcast.56), channel_id=1, replica_groups=mesh['groups'=2,'blk'=4,'col'=4] {'col'}, dimensions={1}, use_global_device_ids=true | all-gather | bytes 640 | tf_op jit(solution)/shard_map/all_gather | solution.py:43
  172.7 0.1 reshape.50
  172.8 0.1 copy.38
  172.9 0.1 reshape.54
  173.0 3.6 %fusion.3 = f32[32,384]{1,0:T(8,128)S(1)} fusion(f32[32,8192]{1,0:T(8,128)S(1)} %copy-done, s32[]{:T(128)S(6)} %select_n.35, f32[1,2048,384]{2,1,0:T(8,128)} %param.8), kind=kOutput, calls=%fused_computation.9 | convolution fusion | flops 301989888 | bytes 3457028 | tf_op jit(solution)/shard_map/dot_general | solution.py:22
  176.7 3.7 %convolution_add_fusion.2 = f32[32,384]{1,0:T(8,128)S(1)} fusion(f32[32,384]{1,0:T(8,128)S(1)} %fusion.3, f32[2048,384]{1,0:T(8,128)} %collective-permute-done, f32[32,8192]{1,0:T(8,128)S(1)} %copy-done, s32[]{:T(128)S(6)} %select_n.37), kind=kOutput, calls=%fused_computation.5 | convolution fusion | flops 302002176 | bytes 3506180 | tf_op jit(solution)/shard_map/while/body/eval_jaxpr/dot_general | solution.py:22
  180.4 3.6 %convolution_add_fusion.1 = f32[32,384]{1,0:T(8,128)S(1)} fusion(f32[32,384]{1,0:T(8,128)S(1)} %convolution_add_fusion.2, f32[2048,384]{1,0:T(8,128)} %collective-permute-done.1, f32[32,8192]{1,0:T(8,128)S(1)} %copy-done, s32[]{:T(128)S(6)} %select_n.39), kind=kOutput, calls=%fused_computation.4 | convolution fusion | flops 302002176 | bytes 3506180 | tf_op jit(solution)/shard_map/while/body/eval_jaxpr/dot_general | solution.py:22
  184.0 31.1 %collective-permute-done.2 = f32[2048,384]{1,0:T(8,128)} collective-permute-done((f32[2048,384]{1,0:T(8,128)}, f32[2048,384]{1,0:T(8,128)}, u32[]{:S(2)}, u32[]{:S(2)}) %collective-permute-start.2) | collective-permute-done | bytes 3145760 | tf_op jit(solution)/shard_map/ppermute | solution.py:10
  215.1 3.6 %convolution_add_fusion = f32[32,384]{1,0:T(8,128)S(1)} fusion(f32[32,384]{1,0:T(8,128)S(1)} %convolution_add_fusion.1, f32[2048,384]{1,0:T(8,128)} %collective-permute-done.2, f32[32,8192]{1,0:T(8,128)S(1)} %copy-done, s32[]{:T(128)S(6)} %select_n.41), kind=kOutput, calls=%fused_computation.3 | convolution fusion | flops 302002176 | bytes 3506180 | tf_op jit(solution)/shard_map/dot_general | solution.py:22
  218.8 0.8 gather_fusion
  219.6 0.7 copy.39
  220.3 3.4 %all-to-all-start.1 = ((f32[32,4,384]{2,0,1:T(8,128)}), f32[32,4,384]{2,0,1:T(8,128)S(1)}, u32[]{:S(2)}, u32[]{:S(2)}) async-start(f32[32,4,384]{2,0,1:T(8,128)} %copy.39), calls=%async_computation.1 | async-start | bytes 393216 | tf_op jit(solution)/shard_map/all_to_all | solution.py:66
  223.7 0.6 broadcast.44
  224.3 0.8 reduce
  225.1 0.1 reshape.64
  225.2 4.7 %all-to-all-done.1 = f32[32,4,384]{2,0,1:T(8,128)S(1)} async-done(((f32[32,4,384]{2,0,1:T(8,128)}), f32[32,4,384]{2,0,1:T(8,128)S(1)}, u32[]{:S(2)}, u32[]{:S(2)}) %all-to-all-start.1) | async-done | bytes 196640 | tf_op jit(solution)/shard_map/all_to_all | solution.py:66
  229.9 0.3 convolution_bitcast_fusion.1
  230.2 1.2 convolution_bitcast_fusion
  231.4 90.0 %all-reduce.2.cloned.1.call-done = f32[192,384]{1,0:T(8,128)} async-done(((f32[192,384]{1,0:T(8,128)}), f32[192,384]{1,0:T(8,128)}) %all-reduce.2.cloned.1.call-update) | async-done | bytes 294928 | tf_op jit(solution)/shard_map/psum | solution.py:74
  321.4 1.7 copy.41
  (27 shorter events, 0.5 us)
Async XLA Ops:
  6.5 166.5 %copy-start = (f32[32,8192]{1,0:T(8,128)S(1)}, f32[32,8192]{1,0:T(8,128)}, u32[]{:S(2)}) copy-start(f32[32,8192]{1,0:T(8,128)} %param.7) | copy-start | bytes 3145732
  6.5 74.3 %collective-permute-start = (f32[2048,384]{1,0:T(8,128)}, f32[2048,384]{1,0:T(8,128)}, u32[]{:S(2)}, u32[]{:S(2)}) collective-permute-start(f32[2048,384]{1,0:T(8,128)} %bitcast.45), channel_id=1, source_target_pairs={{0,4},{4,8},{8,12},{12,0},{1,5},{5,9},{9,13},{13,1},{2,6},{6,10},{... | collective-permute-start | bytes 9437192 | tf_op jit(solution)/shard_map/while/body/eval_jaxpr/ppermute | solution.py:10
  9.6 170.8 %collective-permute-start.1 = (f32[2048,384]{1,0:T(8,128)}, f32[2048,384]{1,0:T(8,128)}, u32[]{:S(2)}, u32[]{:S(2)}) collective-permute-start(f32[2048,384]{1,0:T(8,128)} %bitcast.46), channel_id=1, source_target_pairs={{0,12},{4,0},{8,4},{12,8},{1,13},{5,1},{9,5},{13,9},{2,14},{6,2},{... | collective-permute-start | bytes 9437192 | tf_op jit(solution)/shard_map/while/body/eval_jaxpr/ppermute | solution.py:10
  80.9 134.2 %collective-permute-start.2 = (f32[2048,384]{1,0:T(8,128)}, f32[2048,384]{1,0:T(8,128)}, u32[]{:S(2)}, u32[]{:S(2)}) collective-permute-start(f32[2048,384]{1,0:T(8,128)} %collective-permute-done), channel_id=1, source_target_pairs={{0,4},{4,8},{8,12},{12,0},{1,5},{5,9},{9,13},{13,1},{2,6},{6,10},{... | collective-permute-start | bytes 9437192 | tf_op jit(solution)/shard_map/ppermute | solution.py:10
  98.2 122.1 %all-to-all-start = ((f32[4,1,1536]{2,1,0:T(1,128)}), f32[4,1,1536]{2,1,0:T(1,128)S(1)}, u32[]{:S(2)}, u32[]{:S(2)}) async-start(f32[4,1,1536]{2,1,0:T(1,128)} %reshape.63), calls=%async_computation | async-start | bytes 49152 | tf_op jit(solution)/shard_map/all_to_all | solution.py:67
  184.0 46.2 %copy-start.1 = (f32[6,8,192]{2,1,0:T(8,128)S(1)}, f32[6,8,192]{2,1,0:T(8,128)}, u32[]{:S(2)}) copy-start(f32[6,8,192]{2,1,0:T(8,128)} %param.9) | copy-start | bytes 110596
  220.3 9.6 %all-to-all-start.1 = ((f32[32,4,384]{2,0,1:T(8,128)}), f32[32,4,384]{2,0,1:T(8,128)S(1)}, u32[]{:S(2)}, u32[]{:S(2)}) async-start(f32[32,4,384]{2,0,1:T(8,128)} %copy.39), calls=%async_computation.1 | async-start | bytes 393216 | tf_op jit(solution)/shard_map/all_to_all | solution.py:66
  223.7 97.7 %all-reduce.2.cloned.1.call-start = ((), (), s32[]{:S(2)}) async-start(), calls=%async_computation.2 | async-start | bytes 589824 | tf_op jit(solution)/shard_map/psum | solution.py:74
Sparse Core Ops, SparseCore 0:
  231.5 89.8 all-reduce.1
where the time goes:
time: 330 us
  waiting for transfers between devices  195 us (59%)
  starting transfers between devices  77.6 us (24%)
  blocking collectives  21.2 us (6%)
  matrix products  16 us (5%)
  between operations  13.6 us (4%)
  local copies, waits for them, and re-layouts  5.54 us (2%)
    ppermute x3, waiting for transfers between devices, shifted(): return lax.ppermute(value, axis, pairs)  100 us
    psum x1, waiting for transfers between devices, shards(): return lax.psum(modal, ('blk', 'col'))  90 us
    all_to_all x1, starting transfers between devices, shards(): lax.all_to_all(spread, 'blk', split_axis=1, concat_axis=1, tiled=True)  69.1 us
    dot_general x4, matrix products, product(): jnp.dot(columns, shapes, precision=lax.Precision.HIGHEST, preferred_eleme...  14.6 us
  transfers between devices with their start and end apart: 6, of which 4 were waited for; matrix products, arithmetic and copies ran while one was open for 6% of the time, Pallas kernels for 0%

commit v1 on v0

v1 whole, which is shorter than its diff:
```python
import jax
import jax.numpy as jnp
from jax import lax
from jax.sharding import PartitionSpec as P

HIGH = lax.Precision.HIGH


def swap(value, axis, mask):
    pairs = [(source, source ^ mask) for source in range(lax.axis_size(axis))]
    return lax.ppermute(value, axis, pairs)


def masks(axis):
    count, mask, found = lax.axis_size(axis), 1, []
    while mask < count:
        found.append(mask)
        mask *= 2
    return found


def gathered(value, axis):
    stack = value[None]
    for mask in masks(axis):
        stack = jnp.concatenate([stack, swap(stack, axis, mask)])
    return stack


def dot(left, right):
    return jnp.dot(left, right, precision=HIGH, preferred_element_type=jnp.float32)


def spline(src_rows, dst_nodes, counts, weights, sub_rows, node_count):
    slots = src_rows.shape[-1]
    live = jnp.arange(slots, dtype=jnp.int32) < counts[:, None]
    rows = jnp.arange(sub_rows, dtype=jnp.int32)[:, None, None] == src_rows
    rows = jnp.logical_and(rows, live).astype(jnp.float32)
    nodes = jnp.arange(node_count, dtype=jnp.int32)[:, None, None] == dst_nodes
    spread = weights[:, None] * nodes.astype(jnp.float32)
    matrix = jnp.sum(rows[:, None, None] * spread, axis=-1)
    return jnp.transpose(matrix, (0, 3, 1, 2)).reshape(sub_rows, -1)


def shards(aic, downwash, node_modes, src_rows, dst_nodes, counts, spline_weights):
    blk_count, col_count = lax.axis_size("blk"), lax.axis_size("col")
    blk, col = lax.axis_index("blk"), lax.axis_index("col")
    shapes = downwash[0]
    panels = shapes.shape[0]
    block_rows = aic.shape[0]
    sub_rows = block_rows // col_count
    dofs, node_count, modes = node_modes.shape

    def columns(mask):
        return lax.dynamic_slice_in_dim(aic, (blk ^ mask) * panels, panels, 1)

    order = sorted(range(1, blk_count), key=lambda mask: (mask < blk_count // 2, mask))
    arrived = {mask: swap(columns(mask), "blk", mask) for mask in order}
    arrived[0] = columns(0)
    pieces = jnp.stack([dot(arrived[mask], shapes) for mask in range(blk_count)])

    matrix = spline(
        src_rows[0, 0], dst_nodes[0, 0], counts[0, 0], spline_weights[0, 0], sub_rows, node_count
    )
    flat_modes = node_modes.reshape(dofs * node_count, modes)
    share = dofs * node_count // col_count
    modes_share = lax.dynamic_slice_in_dim(flat_modes, col * share, share, 0)
    natural_blk = blk ^ jnp.arange(blk_count, dtype=jnp.int32)
    natural_col = col ^ jnp.arange(col_count, dtype=jnp.int32)

    def everywhere(value):
        stack = gathered(gathered(value, "blk"), "col")
        return jnp.swapaxes(stack[natural_col], 0, 1)

    if matrix.shape[1] == modes:
        packed = everywhere(jnp.concatenate([modes_share, matrix]))
        all_modes = packed[natural_blk, :, :share].reshape(-1, modes)
        transfer = dot(packed[:, :, share:].reshape(-1, modes), all_modes)
    else:
        all_modes = everywhere(modes_share)[natural_blk].reshape(-1, modes)
        transfer = everywhere(dot(matrix, all_modes)).reshape(-1, modes)
    transfer = transfer.reshape(blk_count, block_rows, modes)

    half = block_rows // 2
    side = col % 2
    kept = lax.dynamic_slice_in_dim(pieces, side * half, half, 1)
    given = lax.dynamic_slice_in_dim(pieces, (1 - side) * half, half, 1)
    kept = kept + swap(given, "col", 1)
    for mask in masks("col")[1:]:
        kept = kept + swap(kept, "col", mask)
    for mask in masks("blk"):
        turned = kept[jnp.arange(blk_count) ^ mask]
        kept = kept + swap(turned, "blk", mask)
    other = swap(kept, "col", 1)
    first = lax.dynamic_slice_in_dim(transfer, side * half, half, 1)
    second = lax.dynamic_slice_in_dim(transfer, (1 - side) * half, half, 1)
    width = shapes.shape[1]
    return dot(first.reshape(-1, modes).T, kept.reshape(-1, width)) + dot(
        second.reshape(-1, modes).T, other.reshape(-1, width)
    )


def solution(mesh):
    placed = (
        P(("groups", "blk"), "col"),
        P(("groups", "col"), "blk", None),
        P(None, "blk", None),
        P("blk", "col", None, None),
        P("blk", "col", None, None),
        P("blk", "col", None),
        P("blk", "col", None, None, None),
    )
    return jax.shard_map(
        shards, mesh=mesh, in_specs=placed, out_specs=P("groups", None), check_vma=False
    )
```

time: 330 us -> 67.4 us (0.20)
  waiting for transfers between devices: 195 us -> 24.2 us
  starting transfers between devices: 77.6 us -> 14 us
  blocking collectives: 21.2 us -> 0 us
  between operations: 13.6 us -> 0.22 us
  local copies, waits for them, and re-layouts: 5.54 us -> 11.5 us
  other arithmetic: 0.87 us -> 6.77 us
  matrix products: 16 us -> 10.2 us
    psum x1 -> x0, waiting for transfers between devices: 90 us -> none  [shards(): return lax.psum(modal, ('blk', 'col'))]
    ppermute x3 -> x12, waiting for transfers between devices: 100 us -> 24.2 us  [swap(): return lax.ppermute(value, axis, pairs)]
    all_to_all x2 -> x0, starting transfers between devices: 72.5 us -> none  [the longest x1 69.1 us: shards(): lax.all_to_all(spread, 'blk', split_axis=1, concat_axis=1, tiled=True)]
    all_gather x4 -> x0, blocking collectives: 21.2 us -> none  [the longest x1 5.43 us: shards(): weight_all = lax.all_gather(spline_weights, 'col', axis=1, tiled=True)]
    ppermute x3 -> x12, starting transfers between devices: 5.05 us -> 14 us  [swap(): return lax.ppermute(value, axis, pairs)]
    dot_general x6 -> x7, matrix products: 16 us -> 10.2 us  [dot(): jnp.dot(left, right, precision=HIGH, preferred_element_type=jnp.float32)]
    all_to_all x2 -> x0, waiting for transfers between devices: 4.72 us -> none  [the longest x1 4.72 us: shards(): lax.all_to_all(forces, 'blk', split_axis=1, concat_axis=1, tiled=True)]
    gather x3 -> x5, local copies, waits for them, and re-layouts: 1.51 us -> 5.85 us  [the longest x2 2.39 us: shards(): all_modes = packed[natural_blk, :, :share].reshape(-1, modes)]
  transfers between devices with their start and end apart: 6 -> 12, of which waited for: 4 -> 5; matrix products, arithmetic and copies ran while one was open for 6% -> 36% of each run, Pallas kernels for 0% -> 0%
where the time goes in v1:
time: 67.4 us; the launch traced here: 66.9 us
  waiting for transfers between devices  24.2 us (36%)
  starting transfers between devices  14 us (21%)
  local copies, waits for them, and re-layouts  11.5 us (17%)
  matrix products  10.2 us (15%)
  other arithmetic  6.77 us (10%)
    ppermute x12, waiting for transfers between devices, swap(): return lax.ppermute(value, axis, pairs)  24.2 us
    ppermute x12, starting transfers between devices, swap(): return lax.ppermute(value, axis, pairs)  14 us
    dot_general x7, matrix products, dot(): jnp.dot(left, right, precision=HIGH, preferred_element_type=jnp.float32)  10.2 us
    concatenate x3, other arithmetic, gathered(): stack = jnp.concatenate([stack, swap(stack, axis, mask)])  2.47 us
    gather x2, local copies, waits for them, and re-layouts, shards(): all_modes = packed[natural_blk, :, :share].reshape(-1, modes)  2.39 us
    dynamic_slice x1, local copies, waits for them, and re-layouts, columns(): return lax.dynamic_slice_in_dim(aic, (blk ^ mask) * panels, panels, 1)  2.15 us
    gather x2, local copies, waits for them, and re-layouts, shards(): turned = kept[jnp.arange(blk_count) ^ mask]  1.75 us
    gather x1, local copies, waits for them, and re-layouts, everywhere(): return jnp.swapaxes(stack[natural_col], 0, 1)  1.71 us
  transfers between devices with their start and end apart: 12, of which 5 were waited for; matrix products, arithmetic and copies ran while one was open for 36% of the time, Pallas kernels for 0%

profile of v1, /device:TPU:0, one launch (start us, length us, event | category | flops | bytes accessed | tf_op | source)
XLA Modules:
  0.0 66.9 jit_solution(4079813618024600807)
XLA Ops:
  0.0 2.2 %constant_dynamic-slice_fusion.3 = (f32[32,2048]{1,0:T(8,128)}, f32[32,2048]{1,0:T(8,128)}, f32[32,2048]{1,0:T(8,128)}) fusion(f32[32,8192]{1,0:T(8,128)} %param.7, s32[]{:T(128)S(6)} %select_n.76, s32[]{:T(128)S(6)} %select_n.78, s32[]{:T(128)S(6)} %select_n.77), kind=kLoop, calls=%fused_computation.49 | loop fusion | bytes 1572876 | tf_op jit(solution)/shard_map/dynamic_slice | solution.py:54
  2.2 5.0 %collective-permute-start.6 = (f32[32,2048]{1,0:T(8,128)}, f32[32,2048]{1,0:T(8,128)}, u32[]{:S(2)}, u32[]{:S(2)}) collective-permute-start(f32[32,2048]{1,0:T(8,128)} %get-tuple-element.6), channel_id=1, source_target_pairs={{0,12},{4,8},{8,4},{12,0},{1,13},{5,9},{9,5},{13,1},{2,14},{6,10},... | collective-permute-start | bytes 786440 | tf_op jit(solution)/shard_map/ppermute | solution.py:11
  7.8 0.7 %fusion.29 = f32[8,4,8]{2,0,1:T(8,128)S(1)} fusion(s32[4,8]{1,0:T(4,128)} %bitcast.62), kind=kLoop, calls=%fused_computation.38 | loop fusion | flops 512 | bytes 1152 | tf_op jit(solution)/shard_map/convert_element_type | solution.py:39
  8.5 0.7 %iota_compare_fusion.2 = pred[4,8]{1,0:T(4,128)(4,1)S(1)} fusion(s32[4]{0:T(128)} %bitcast.64), kind=kLoop, calls=%fused_computation.54 | loop fusion | flops 32 | bytes 48 | tf_op jit(solution)/shard_map/lt | solution.py:35
  9.2 0.7 %broadcast_multiply_fusion = f32[6,8,4,8]{3,1,2,0:T(8,128)S(1)} fusion(f32[8,4,8]{2,0,1:T(8,128)S(1)} %fusion.29, f32[6,4,8]{2,1,0:T(4,128)} %bitcast.60), kind=kLoop, calls=%fused_computation.31 | loop fusion | flops 1536 | bytes 7936 | tf_op jit(solution)/shard_map/mul | solution.py:39
  9.9 0.7 %fusion.28 = f32[8,4,8]{2,1,0:T(4,128)S(1)} fusion(s32[4,8]{1,0:T(4,128)} %bitcast.63, pred[4,8]{1,0:T(4,128)(4,1)S(1)} %iota_compare_fusion.2), kind=kLoop, calls=%fused_computation.37 | loop fusion | flops 768 | bytes 1184 | tf_op jit(solution)/shard_map/convert_element_type | solution.py:37
  11.1 0.8 %constant_dynamic-slice_fusion.4 = f32[12,192]{1,0:T(8,128)S(1)} fusion(f32[48,192]{1,0:T(8,128)} %bitcast.61, s32[]{:T(128)S(6)} %select_n.70), kind=kLoop, calls=%fused_computation.53 | loop fusion | bytes 18436 | tf_op jit(solution)/shard_map/dynamic_slice | solution.py:66
  11.9 1.5 %collective-permute-start = (f32[1,20,192]{2,0,1:T(1,128)S(1)}, f32[1,20,192]{2,0,1:T(1,128)S(1)}, u32[]{:S(2)}, u32[]{:S(2)}) collective-permute-start(f32[1,20,192]{2,0,1:T(1,128)S(1)} %broadcast_in_dim.4), channel_id=1, source_target_pairs={{0,4},{4,0},{8,12},{12,8},{1,5},{5,1},{9,13},{13,9},{2,6},{6,2},{1... | collective-permute-start | bytes 46088 | tf_op jit(solution)/shard_map/ppermute | solution.py:11
  13.4 1.9 %fusion.9 = f32[1,32,384]{2,1,0:T(8,128)S(1)} fusion(f32[1,2048,384]{2,1,0:T(8,128)S(1)} %copy-done, f32[32,8192]{1,0:T(8,128)} %param.7, s32[]{:T(128)S(6)} %select_n.75), kind=kOutput, calls=%fused_computation.15 | convolution fusion | flops 150994944 | bytes 3457028 | tf_op jit(solution)/shard_map/dot_general | solution.py:30
  15.4 9.4 %collective-permute-done = f32[1,20,192]{2,0,1:T(1,128)S(1)} collective-permute-done((f32[1,20,192]{2,0,1:T(1,128)S(1)}, f32[1,20,192]{2,0,1:T(1,128)S(1)}, u32[]{:S(2)}, u32[]{:S(2)}) %collective-permute-start) | collective-permute-done | bytes 15392 | tf_op jit(solution)/shard_map/ppermute | solution.py:11
  24.8 1.4 %collective-permute-start.1 = (f32[2,20,192]{2,0,1:T(2,128)S(1)}, f32[2,20,192]{2,0,1:T(2,128)S(1)}, u32[]{:S(2)}, u32[]{:S(2)}) collective-permute-start(f32[2,20,192]{2,0,1:T(2,128)S(1)} %pad_maximum_fusion.3), channel_id=1, source_target_pairs={{0,8},{4,12},{8,0},{12,4},{1,9},{5,13},{9,1},{13,5},{2,10},{6,14},... | collective-permute-start | bytes 92168 | tf_op jit(solution)/shard_map/ppermute | solution.py:11
  26.2 4.9 %collective-permute-done.1 = f32[2,20,192]{2,0,1:T(2,128)S(1)} collective-permute-done((f32[2,20,192]{2,0,1:T(2,128)S(1)}, f32[2,20,192]{2,0,1:T(2,128)S(1)}, u32[]{:S(2)}, u32[]{:S(2)}) %collective-permute-start.1) | collective-permute-done | bytes 30752 | tf_op jit(solution)/shard_map/ppermute | solution.py:11
  31.2 1.9 %fusion.18 = f32[1,32,384]{2,1,0:T(8,128)S(1)} fusion(f32[32,2048]{1,0:T(8,128)} %collective-permute-done.6, f32[1,2048,384]{2,1,0:T(8,128)S(1)} %copy-done), kind=kOutput, calls=%fused_computation.18 | convolution fusion | flops 150994944 | bytes 3457024 | tf_op jit(solution)/shard_map/dot_general | solution.py:30
  33.1 1.9 %fusion.15 = f32[1,32,384]{2,1,0:T(8,128)S(1)} fusion(f32[32,2048]{1,0:T(8,128)} %collective-permute-done.5, f32[1,2048,384]{2,1,0:T(8,128)S(1)} %copy-done), kind=kOutput, calls=%fused_computation.17 | convolution fusion | flops 150994944 | bytes 3457024 | tf_op jit(solution)/shard_map/dot_general | solution.py:30
  35.1 1.9 %fusion.12 = f32[1,32,384]{2,1,0:T(8,128)S(1)} fusion(f32[32,2048]{1,0:T(8,128)} %collective-permute-done.4, f32[1,2048,384]{2,1,0:T(8,128)S(1)} %copy-done), kind=kOutput, calls=%fused_computation.16 | convolution fusion | flops 150994944 | bytes 3457024 | tf_op jit(solution)/shard_map/dot_general | solution.py:30
  37.6 0.7 %pad_maximum_fusion.2 = f32[2,4,20,192]{3,1,2,0:T(4,128)} fusion(f32[1,4,20,192]{3,1,2,0:T(4,128)S(1)} %collective-permute-done.2, f32[1,4,20,192]{3,1,2,0:T(4,128)S(1)} %maximum_bitcast_fusion), kind=kLoop, calls=%fused_computation.23 | loop fusion | flops 30720 | bytes 245760 | tf_op jit(solution)/shard_map/concatenate | solution.py:25
  38.3 1.5 %collective-permute-start.3 = (f32[2,4,20,192]{3,1,2,0:T(4,128)}, f32[2,4,20,192]{3,1,2,0:T(4,128)}, u32[]{:S(2)}, u32[]{:S(2)}) collective-permute-start(f32[2,4,20,192]{3,1,2,0:T(4,128)} %pad_maximum_fusion.2), channel_id=1, source_target_pairs={{0,2},{1,3},{2,0},{3,1},{4,6},{5,7},{6,4},{7,5},{8,10},{9,11},{10,... | collective-permute-start | bytes 368648 | tf_op jit(solution)/shard_map/ppermute | solution.py:11
  40.4 6.3 %collective-permute-done.8 = f32[4,16,384]{2,1,0:T(8,128)S(1)} collective-permute-done((f32[4,16,384]{2,1,0:T(8,128)S(1)}, f32[4,16,384]{2,1,0:T(8,128)S(1)}, u32[]{:S(2)}, u32[]{:S(2)}) %collective-permute-start.8) | collective-permute-done | bytes 98336 | tf_op jit(solution)/shard_map/ppermute | solution.py:11
  47.4 1.3 %collective-permute-start.9 = (f32[4,16,384]{2,1,0:T(8,128)S(1)}, f32[4,16,384]{2,1,0:T(8,128)S(1)}, u32[]{:S(2)}, u32[]{:S(2)}) collective-permute-start(f32[4,16,384]{2,1,0:T(8,128)S(1)} %gather_fusion.2), channel_id=1, source_target_pairs={{0,4},{4,0},{8,12},{12,8},{1,5},{5,1},{9,13},{13,9},{2,6},{6,2},{1... | collective-permute-start | bytes 294920 | tf_op jit(solution)/shard_map/ppermute | solution.py:11
  48.6 3.4 %collective-permute-done.9 = f32[4,16,384]{2,1,0:T(8,128)S(1)} collective-permute-done((f32[4,16,384]{2,1,0:T(8,128)S(1)}, f32[4,16,384]{2,1,0:T(8,128)S(1)}, u32[]{:S(2)}, u32[]{:S(2)}) %collective-permute-start.9) | collective-permute-done | bytes 98336 | tf_op jit(solution)/shard_map/ppermute | solution.py:11
  52.1 1.2 %gather_fusion.3 = f32[4,16,384]{2,1,0:T(8,128)} fusion(f32[4,16,384]{2,1,0:T(8,128)S(1)} %add.97, s32[1024]{0:T(1024)S(1)} %pad_clamp_fusion), kind=kCustom, calls=%fused_computation.3 | custom fusion | bytes 196624 | tf_op jit(solution)/shard_map/gather | solution.py:91
  53.3 1.5 %collective-permute-start.10 = (f32[4,16,384]{2,1,0:T(8,128)}, f32[4,16,384]{2,1,0:T(8,128)}, u32[]{:S(2)}, u32[]{:S(2)}) collective-permute-start(f32[4,16,384]{2,1,0:T(8,128)} %gather_fusion.3), channel_id=1, source_target_pairs={{0,8},{4,12},{8,0},{12,4},{1,9},{5,13},{9,1},{13,5},{2,10},{6,14},... | collective-permute-start | bytes 294920 | tf_op jit(solution)/shard_map/ppermute | solution.py:11
  54.7 1.7 %pad_maximum_fusion = f32[4,4,20,192]{3,1,2,0:T(4,128)} fusion(f32[2,4,20,192]{3,1,2,0:T(4,128)} %collective-permute-done.3, f32[1,4,20,192]{3,1,2,0:T(4,128)S(1)} %collective-permute-done.2, f32[1,4,20,192]{3,1,2,0:T(4,128)S(1)} %maximum_bitcast_fusion), kind=kLoop, calls=%fused_computation.20 | loop fusion | flops 122880 | bytes 491520 | tf_op jit(solution)/shard_map/concatenate | solution.py:25
  56.4 1.7 %gather_fusion = f32[4,4,20,192]{3,1,2,0:T(4,128)S(1)} fusion(f32[4,4,20,192]{3,1,2,0:T(4,128)} %pad_maximum_fusion, s32[1024]{0:T(1024)S(1)} %pad_clamp_fusion.2), kind=kCustom, calls=%fused_computation | custom fusion | bytes 491536 | tf_op jit(solution)/shard_map/gather | solution.py:72
  58.2 0.9 %copy.14 = f32[4,4,20,192]{3,1,0,2:T(4,128)} copy(f32[4,4,20,192]{3,0,2,1:T(4,128)S(1)} %bitcast.57) | data formatting | bytes 491520 | tf_op jit(solution)/shard_map/transpose | solution.py:72
  59.1 0.7 slice.12
  59.8 1.6 %gather_fusion.1 = f32[4,4,12,192]{3,1,2,0:T(4,128)S(1)} fusion(f32[4,4,20,192]{3,1,0,2:T(4,128)} %copy.14, s32[4]{0:T(128)S(1)} %fusion.36), kind=kCustom, calls=%fused_computation.1 | custom fusion | bytes 294944 | tf_op jit(solution)/shard_map/gather | solution.py:76
  61.4 0.7 %copy.15 = f32[4,4,12,192]{3,2,1,0:T(8,128)} copy(f32[4,4,12,192]{3,1,2,0:T(4,128)S(1)} %gather_fusion.1) | data formatting | bytes 294912 | tf_op jit(solution)/shard_map/gather | solution.py:76
  62.1 1.0 %reshape.148 = f32[192,192,1]{1,0,2:T(8,128)S(1)} reshape(f32[4,4,12,192]{3,2,1,0:T(8,128)} %copy.15) | data formatting | bytes 294912 | tf_op jit(solution)/shard_map/reshape | solution.py:76
  63.1 1.0 %add.99 = f32[4,16,384]{2,1,0:T(8,128)S(1)} add(f32[4,16,384]{2,1,0:T(8,128)} %copy-done.1, f32[4,16,384]{2,1,0:T(8,128)} %collective-permute-done.10) | non-fusion elementwise | flops 24576 | bytes 294912 | tf_op jit(solution)/shard_map/add | solution.py:92
  64.2 1.1 %fusion.22 = f32[4,32,192]{2,1,0:T(8,128)S(1)} fusion(f32[192,192,1]{1,0,2:T(8,128)S(1)} %reshape.148, f32[4,4,8,192]{3,0,2,1:T(4,128)} %slice.12), kind=kOutput, calls=%fused_computation.24 | convolution fusion | flops 28311552 | bytes 344064 | tf_op jit(solution)/shard_map/dot_general | solution.py:30
  65.8 1.1 %fusion.8 = f32[192,384]{1,0:T(8,128)} fusion(f32[192,384]{1,0:T(8,128)S(1)} %convolution_bitcast_fusion, f32[4,16,384]{2,1,0:T(8,128)S(1)} %add.99, f32[4,32,192]{2,1,0:T(8,128)S(1)} %fusion.22, s32[]{:T(128)S(6)} %select_n.74), kind=kOutput, calls=%fused_computation.14 | convolution fusion | flops 28385280 | bytes 753668 | tf_op jit(solution)/shard_map/dot_general | solution.py:30
  (39 shorter events, 3.7 us)
Async XLA Ops:
  0.0 13.4 %copy-start = (f32[1,2048,384]{2,1,0:T(8,128)S(1)}, f32[1,2048,384]{2,1,0:T(8,128)}, u32[]{:S(2)}) copy-start(f32[1,2048,384]{2,1,0:T(8,128)} %param.8) | copy-start | bytes 9437188
  2.2 29.0 %collective-permute-start.6 = (f32[32,2048]{1,0:T(8,128)}, f32[32,2048]{1,0:T(8,128)}, u32[]{:S(2)}, u32[]{:S(2)}) collective-permute-start(f32[32,2048]{1,0:T(8,128)} %get-tuple-element.6), channel_id=1, source_target_pairs={{0,12},{4,8},{8,4},{12,0},{1,13},{5,9},{9,5},{13,1},{2,14},{6,10},... | collective-permute-start | bytes 786440 | tf_op jit(solution)/shard_map/ppermute | solution.py:11
  7.2 25.9 %collective-permute-start.5 = (f32[32,2048]{1,0:T(8,128)}, f32[32,2048]{1,0:T(8,128)}, u32[]{:S(2)}, u32[]{:S(2)}) collective-permute-start(f32[32,2048]{1,0:T(8,128)} %get-tuple-element.7), channel_id=1, source_target_pairs={{0,8},{4,12},{8,0},{12,4},{1,9},{5,13},{9,1},{13,5},{2,10},{6,14},... | collective-permute-start | bytes 786440 | tf_op jit(solution)/shard_map/ppermute | solution.py:11
  7.2 27.9 %collective-permute-start.4 = (f32[32,2048]{1,0:T(8,128)}, f32[32,2048]{1,0:T(8,128)}, u32[]{:S(2)}, u32[]{:S(2)}) collective-permute-start(f32[32,2048]{1,0:T(8,128)} %get-tuple-element.5), channel_id=1, source_target_pairs={{0,4},{4,0},{8,12},{12,8},{1,5},{5,1},{9,13},{13,9},{2,6},{6,2},{1... | collective-permute-start | bytes 786440 | tf_op jit(solution)/shard_map/ppermute | solution.py:11
  11.9 12.9 %collective-permute-start = (f32[1,20,192]{2,0,1:T(1,128)S(1)}, f32[1,20,192]{2,0,1:T(1,128)S(1)}, u32[]{:S(2)}, u32[]{:S(2)}) collective-permute-start(f32[1,20,192]{2,0,1:T(1,128)S(1)} %broadcast_in_dim.4), channel_id=1, source_target_pairs={{0,4},{4,0},{8,12},{12,8},{1,5},{5,1},{9,13},{13,9},{2,6},{6,2},{1... | collective-permute-start | bytes 46088 | tf_op jit(solution)/shard_map/ppermute | solution.py:11
  24.8 6.2 %collective-permute-start.1 = (f32[2,20,192]{2,0,1:T(2,128)S(1)}, f32[2,20,192]{2,0,1:T(2,128)S(1)}, u32[]{:S(2)}, u32[]{:S(2)}) collective-permute-start(f32[2,20,192]{2,0,1:T(2,128)S(1)} %pad_maximum_fusion.3), channel_id=1, source_target_pairs={{0,8},{4,12},{8,0},{12,4},{1,9},{5,13},{9,1},{13,5},{2,10},{6,14},... | collective-permute-start | bytes 92168 | tf_op jit(solution)/shard_map/ppermute | solution.py:11
  31.1 6.5 %collective-permute-start.2 = (f32[1,4,20,192]{3,1,2,0:T(4,128)S(1)}, f32[1,4,20,192]{3,1,2,0:T(4,128)S(1)}, u32[]{:S(2)}, u32[]{:S(2)}) collective-permute-start(f32[1,4,20,192]{3,1,2,0:T(4,128)S(1)} %maximum_bitcast_fusion), channel_id=1, source_target_pairs={{0,1},{1,0},{2,3},{3,2},{4,5},{5,4},{6,7},{7,6},{8,9},{9,8},{10,11... | collective-permute-start | bytes 184328 | tf_op jit(solution)/shard_map/ppermute | solution.py:11
  37.1 2.8 %collective-permute-start.7 = (f32[4,16,384]{2,1,0:T(8,128)S(1)}, f32[4,16,384]{2,1,0:T(8,128)S(1)}, u32[]{:S(2)}, u32[]{:S(2)}) collective-permute-start(f32[4,16,384]{2,1,0:T(8,128)S(1)} %constant_dynamic-slice_fusion), channel_id=1, source_target_pairs={{0,1},{1,0},{2,3},{3,2},{4,5},{5,4},{6,7},{7,6},{8,9},{9,8},{10,11... | collective-permute-start | bytes 294920 | tf_op jit(solution)/shard_map/ppermute | solution.py:11
  38.3 16.4 %collective-permute-start.3 = (f32[2,4,20,192]{3,1,2,0:T(4,128)}, f32[2,4,20,192]{3,1,2,0:T(4,128)}, u32[]{:S(2)}, u32[]{:S(2)}) collective-permute-start(f32[2,4,20,192]{3,1,2,0:T(4,128)} %pad_maximum_fusion.2), channel_id=1, source_target_pairs={{0,2},{1,3},{2,0},{3,1},{4,6},{5,7},{6,4},{7,5},{8,10},{9,11},{10,... | collective-permute-start | bytes 368648 | tf_op jit(solution)/shard_map/ppermute | solution.py:11
  39.8 6.9 %collective-permute-start.8 = (f32[4,16,384]{2,1,0:T(8,128)S(1)}, f32[4,16,384]{2,1,0:T(8,128)S(1)}, u32[]{:S(2)}, u32[]{:S(2)}) collective-permute-start(f32[4,16,384]{2,1,0:T(8,128)S(1)} %dynamic-slice_add_fusion), channel_id=1, source_target_pairs={{0,2},{1,3},{2,0},{3,1},{4,6},{5,7},{6,4},{7,5},{8,10},{9,11},{10,... | collective-permute-start | bytes 294920 | tf_op jit(solution)/shard_map/ppermute | solution.py:11
  47.4 4.7 %collective-permute-start.9 = (f32[4,16,384]{2,1,0:T(8,128)S(1)}, f32[4,16,384]{2,1,0:T(8,128)S(1)}, u32[]{:S(2)}, u32[]{:S(2)}) collective-permute-start(f32[4,16,384]{2,1,0:T(8,128)S(1)} %gather_fusion.2), channel_id=1, source_target_pairs={{0,4},{4,0},{8,12},{12,8},{1,5},{5,1},{9,13},{13,9},{2,6},{6,2},{1... | collective-permute-start | bytes 294920 | tf_op jit(solution)/shard_map/ppermute | solution.py:11
  52.0 2.7 %copy-start.1 = (f32[4,16,384]{2,1,0:T(8,128)}, f32[4,16,384]{2,1,0:T(8,128)S(1)}, u32[]{:S(2)}) copy-start(f32[4,16,384]{2,1,0:T(8,128)S(1)} %add.97) | copy-start | bytes 294916
  53.3 9.9 %collective-permute-start.10 = (f32[4,16,384]{2,1,0:T(8,128)}, f32[4,16,384]{2,1,0:T(8,128)}, u32[]{:S(2)}, u32[]{:S(2)}) collective-permute-start(f32[4,16,384]{2,1,0:T(8,128)} %gather_fusion.3), channel_id=1, source_target_pairs={{0,8},{4,12},{8,0},{12,4},{1,9},{5,13},{9,1},{13,5},{2,10},{6,14},... | collective-permute-start | bytes 294920 | tf_op jit(solution)/shard_map/ppermute | solution.py:11
  64.1 1.4 %collective-permute-start.11 = (f32[4,16,384]{2,1,0:T(8,128)S(1)}, f32[4,16,384]{2,1,0:T(8,128)S(1)}, u32[]{:S(2)}, u32[]{:S(2)}) collective-permute-start(f32[4,16,384]{2,1,0:T(8,128)S(1)} %add.99), channel_id=1, source_target_pairs={{0,1},{1,0},{2,3},{3,2},{4,5},{5,4},{6,7},{7,6},{8,9},{9,8},{10,11... | collective-permute-start | bytes 294920 | tf_op jit(solution)/shard_map/ppermute | solution.py:11

commit v2 on v1

--- a/solution.py
+++ b/solution.py
@@ -1,9 +1,18 @@
+import functools
+
 import jax
 import jax.numpy as jnp
 from jax import lax
+from jax.experimental import pallas as pl
+from jax.experimental.pallas import tpu as pltpu
 from jax.sharding import PartitionSpec as P
 
 HIGH = lax.Precision.HIGH
+HIGHEST = lax.Precision.HIGHEST
+VMEM = pl.BlockSpec(memory_space=pltpu.VMEM)
+SMEM = pl.BlockSpec(memory_space=pltpu.SMEM)
+ANY = pl.BlockSpec(memory_space=pl.ANY)
+ROOM = pltpu.CompilerParams(vmem_limit_bytes=32 * 1024 * 1024)
 
 
 def swap(value, axis, mask):
@@ -41,7 +50,7 @@
     return jnp.transpose(matrix, (0, 3, 1, 2)).reshape(sub_rows, -1)
 
 
-def shards(aic, downwash, node_modes, src_rows, dst_nodes, counts, spline_weights):
+def by_parts(aic, downwash, node_modes, src_rows, dst_nodes, counts, spline_weights):
     blk_count, col_count = lax.axis_size("blk"), lax.axis_size("col")
     blk, col = lax.axis_index("blk"), lax.axis_index("col")
     shapes = downwash[0]
@@ -99,6 +108,278 @@
     )
 
 
+def cost(microseconds):
+    return pl.CostEstimate(flops=0, bytes_accessed=int(microseconds * 3.5e6), transcendentals=0)
+
+
+def after(value, *others):
+    return lax.optimization_barrier((value, *others))[0]
+
+
+def f32(*shape):
+    return jax.ShapeDtypeStruct(shape, jnp.float32)
+
+
+def cut_kernel(pieces, aic, *refs):
+    outs, sems = refs[:-1], refs[-1]
+    blk = lax.axis_index("blk")
+    copies = []
+    for at, (mask, first, rows) in enumerate(pieces):
+        panels = outs[at].shape[1]
+        start = pl.multiple_of((blk ^ mask) * panels, 128)
+        source = aic.at[pl.ds(first, rows), pl.ds(start, panels)]
+        copies.append(pltpu.make_async_copy(source, outs[at], sems.at[at]))
+        copies[-1].start()
+    for copy in copies:
+        copy.wait()
+
+
+def cut_out(aic, panels, pieces):
+    return pl.pallas_call(
+        functools.partial(cut_kernel, pieces),
+        out_shape=[f32(rows, panels) for _, _, rows in pieces],
+        in_specs=[ANY],
+        out_specs=[VMEM] * len(pieces),
+        scratch_shapes=[pltpu.SemaphoreType.DMA((len(pieces),))],
+        cost_estimate=cost(2),
+    )(aic)
+
+
+def spline_kernel(src_rows, dst_nodes, counts, weights, modes, pack):
+    owners, slots = src_rows.shape[2:]
+    dofs, node_count, width = modes.shape
+    sub_rows = pack.shape[0] - dofs * node_count // lax.axis_size("col")
+    shape = (sub_rows, owners * dofs * node_count)
+    row = lax.broadcasted_iota(jnp.int32, shape, 0)
+    place = lax.broadcasted_iota(jnp.int32, shape, 1)
+    total = jnp.zeros(shape, jnp.float32)
+    for owner in range(owners):
+        live = counts[0, 0, owner]
+        for slot in range(slots):
+            node = owner * dofs * node_count + dst_nodes[0, 0, owner, slot]
+            term = jnp.zeros(shape, jnp.float32)
+            for dof in range(dofs):
+                term = jnp.where(place == node + dof * node_count, weights[0, 0, dof, owner, slot], term)
+            here = jnp.where(slot < live, src_rows[0, 0, owner, slot], -1)
+            total = total + jnp.where(row == here, term, 0.0)
+    pack[:sub_rows, :] = total
+    flat = modes[...].reshape(dofs * node_count, width)
+    share = dofs * node_count // lax.axis_size("col")
+    col = lax.axis_index("col")
+    for turn in range(lax.axis_size("col")):
+
+        @pl.when(col == turn)
+        def _():
+            pack[sub_rows:, :] = flat[turn * share : (turn + 1) * share]
+
+
+def transfer_kernel(sub_rows, packs, high, low, modes, spread):
+    cols, blk_count = packs.shape[:2]
+    blk, col = lax.axis_index("blk"), lax.axis_index("col")
+    share = packs.shape[2] - sub_rows
+    half = blk_count // 2
+    quarter = cols // 2
+    own = blk // half * half
+    bits = cols.bit_length() - 1
+
+    def entry(place):
+        mask = col ^ place
+        return sum(((mask >> bit) & 1) << (bits - 1 - bit) for bit in range(bits))
+
+    for b in range(blk_count):
+        for c in range(cols):
+            at = (b * cols + c) * share
+            modes[at : at + share, :] = packs[entry(c), blk ^ b, sub_rows:, :]
+    at = 0
+    for turn in range(2):
+        for b in range(blk_count):
+            block = own + b if b < half else half - own + b - half
+            for c in range(quarter):
+                place = (lax.rem(col, 2) ^ turn) * quarter + c
+                spread[at : at + sub_rows, :] = packs[entry(place), blk ^ block, :sub_rows, :]
+                at += sub_rows
+    whole = lax.dot_general(
+        modes[...], spread[...], (((0,), (1,)), ((), ())), precision=HIGHEST,
+        preferred_element_type=jnp.float32,
+    )
+    high[...], low[...] = split(whole)
+
+
+def last_kernel(high, low, total, other, out):
+    right_high, right_low = split(jnp.concatenate([total[...], other[...]]))
+    out[...] = mxu(high[...], right_high) + (mxu(high[...], right_low) + mxu(low[...], right_high))
+
+
+def split(value):
+    high = value.astype(jnp.bfloat16)
+    return high, (value - high.astype(jnp.float32)).astype(jnp.bfloat16)
+
+
+def mxu(left, right):
+    return jnp.dot(left, right, preferred_element_type=jnp.float32)
+
+
+def halves_kernel(shapes, high, low, buffer, sems):
+    steps = buffer.shape[0]
+    rows = buffer.shape[1]
+    copies = [
+        pltpu.make_async_copy(shapes.at[pl.ds(step * rows, rows), :], buffer.at[step], sems.at[step])
+        for step in range(steps)
+    ]
+    for copy in copies:
+        copy.start()
+    for step, copy in enumerate(copies):
+        copy.wait()
+        at = pl.ds(step * rows, rows)
+        high[at, :], low[at, :] = split(buffer[step])
+
+
+def halves(shapes, steps):
+    rows = shapes.shape[0] // steps
+    return pl.pallas_call(
+        halves_kernel,
+        out_shape=[jax.ShapeDtypeStruct(shapes.shape, jnp.bfloat16)] * 2,
+        in_specs=[ANY],
+        out_specs=[VMEM] * 2,
+        scratch_shapes=[
+            pltpu.VMEM((steps, rows, shapes.shape[1]), jnp.float32),
+            pltpu.SemaphoreType.DMA((steps,)),
+        ],
+        compiler_params=ROOM,
+        cost_estimate=cost(1),
+    )(shapes)
+
+
+def product(pieces, high, low):
+    rows = [split(piece[...]) for piece in pieces]
+    left_high = jnp.concatenate([r[0] for r in rows])
+    left_low = jnp.concatenate([r[1] for r in rows])
+    size = left_high.shape[0]
+    both = mxu(jnp.concatenate([left_high, left_low]), high[...])
+    return both[:size] + both[size:] + mxu(left_high, low[...])
+
+
+def early_kernel(*refs):
+    *pieces, high, low, out = refs
+    out[...] = product(pieces, high, low).reshape(out.shape)
+
+
+def late_kernel(groups, *refs):
+    *pieces, early, high, low, kept, given, total = refs
+    done = early.shape[0]
+    total[:done] = early[...]
+    total[done:] = product(pieces, high, low).reshape(total[done:].shape)
+    blk, core = lax.axis_index("blk"), lax.rem(lax.axis_index("col"), 2)
+    half = total.shape[1] // 2
+    at = first = 0
+    for group in groups:
+        for index in range(group):
+            source = first + ((blk & (group - 1)) ^ index)
+            kept[at : at + half, :] = total[source, pl.ds(pl.multiple_of(core * half, 8), half), :]
+            given[at : at + half, :] = total[source, pl.ds(pl.multiple_of((1 - core) * half, 8), half), :]
+            at += half
+        first += group
+
+
+def early_products(pieces, high, low):
+    return pl.pallas_call(
+        early_kernel,
+        out_shape=f32(len(pieces), pieces[0].shape[0], high.shape[1]),
+        in_specs=[VMEM] * (len(pieces) + 2),
+        out_specs=VMEM,
+        compiler_params=ROOM,
+        cost_estimate=cost(1),
+    )(*pieces, high, low)
+
+
+def late_products(groups, pieces, early, high, low):
+    count, (rows, width) = sum(groups), early.shape[1:]
+    return pl.pallas_call(
+        functools.partial(late_kernel, groups),
+        out_shape=[f32(rows * count // 2, width)] * 2,
+        in_specs=[VMEM] * (len(pieces) + 3),
+        out_specs=[VMEM] * 2,
+        scratch_shapes=[pltpu.VMEM((count, rows, width), jnp.float32)],
+        compiler_params=ROOM,
+        cost_estimate=cost(0.1),
+    )(*pieces, early, high, low)
+
+
+def shards(aic, downwash, node_modes, src_rows, dst_nodes, counts, spline_weights):
+    blk_count, col_count = lax.axis_size("blk"), lax.axis_size("col")
+    shapes = downwash[0]
+    panels, width = shapes.shape
+    block_rows = aic.shape[0]
+    sub_rows = block_rows // col_count
+    dofs, node_count, modes = node_modes.shape
+    loads = blk_count * dofs * node_count
+    half = blk_count // 2
+
+    share = dofs * node_count // col_count
+    blk = lax.axis_index("blk")
+
+    def columns(mask, source=aic):
+        return lax.dynamic_slice_in_dim(source, (blk ^ mask) * panels, panels, 1)
+
+    far_masks = list(range(half, blk_count))
+    near = [columns(mask) for mask in range(1, half)]
+    far = [columns(mask) for mask in far_masks]
+    rest, lists, shapes, *cuts = lax.optimization_barrier((aic, src_rows, shapes, *near, *far))
+    near, far = cuts[: half - 1], cuts[half - 1 :]
+    near = [swap(piece, "blk", mask + 1) for mask, piece in enumerate(near)]
+    far[:-1] = [swap(piece, "blk", mask) for mask, piece in zip(far_masks, far[:-1])]
+    near = [columns(0, rest), *near]
+    high, low = halves(shapes, 4)
+
+    pack = pl.pallas_call(
+        spline_kernel,
+        out_shape=f32(sub_rows + share, modes),
+        in_specs=[SMEM] * 4 + [VMEM],
+        out_specs=VMEM,
+        cost_estimate=cost(1),
+    )(lists, dst_nodes, counts, spline_weights, node_modes)
+    far[-1] = swap(after(far[-1], pack), "blk", far_masks[-1])
+    packs = [pack] + [swap(pack, "blk", mask) for mask in range(1, blk_count)]
+    waiting = lax.optimization_barrier((*packs, *near, *far[:-1]))
+    packs, near, far[:-1] = waiting[:blk_count], waiting[blk_count : blk_count + half], waiting[blk_count + half :]
+    packs = jnp.stack(packs)[None]
+    col_masks = masks("col")
+    for mask in col_masks[:0:-1]:
+        packs = jnp.concatenate([packs, swap(packs, "col", mask)])
+    packs, high = lax.optimization_barrier((packs, high))
+    early = early_products([*near, *far[:-1]], high, low)
+    total, given = late_products((half, half), far[-1:], early, high, low)
+    packs = jnp.concatenate([packs, swap(packs, "col", 1)])
+    given = swap(given, "col", 1)
+    total = total + given
+    for mask in masks("col")[1:]:
+        total = total + swap(total, "col", mask)
+    for mask in masks("blk")[:-1]:
+        total = total + swap(total, "blk", mask)
+    there = swap(total, "blk", half)
+    transfer = pl.pallas_call(
+        functools.partial(transfer_kernel, sub_rows),
+        out_shape=[jax.ShapeDtypeStruct((modes, blk_count * block_rows), jnp.bfloat16)] * 2,
+        in_specs=[VMEM],
+        out_specs=[VMEM] * 2,
+        scratch_shapes=[
+            pltpu.VMEM((loads, modes), jnp.float32),
+            pltpu.VMEM((blk_count * block_rows, loads), jnp.float32),
+        ],
+        cost_estimate=cost(3),
+    )(packs)
+    there, *transfer = lax.optimization_barrier((there, *transfer))
+    rows = total.shape[0] // 2
+    total = total + jnp.concatenate([there[rows:], there[:rows]])
+    other = swap(total, "col", 1)
+    return pl.pallas_call(
+        last_kernel,
+        out_shape=f32(modes, width),
+        in_specs=[VMEM] * 4,
+        compiler_params=ROOM,
+    )(*transfer, total, other)
+
+
 def solution(mesh):
     placed = (
         P(("groups", "blk"), "col"),
@@ -109,6 +390,12 @@
         P("blk", "col", None),
         P("blk", "col", None, None, None),
     )
-    return jax.shard_map(
-        shards, mesh=mesh, in_specs=placed, out_specs=P("groups", None), check_vma=False
-    )
+
+    def program(*arrays):
+        dofs, nodes, modes = arrays[2].shape
+        body = shards if dofs * nodes == modes else by_parts
+        return jax.shard_map(
+            body, mesh=mesh, in_specs=placed, out_specs=P("groups", None), check_vma=False
+        )(*arrays)
+
+    return program

time: 67.4 us -> 52.7 us (0.78)
  matrix products: 10.2 us -> 0 us
  waiting for transfers between devices: 24.2 us -> 15.2 us
  starting transfers between devices: 14 us -> 22.8 us
  Pallas kernels: 0 us -> 6.93 us
  local copies, waits for them, and re-layouts: 11.5 us -> 5.62 us
  other arithmetic: 6.77 us -> 1.61 us
    dot_general x7 -> x0, matrix products: 10.2 us -> none  [dot(): jnp.dot(left, right, precision=HIGH, preferred_element_type=jnp.float32)]
    ppermute x12 -> x13, waiting for transfers between devices: 24.2 us -> 15.2 us  [swap(): return lax.ppermute(value, axis, pairs)]
    ppermute x12 -> x13, starting transfers between devices: 14 us -> 22.8 us  [swap(): return lax.ppermute(value, axis, pairs)]
    pallas_call x0 -> x6, Pallas kernels: none -> 6.93 us  [the longest x1 2.02 us: shards(): pl.pallas_call(functools.partial(transfer_kernel, sub_rows), out_shape=[j...]
    gather x5 -> x0, local copies, waits for them, and re-layouts: 5.85 us -> none  [the longest x2 2.39 us: shards(): all_modes = packed[natural_blk, :, :share].reshape(-1, modes)]
    unnamed x4 -> x6, local copies, waits for them, and re-layouts: 0.01 us -> 3.49 us
    concatenate x5 -> x2, other arithmetic: 2.49 us -> 0.8 us  [the longest x1 0.78 us: shards(): packs = jnp.concatenate([packs, swap(packs, 'col', 1)])]
    convert_element_type x2 -> x0, other arithmetic: 1.37 us -> none  [the longest x1 0.69 us: spline(): rows = jnp.logical_and(rows, live).astype(jnp.float32)]
  transfers between devices with their start and end apart: 12 -> 13, of which waited for: 5 -> 7; matrix products, arithmetic and copies ran while one was open for 36% -> 5% of each run, Pallas kernels for 0% -> 10%
where the time goes in v2:
time: 52.7 us; the launch traced here: 52.2 us
  starting transfers between devices  22.8 us (43%)
  waiting for transfers between devices  15.2 us (29%)
  Pallas kernels  6.93 us (13%)
  local copies, waits for them, and re-layouts  5.62 us (11%)
  other arithmetic  1.61 us (3%)
    ppermute x13, starting transfers between devices, swap(): return lax.ppermute(value, axis, pairs)  22.8 us
    ppermute x13, waiting for transfers between devices, swap(): return lax.ppermute(value, axis, pairs)  15.2 us
    unnamed x6, local copies, waits for them, and re-layouts  3.49 us
    dynamic_slice x2, local copies, waits for them, and re-layouts, columns(): return lax.dynamic_slice_in_dim(source, (blk ^ mask) * panels, panels, 1)  2.13 us
    pallas_call x1, Pallas kernels, shards(): pl.pallas_call(functools.partial(transfer_kernel, sub_rows), out_shape=[j...  2.02 us
    pallas_call x1, Pallas kernels, shards(): pl.pallas_call(spline_kernel, out_shape=f32(sub_rows + share, modes), in_...  1.83 us
  transfers between devices with their start and end apart: 13, of which 7 were waited for; matrix products, arithmetic and copies ran while one was open for 5% of the time, Pallas kernels for 10%

profile of v2, /device:TPU:0, one launch (start us, length us, event | category | flops | bytes accessed | tf_op | source)
XLA Modules:
  0.0 52.2 jit_solution(13907276570695743113)
XLA Ops:
  0.0 1.2 %constant_dynamic-slice_fusion.1 = (f32[32,2048]{1,0:T(8,128)S(1)}, f32[32,2048]{1,0:T(8,128)S(1)}, f32[32,2048]{1,0:T(8,128)S(1)}) fusion(f32[32,8192]{1,0:T(8,128)} %param.7, s32[]{:T(128)S(6)} %select_n.14, s32[]{:T(128)S(6)} %select_n.13, s32[]{:T(128)S(6)} %select_n.12), kind=kLoop, calls=%fused_computation.5 | loop fusion | bytes 1572876 | tf_op jit(solution)/shard_map/dynamic_slice | solution.py:322
  1.2 3.1 %collective-permute-start.4 = (f32[32,2048]{1,0:T(8,128)S(1)}, f32[32,2048]{1,0:T(8,128)S(1)}, u32[]{:S(2)}, u32[]{:S(2)}) collective-permute-start(f32[32,2048]{1,0:T(8,128)S(1)} %get-tuple-element.34), channel_id=1, source_target_pairs={{0,4},{4,0},{8,12},{12,8},{1,5},{5,1},{9,13},{13,9},{2,6},{6,2},{1... | collective-permute-start | bytes 786440 | tf_op jit(solution)/shard_map/ppermute | solution.py:20
  4.3 2.6 %collective-permute-start.5 = (f32[32,2048]{1,0:T(8,128)S(1)}, f32[32,2048]{1,0:T(8,128)S(1)}, u32[]{:S(2)}, u32[]{:S(2)}) collective-permute-start(f32[32,2048]{1,0:T(8,128)S(1)} %get-tuple-element.35), channel_id=1, source_target_pairs={{0,8},{4,12},{8,0},{12,4},{1,9},{5,13},{9,1},{13,5},{2,10},{6,14},... | collective-permute-start | bytes 786440 | tf_op jit(solution)/shard_map/ppermute | solution.py:20
  6.8 1.8 %shard_map.73 = f32[20,192]{1,0:T(8,128)} custom-call(s32[1,1,4,8]{3,2,1,0:T(4,128)} %src_rows, s32[1,1,4,8]{3,2,1,0:T(4,128)} %dst_nodes.1, s32[1,1,4]{2,1,0:T(1,128)} %counts.1, f32[1,1,6,4,8]{4,3,2,1,0:T(4,128)} %weights.1, f32[6,8,192]{2,1,0:T(8,128)} %modes.1), custom_call_target="tpu_custom_call" | custom-call | bytes 3500000 | tf_op jit(solution)/shard_map/pallas_call | solution.py:334
  8.7 1.9 %collective-permute-start.2 = (f32[20,192]{1,0:T(8,128)}, f32[20,192]{1,0:T(8,128)S(1)}, u32[]{:S(2)}, u32[]{:S(2)}) collective-permute-start(f32[20,192]{1,0:T(8,128)} %shard_map.73), channel_id=1, source_target_pairs={{0,8},{4,12},{8,0},{12,4},{1,9},{5,13},{9,1},{13,5},{2,10},{6,14},... | collective-permute-start | bytes 46088 | tf_op jit(solution)/shard_map/ppermute | solution.py:20
  10.6 2.5 %collective-permute-start.1 = (f32[20,192]{1,0:T(8,128)}, f32[20,192]{1,0:T(8,128)S(1)}, u32[]{:S(2)}, u32[]{:S(2)}) collective-permute-start(f32[20,192]{1,0:T(8,128)} %shard_map.73), channel_id=1, source_target_pairs={{0,4},{4,0},{8,12},{12,8},{1,5},{5,1},{9,13},{13,9},{2,6},{6,2},{1... | collective-permute-start | bytes 46088 | tf_op jit(solution)/shard_map/ppermute | solution.py:20
  13.1 1.0 %constant_dynamic-slice_fusion.refs_0_ = f32[32,2048]{1,0:T(8,128)S(1)} fusion(f32[32,8192]{1,0:T(8,128)} %param.7, s32[]{:T(128)S(6)} %select_n.15), kind=kLoop, calls=%fused_computation.4 | loop fusion | bytes 524292 | tf_op jit(solution)/shard_map/dynamic_slice | solution.py:322
  14.0 5.4 %collective-permute-done.3 = f32[20,192]{1,0:T(8,128)S(1)} collective-permute-done((f32[20,192]{1,0:T(8,128)}, f32[20,192]{1,0:T(8,128)S(1)}, u32[]{:S(2)}, u32[]{:S(2)}) %collective-permute-start.3) | collective-permute-done | bytes 15392 | tf_op jit(solution)/shard_map/ppermute | solution.py:20
  19.5 1.3 %collective-permute-start = (f32[32,2048]{1,0:T(8,128)S(1)}, f32[32,2048]{1,0:T(8,128)S(1)}, u32[]{:S(2)}, u32[]{:S(2)}) collective-permute-start(f32[32,2048]{1,0:T(8,128)S(1)} %get-tuple-element.32), channel_id=1, source_target_pairs={{0,12},{4,8},{8,4},{12,0},{1,13},{5,9},{9,5},{13,1},{2,14},{6,10},... | collective-permute-start | bytes 786440 | tf_op jit(solution)/shard_map/ppermute | solution.py:20
  20.8 0.8 %maximum_bitcast_fusion = f32[1,4,20,192]{3,2,1,0:T(8,128)S(1)} fusion(f32[1,20,192]{2,1,0:T(8,128)S(1)} %bitcast.9, f32[1,20,192]{2,1,0:T(8,128)S(1)} %bitcast.10, f32[1,20,192]{2,1,0:T(8,128)S(1)} %bitcast.11, f32[1,20,192]{2,1,0:T(8,128)} %bitcast.8), kind=kLoop, calls=%fused_computation.2 | loop fusion | flops 46080 | bytes 122880 | tf_op jit(solution)/shard_map/broadcast_in_dim | solution.py:345
  21.6 1.6 %collective-permute-start.6 = (f32[1,4,20,192]{3,2,1,0:T(8,128)S(1)}, f32[1,4,20,192]{3,2,1,0:T(8,128)S(1)}, u32[]{:S(2)}, u32[]{:S(2)}) collective-permute-start(f32[1,4,20,192]{3,2,1,0:T(8,128)S(1)} %maximum_bitcast_fusion), channel_id=1, source_target_pairs={{0,2},{1,3},{2,0},{3,1},{4,6},{5,7},{6,4},{7,5},{8,10},{9,11},{10,... | collective-permute-start | bytes 184328 | tf_op jit(solution)/shard_map/ppermute | solution.py:20
  23.1 1.9 %copy-done = f32[1,2048,384]{2,1,0:T(8,128)S(1)} copy-done((f32[1,2048,384]{2,1,0:T(8,128)S(1)}, f32[1,2048,384]{2,1,0:T(8,128)}, u32[]{:S(2)}) %copy-start) | copy-done | bytes 3145752
  25.0 0.7 %shard_map.74 = (bf16[2048,384]{1,0:T(8,128)(2,1)S(1)}, bf16[2048,384]{1,0:T(8,128)(2,1)S(1)}) custom-call(f32[2048,384]{1,0:T(8,128)S(1)} %bitcast.7), custom_call_target="tpu_custom_call" | custom-call | bytes 3500000 | tf_op jit(solution)/shard_map/pallas_call | solution.py:239
  25.7 0.5 %collective-permute-done.6 = f32[1,4,20,192]{3,2,1,0:T(8,128)S(1)} collective-permute-done((f32[1,4,20,192]{3,2,1,0:T(8,128)S(1)}, f32[1,4,20,192]{3,2,1,0:T(8,128)S(1)}, u32[]{:S(2)}, u32[]{:S(2)}) %collective-permute-start.6) | collective-permute-done | bytes 61472 | tf_op jit(solution)/shard_map/ppermute | solution.py:20
  26.3 0.8 %shard_map.75.refs_1_ = f32[3,32,384]{2,1,0:T(8,128)S(1)} custom-call(f32[32,2048]{1,0:T(8,128)S(1)} %constant_dynamic-slice_fusion.refs_0_, f32[32,2048]{1,0:T(8,128)S(1)} %collective-permute-done.4.refs_1_, f32[32,2048]{1,0:T(8,128)S(1)} %collective-permute-done.5.refs_2_, bf16[2048,384]{1,0:T(8,128)(2,1)S(1)} %get-tuple-element.45.refs_3_.refs_2_, ...), custom_call_target="tpu_custom_call" | custom-call | bytes 3500000 | tf_op jit(solution)/shard_map/pallas_call | solution.py:285
  27.1 0.7 %collective-permute-done.refs_0_ = f32[32,2048]{1,0:T(8,128)S(1)} collective-permute-done((f32[32,2048]{1,0:T(8,128)S(1)}, f32[32,2048]{1,0:T(8,128)S(1)}, u32[]{:S(2)}, u32[]{:S(2)}) %collective-permute-start) | collective-permute-done | bytes 262176 | tf_op jit(solution)/shard_map/ppermute | solution.py:20
  27.8 0.6 %shard_map.76 = (f32[64,384]{1,0:T(8,128)S(1)}, f32[64,384]{1,0:T(8,128)S(1)}) custom-call(f32[32,2048]{1,0:T(8,128)S(1)} %collective-permute-done.refs_0_, f32[3,32,384]{2,1,0:T(8,128)S(1)} %shard_map.75.refs_1_, bf16[2048,384]{1,0:T(8,128)(2,1)S(1)} %get-tuple-element.45.refs_3_.refs_2_, bf16[2048,384]{1,0:T(8,128)(2,1)S(1)} %get-tuple-element.46.refs_4_.refs_3_), custom_call_target="tpu_custom_call" | custom-call | bytes 350000 | tf_op jit(solution)/shard_map/pallas_call | solution.py:297
  28.4 0.1 collective-permute-start.7
  28.5 1.3 %collective-permute-done.7 = f32[64,384]{1,0:T(8,128)S(1)} collective-permute-done((f32[64,384]{1,0:T(8,128)S(1)}, f32[64,384]{1,0:T(8,128)S(1)}, u32[]{:S(2)}, u32[]{:S(2)}) %collective-permute-start.7) | collective-permute-done | bytes 98336 | tf_op jit(solution)/shard_map/ppermute | solution.py:20
  29.8 1.6 %collective-permute-start.8 = (f32[64,384]{1,0:T(8,128)S(1)}, f32[64,384]{1,0:T(8,128)S(1)}, u32[]{:S(2)}, u32[]{:S(2)}) collective-permute-start(f32[64,384]{1,0:T(8,128)S(1)} %add.28), channel_id=1, source_target_pairs={{0,2},{1,3},{2,0},{3,1},{4,6},{5,7},{6,4},{7,5},{8,10},{9,11},{10,... | collective-permute-start | bytes 294920 | tf_op jit(solution)/shard_map/ppermute | solution.py:20
  31.3 3.4 %collective-permute-done.8 = f32[64,384]{1,0:T(8,128)S(1)} collective-permute-done((f32[64,384]{1,0:T(8,128)S(1)}, f32[64,384]{1,0:T(8,128)S(1)}, u32[]{:S(2)}, u32[]{:S(2)}) %collective-permute-start.8) | collective-permute-done | bytes 98336 | tf_op jit(solution)/shard_map/ppermute | solution.py:20
  34.7 5.4 %collective-permute-start.9 = (f32[64,384]{1,0:T(8,128)S(1)}, f32[64,384]{1,0:T(8,128)S(1)}, u32[]{:S(2)}, u32[]{:S(2)}) collective-permute-start(f32[64,384]{1,0:T(8,128)S(1)} %add.29), channel_id=1, source_target_pairs={{0,4},{4,0},{8,12},{12,8},{1,5},{5,1},{9,13},{13,9},{2,6},{6,2},{1... | collective-permute-start | bytes 294920 | tf_op jit(solution)/shard_map/ppermute | solution.py:20
  40.1 2.6 %collective-permute-done.9 = f32[64,384]{1,0:T(8,128)S(1)} collective-permute-done((f32[64,384]{1,0:T(8,128)S(1)}, f32[64,384]{1,0:T(8,128)S(1)}, u32[]{:S(2)}, u32[]{:S(2)}) %collective-permute-start.9) | collective-permute-done | bytes 98336 | tf_op jit(solution)/shard_map/ppermute | solution.py:20
  42.7 2.7 %collective-permute-start.10 = (f32[64,384]{1,0:T(8,128)S(1)}, f32[64,384]{1,0:T(8,128)S(1)}, u32[]{:S(2)}, u32[]{:S(2)}) collective-permute-start(f32[64,384]{1,0:T(8,128)S(1)} %add.30), channel_id=1, source_target_pairs={{0,8},{4,12},{8,0},{12,4},{1,9},{5,13},{9,1},{13,5},{2,10},{6,14},... | collective-permute-start | bytes 294920 | tf_op jit(solution)/shard_map/ppermute | solution.py:20
  45.4 0.8 %pad_maximum_fusion.packs = f32[4,4,20,192]{3,2,1,0:T(8,128)} fusion(f32[2,4,20,192]{3,2,1,0:T(8,128)S(1)} %collective-permute-done.11, f32[2,4,20,192]{3,2,1,0:T(8,128)S(1)} %pad_maximum_fusion.1), kind=kLoop, calls=%fused_computation | loop fusion | flops 61440 | bytes 491520 | tf_op jit(solution)/shard_map/concatenate | solution.py:352
  46.2 2.0 %shard_map.77 = (bf16[192,128]{1,0:T(8,128)(2,1)}, bf16[192,128]{1,0:T(8,128)(2,1)}) custom-call(f32[4,4,20,192]{3,2,1,0:T(8,128)} %pad_maximum_fusion.packs), custom_call_target="tpu_custom_call" | custom-call | bytes 10500000 | tf_op jit(solution)/shard_map/pallas_call | solution.py:360
  48.2 0.0 collective-permute-done.10
  48.3 0.1 collective-permute-start.12
  48.4 1.3 %collective-permute-done.12.other = f32[64,384]{1,0:T(8,128)S(1)} collective-permute-done((f32[64,384]{1,0:T(8,128)S(1)}, f32[64,384]{1,0:T(8,128)S(1)}, u32[]{:S(2)}, u32[]{:S(2)}) %collective-permute-start.12) | collective-permute-done | bytes 98336 | tf_op jit(solution)/shard_map/ppermute | solution.py:20
  49.7 0.8 %copy-done.1 = bf16[192,128]{1,0:T(8,128)(2,1)S(1)} copy-done((bf16[192,128]{1,0:T(8,128)(2,1)S(1)}, bf16[192,128]{1,0:T(8,128)(2,1)}, u32[]{:S(2)}) %copy-start.1) | copy-done | bytes 49176
  50.5 0.8 %copy-done.2 = bf16[192,128]{1,0:T(8,128)(2,1)S(1)} copy-done((bf16[192,128]{1,0:T(8,128)(2,1)S(1)}, bf16[192,128]{1,0:T(8,128)(2,1)}, u32[]{:S(2)}) %copy-start.2) | copy-done | bytes 49176
  51.2 1.0 %shard_map.78 = f32[192,384]{1,0:T(8,128)} custom-call(bf16[192,128]{1,0:T(8,128)(2,1)S(1)} %copy-done.1, bf16[192,128]{1,0:T(8,128)(2,1)S(1)} %copy-done.2, f32[64,384]{1,0:T(8,128)S(1)} %maximum_add_fusion.total, f32[64,384]{1,0:T(8,128)S(1)} %collective-permute-done.12.other), custom_call_target="tpu_custom_call" | custom-call | tf_op jit(solution)/shard_map/pallas_call | solution.py:375
  (16 shorter events, 0.1 us)
Async XLA Ops:
  1.2 19.7 %collective-permute-start.4 = (f32[32,2048]{1,0:T(8,128)S(1)}, f32[32,2048]{1,0:T(8,128)S(1)}, u32[]{:S(2)}, u32[]{:S(2)}) collective-permute-start(f32[32,2048]{1,0:T(8,128)S(1)} %get-tuple-element.34), channel_id=1, source_target_pairs={{0,4},{4,0},{8,12},{12,8},{1,5},{5,1},{9,13},{13,9},{2,6},{6,2},{1... | collective-permute-start | bytes 786440 | tf_op jit(solution)/shard_map/ppermute | solution.py:20
  4.3 16.6 %collective-permute-start.5 = (f32[32,2048]{1,0:T(8,128)S(1)}, f32[32,2048]{1,0:T(8,128)S(1)}, u32[]{:S(2)}, u32[]{:S(2)}) collective-permute-start(f32[32,2048]{1,0:T(8,128)S(1)} %get-tuple-element.35), channel_id=1, source_target_pairs={{0,8},{4,12},{8,0},{12,4},{1,9},{5,13},{9,1},{13,5},{2,10},{6,14},... | collective-permute-start | bytes 786440 | tf_op jit(solution)/shard_map/ppermute | solution.py:20
  8.7 10.8 %collective-permute-start.3 = (f32[20,192]{1,0:T(8,128)}, f32[20,192]{1,0:T(8,128)S(1)}, u32[]{:S(2)}, u32[]{:S(2)}) collective-permute-start(f32[20,192]{1,0:T(8,128)} %shard_map.73), channel_id=1, source_target_pairs={{0,12},{4,8},{8,4},{12,0},{1,13},{5,9},{9,5},{13,1},{2,14},{6,10},... | collective-permute-start | bytes 46088 | tf_op jit(solution)/shard_map/ppermute | solution.py:20
  8.7 12.1 %collective-permute-start.2 = (f32[20,192]{1,0:T(8,128)}, f32[20,192]{1,0:T(8,128)S(1)}, u32[]{:S(2)}, u32[]{:S(2)}) collective-permute-start(f32[20,192]{1,0:T(8,128)} %shard_map.73), channel_id=1, source_target_pairs={{0,8},{4,12},{8,0},{12,4},{1,9},{5,13},{9,1},{13,5},{2,10},{6,14},... | collective-permute-start | bytes 46088 | tf_op jit(solution)/shard_map/ppermute | solution.py:20
  10.6 10.2 %collective-permute-start.1 = (f32[20,192]{1,0:T(8,128)}, f32[20,192]{1,0:T(8,128)S(1)}, u32[]{:S(2)}, u32[]{:S(2)}) collective-permute-start(f32[20,192]{1,0:T(8,128)} %shard_map.73), channel_id=1, source_target_pairs={{0,4},{4,0},{8,12},{12,8},{1,5},{5,1},{9,13},{13,9},{2,6},{6,2},{1... | collective-permute-start | bytes 46088 | tf_op jit(solution)/shard_map/ppermute | solution.py:20
  19.5 8.3 %collective-permute-start = (f32[32,2048]{1,0:T(8,128)S(1)}, f32[32,2048]{1,0:T(8,128)S(1)}, u32[]{:S(2)}, u32[]{:S(2)}) collective-permute-start(f32[32,2048]{1,0:T(8,128)S(1)} %get-tuple-element.32), channel_id=1, source_target_pairs={{0,12},{4,8},{8,4},{12,0},{1,13},{5,9},{9,5},{13,1},{2,14},{6,10},... | collective-permute-start | bytes 786440 | tf_op jit(solution)/shard_map/ppermute | solution.py:20
  21.6 4.7 %collective-permute-start.6 = (f32[1,4,20,192]{3,2,1,0:T(8,128)S(1)}, f32[1,4,20,192]{3,2,1,0:T(8,128)S(1)}, u32[]{:S(2)}, u32[]{:S(2)}) collective-permute-start(f32[1,4,20,192]{3,2,1,0:T(8,128)S(1)} %maximum_bitcast_fusion), channel_id=1, source_target_pairs={{0,2},{1,3},{2,0},{3,1},{4,6},{5,7},{6,4},{7,5},{8,10},{9,11},{10,... | collective-permute-start | bytes 184328 | tf_op jit(solution)/shard_map/ppermute | solution.py:20
  23.1 1.9 %copy-start = (f32[1,2048,384]{2,1,0:T(8,128)S(1)}, f32[1,2048,384]{2,1,0:T(8,128)}, u32[]{:S(2)}) copy-start(f32[1,2048,384]{2,1,0:T(8,128)} %param.8) | copy-start | bytes 9437188
  28.4 1.4 %collective-permute-start.7 = (f32[64,384]{1,0:T(8,128)S(1)}, f32[64,384]{1,0:T(8,128)S(1)}, u32[]{:S(2)}, u32[]{:S(2)}) collective-permute-start(f32[64,384]{1,0:T(8,128)S(1)} %get-tuple-element.48), channel_id=1, source_target_pairs={{0,1},{1,0},{2,3},{3,2},{4,5},{5,4},{6,7},{7,6},{8,9},{9,8},{10,11... | collective-permute-start | bytes 294920 | tf_op jit(solution)/shard_map/ppermute | solution.py:20
  29.8 4.9 %collective-permute-start.8 = (f32[64,384]{1,0:T(8,128)S(1)}, f32[64,384]{1,0:T(8,128)S(1)}, u32[]{:S(2)}, u32[]{:S(2)}) collective-permute-start(f32[64,384]{1,0:T(8,128)S(1)} %add.28), channel_id=1, source_target_pairs={{0,2},{1,3},{2,0},{3,1},{4,6},{5,7},{6,4},{7,5},{8,10},{9,11},{10,... | collective-permute-start | bytes 294920 | tf_op jit(solution)/shard_map/ppermute | solution.py:20
  31.3 14.1 %collective-permute-start.11 = (f32[2,4,20,192]{3,2,1,0:T(8,128)S(1)}, f32[2,4,20,192]{3,2,1,0:T(8,128)S(1)}, u32[]{:S(2)}, u32[]{:S(2)}) collective-permute-start(f32[2,4,20,192]{3,2,1,0:T(8,128)S(1)} %pad_maximum_fusion.1), channel_id=1, source_target_pairs={{0,1},{1,0},{2,3},{3,2},{4,5},{5,4},{6,7},{7,6},{8,9},{9,8},{10,11... | collective-permute-start | bytes 368648 | tf_op jit(solution)/shard_map/ppermute | solution.py:20
  34.7 8.0 %collective-permute-start.9 = (f32[64,384]{1,0:T(8,128)S(1)}, f32[64,384]{1,0:T(8,128)S(1)}, u32[]{:S(2)}, u32[]{:S(2)}) collective-permute-start(f32[64,384]{1,0:T(8,128)S(1)} %add.29), channel_id=1, source_target_pairs={{0,4},{4,0},{8,12},{12,8},{1,5},{5,1},{9,13},{13,9},{2,6},{6,2},{1... | collective-permute-start | bytes 294920 | tf_op jit(solution)/shard_map/ppermute | solution.py:20
  42.7 5.6 %collective-permute-start.10 = (f32[64,384]{1,0:T(8,128)S(1)}, f32[64,384]{1,0:T(8,128)S(1)}, u32[]{:S(2)}, u32[]{:S(2)}) collective-permute-start(f32[64,384]{1,0:T(8,128)S(1)} %add.30), channel_id=1, source_target_pairs={{0,8},{4,12},{8,0},{12,4},{1,9},{5,13},{9,1},{13,5},{2,10},{6,14},... | collective-permute-start | bytes 294920 | tf_op jit(solution)/shard_map/ppermute | solution.py:20
  48.3 1.4 %collective-permute-start.12 = (f32[64,384]{1,0:T(8,128)S(1)}, f32[64,384]{1,0:T(8,128)S(1)}, u32[]{:S(2)}, u32[]{:S(2)}) collective-permute-start(f32[64,384]{1,0:T(8,128)S(1)} %maximum_add_fusion.total), channel_id=1, source_target_pairs={{0,1},{1,0},{2,3},{3,2},{4,5},{5,4},{6,7},{7,6},{8,9},{9,8},{10,11... | collective-permute-start | bytes 294920 | tf_op jit(solution)/shard_map/ppermute | solution.py:20
  49.6 0.8 %copy-start.1 = (bf16[192,128]{1,0:T(8,128)(2,1)S(1)}, bf16[192,128]{1,0:T(8,128)(2,1)}, u32[]{:S(2)}) copy-start(bf16[192,128]{1,0:T(8,128)(2,1)} %get-tuple-element.52.high) | copy-start | bytes 147460
  50.4 0.8 %copy-start.2 = (bf16[192,128]{1,0:T(8,128)(2,1)S(1)}, bf16[192,128]{1,0:T(8,128)(2,1)}, u32[]{:S(2)}) copy-start(bf16[192,128]{1,0:T(8,128)(2,1)} %get-tuple-element.53.low) | copy-start | bytes 147460

commit v3 on v2

--- a/solution.py
+++ b/solution.py
@@ -120,35 +120,32 @@
     return jax.ShapeDtypeStruct(shape, jnp.float32)
 
 
-def cut_kernel(pieces, aic, *refs):
-    outs, sems = refs[:-1], refs[-1]
-    blk = lax.axis_index("blk")
-    copies = []
-    for at, (mask, first, rows) in enumerate(pieces):
-        panels = outs[at].shape[1]
-        start = pl.multiple_of((blk ^ mask) * panels, 128)
-        source = aic.at[pl.ds(first, rows), pl.ds(start, panels)]
-        copies.append(pltpu.make_async_copy(source, outs[at], sems.at[at]))
-        copies[-1].start()
-    for copy in copies:
-        copy.wait()
-
-
-def cut_out(aic, panels, pieces):
-    return pl.pallas_call(
-        functools.partial(cut_kernel, pieces),
-        out_shape=[f32(rows, panels) for _, _, rows in pieces],
-        in_specs=[ANY],
-        out_specs=[VMEM] * len(pieces),
-        scratch_shapes=[pltpu.SemaphoreType.DMA((len(pieces),))],
-        cost_estimate=cost(2),
-    )(aic)
+def folded(rows):
+    return rows + rows // 2
+
+
+def fold(value, out, start):
+    rows, width = value.shape
+    wide, half = 2 * width // 3, rows // 2
+    below = start + rows
+    out[start:below, :] = value[:, :wide]
+    out[below : below + half, : wide // 2] = value[:half, wide:]
+    out[below : below + half, wide // 2 :] = value[half:, wide:]
+
+
+def unfold(value, out, start):
+    rows, wide = value.shape[0] * 2 // 3, value.shape[1]
+    middle, end = start + rows // 2, start + rows
+    out[start:end, :wide] = value[:rows]
+    out[start:middle, wide:] = value[rows:, : wide // 2]
+    out[middle:end, wide:] = value[rows:, wide // 2 :]
 
 
 def spline_kernel(src_rows, dst_nodes, counts, weights, modes, pack):
     owners, slots = src_rows.shape[2:]
     dofs, node_count, width = modes.shape
-    sub_rows = pack.shape[0] - dofs * node_count // lax.axis_size("col")
+    share = dofs * node_count // lax.axis_size("col")
+    sub_rows = (pack.shape[0] - folded(share)) * 2 // 3
     shape = (sub_rows, owners * dofs * node_count)
     row = lax.broadcasted_iota(jnp.int32, shape, 0)
     place = lax.broadcasted_iota(jnp.int32, shape, 1)
@@ -162,21 +159,21 @@
                 term = jnp.where(place == node + dof * node_count, weights[0, 0, dof, owner, slot], term)
             here = jnp.where(slot < live, src_rows[0, 0, owner, slot], -1)
             total = total + jnp.where(row == here, term, 0.0)
-    pack[:sub_rows, :] = total
+    fold(total, pack, 0)
     flat = modes[...].reshape(dofs * node_count, width)
-    share = dofs * node_count // lax.axis_size("col")
     col = lax.axis_index("col")
     for turn in range(lax.axis_size("col")):
 
         @pl.when(col == turn)
         def _():
-            pack[sub_rows:, :] = flat[turn * share : (turn + 1) * share]
+            fold(flat[turn * share : (turn + 1) * share], pack, folded(sub_rows))
 
 
 def transfer_kernel(sub_rows, packs, high, low, modes, spread):
     cols, blk_count = packs.shape[:2]
     blk, col = lax.axis_index("blk"), lax.axis_index("col")
-    share = packs.shape[2] - sub_rows
+    spline_rows = folded(sub_rows)
+    share = (packs.shape[2] - spline_rows) * 2 // 3
     half = blk_count // 2
     quarter = cols // 2
     own = blk // half * half
@@ -189,14 +186,14 @@
     for b in range(blk_count):
         for c in range(cols):
             at = (b * cols + c) * share
-            modes[at : at + share, :] = packs[entry(c), blk ^ b, sub_rows:, :]
+            unfold(packs[entry(c), blk ^ b, spline_rows:, :], modes, at)
     at = 0
     for turn in range(2):
         for b in range(blk_count):
             block = own + b if b < half else half - own + b - half
             for c in range(quarter):
                 place = (lax.rem(col, 2) ^ turn) * quarter + c
-                spread[at : at + sub_rows, :] = packs[entry(place), blk ^ block, :sub_rows, :]
+                unfold(packs[entry(place), blk ^ block, :spline_rows, :], spread, at)
                 at += sub_rows
     whole = lax.dot_general(
         modes[...], spread[...], (((0,), (1,)), ((), ())), precision=HIGHEST,
@@ -246,7 +243,7 @@
             pltpu.SemaphoreType.DMA((steps,)),
         ],
         compiler_params=ROOM,
-        cost_estimate=cost(1),
+        cost_estimate=cost(0.001),
     )(shapes)
 
 
@@ -261,22 +258,24 @@
 
 def early_kernel(*refs):
     *pieces, high, low, out = refs
-    out[...] = product(pieces, high, low).reshape(out.shape)
+    out[...] = product(pieces, high, low)
 
 
 def late_kernel(groups, *refs):
     *pieces, early, high, low, kept, given, total = refs
     done = early.shape[0]
-    total[:done] = early[...]
-    total[done:] = product(pieces, high, low).reshape(total[done:].shape)
+    total[:done, :] = early[...]
+    total[done:, :] = product(pieces, high, low)
     blk, core = lax.axis_index("blk"), lax.rem(lax.axis_index("col"), 2)
-    half = total.shape[1] // 2
+    rows = total.shape[0] // sum(groups)
+    half = rows // 2
     at = first = 0
     for group in groups:
         for index in range(group):
-            source = first + ((blk & (group - 1)) ^ index)
-            kept[at : at + half, :] = total[source, pl.ds(pl.multiple_of(core * half, 8), half), :]
-            given[at : at + half, :] = total[source, pl.ds(pl.multiple_of((1 - core) * half, 8), half), :]
+            source = (first + ((blk & (group - 1)) ^ index)) * rows
+            for side, out in ((core, kept), (1 - core, given)):
+                place = pl.multiple_of(source + side * half, 8)
+                out[at : at + half, :] = total[pl.ds(place, half), :]
             at += half
         first += group
 
@@ -284,25 +283,43 @@
 def early_products(pieces, high, low):
     return pl.pallas_call(
         early_kernel,
-        out_shape=f32(len(pieces), pieces[0].shape[0], high.shape[1]),
+        out_shape=f32(sum(piece.shape[0] for piece in pieces), high.shape[1]),
         in_specs=[VMEM] * (len(pieces) + 2),
         out_specs=VMEM,
         compiler_params=ROOM,
-        cost_estimate=cost(1),
+        cost_estimate=cost(0.001),
     )(*pieces, high, low)
 
 
 def late_products(groups, pieces, early, high, low):
-    count, (rows, width) = sum(groups), early.shape[1:]
+    width = high.shape[1]
+    rows = early.shape[0] + sum(piece.shape[0] for piece in pieces)
     return pl.pallas_call(
         functools.partial(late_kernel, groups),
-        out_shape=[f32(rows * count // 2, width)] * 2,
+        out_shape=[f32(rows // 2, width)] * 2,
         in_specs=[VMEM] * (len(pieces) + 3),
         out_specs=[VMEM] * 2,
-        scratch_shapes=[pltpu.VMEM((count, rows, width), jnp.float32)],
-        compiler_params=ROOM,
-        cost_estimate=cost(0.1),
+        scratch_shapes=[pltpu.VMEM((rows, width), jnp.float32)],
+        compiler_params=ROOM,
+        cost_estimate=cost(0.001),
     )(*pieces, early, high, low)
+
+
+def joined_kernel(*refs):
+    *parts, out = refs
+    for index, part in enumerate(parts):
+        out[index] = part[...]
+
+
+def joined(*parts):
+    return pl.pallas_call(
+        joined_kernel,
+        out_shape=f32(len(parts), *parts[0].shape),
+        in_specs=[VMEM] * len(parts),
+        out_specs=VMEM,
+        compiler_params=ROOM,
+        cost_estimate=cost(0.001),
+    )(*parts)
 
 
 def shards(aic, downwash, node_modes, src_rows, dst_nodes, counts, spline_weights):
@@ -322,36 +339,37 @@
         return lax.dynamic_slice_in_dim(source, (blk ^ mask) * panels, panels, 1)
 
     far_masks = list(range(half, blk_count))
-    near = [columns(mask) for mask in range(1, half)]
-    far = [columns(mask) for mask in far_masks]
-    rest, lists, shapes, *cuts = lax.optimization_barrier((aic, src_rows, shapes, *near, *far))
-    near, far = cuts[: half - 1], cuts[half - 1 :]
+    far = [columns(mask) for mask in far_masks[:-1]]
+    rest, *far = lax.optimization_barrier((aic, *far))
+    far = [swap(piece, "blk", mask) for mask, piece in zip(far_masks, far)]
+    near = [columns(mask, rest) for mask in range(1, half)]
+    last = columns(far_masks[-1], rest)
+    rest, lists, shapes, last, *near = lax.optimization_barrier((rest, src_rows, shapes, last, *near))
     near = [swap(piece, "blk", mask + 1) for mask, piece in enumerate(near)]
-    far[:-1] = [swap(piece, "blk", mask) for mask, piece in zip(far_masks, far[:-1])]
     near = [columns(0, rest), *near]
     high, low = halves(shapes, 4)
 
     pack = pl.pallas_call(
         spline_kernel,
-        out_shape=f32(sub_rows + share, modes),
+        out_shape=f32(folded(sub_rows) + folded(share), 2 * modes // 3),
         in_specs=[SMEM] * 4 + [VMEM],
         out_specs=VMEM,
-        cost_estimate=cost(1),
+        compiler_params=ROOM,
+        cost_estimate=cost(0.001),
     )(lists, dst_nodes, counts, spline_weights, node_modes)
-    far[-1] = swap(after(far[-1], pack), "blk", far_masks[-1])
+    last = swap(after(last, pack), "blk", far_masks[-1])
     packs = [pack] + [swap(pack, "blk", mask) for mask in range(1, blk_count)]
-    waiting = lax.optimization_barrier((*packs, *near, *far[:-1]))
-    packs, near, far[:-1] = waiting[:blk_count], waiting[blk_count : blk_count + half], waiting[blk_count + half :]
-    packs = jnp.stack(packs)[None]
-    col_masks = masks("col")
-    for mask in col_masks[:0:-1]:
-        packs = jnp.concatenate([packs, swap(packs, "col", mask)])
+    waiting = lax.optimization_barrier((*packs, *near, *far))
+    packs, near, far = waiting[:blk_count], waiting[blk_count : blk_count + half], waiting[blk_count + half :]
+    packs = joined(*packs)[None]
+    for mask in masks("col")[:0:-1]:
+        packs = joined(packs, swap(packs, "col", mask)).reshape(-1, *packs.shape[1:])
     packs, high = lax.optimization_barrier((packs, high))
-    early = early_products([*near, *far[:-1]], high, low)
-    total, given = late_products((half, half), far[-1:], early, high, low)
+
+    early = early_products([*near, *far], high, low)
+    total, given = late_products((half, half), [last], early, high, low)
     packs = jnp.concatenate([packs, swap(packs, "col", 1)])
-    given = swap(given, "col", 1)
-    total = total + given
+    total = total + swap(given, "col", 1)
     for mask in masks("col")[1:]:
         total = total + swap(total, "col", mask)
     for mask in masks("blk")[:-1]:
@@ -366,6 +384,7 @@
             pltpu.VMEM((loads, modes), jnp.float32),
             pltpu.VMEM((blk_count * block_rows, loads), jnp.float32),
         ],
+        compiler_params=ROOM,
         cost_estimate=cost(3),
     )(packs)
     there, *transfer = lax.optimization_barrier((there, *transfer))
@@ -375,7 +394,6 @@
     return pl.pallas_call(
         last_kernel,
         out_shape=f32(modes, width),
-        in_specs=[VMEM] * 4,
         compiler_params=ROOM,
     )(*transfer, total, other)
 
@@ -393,7 +411,9 @@
 
     def program(*arrays):
         dofs, nodes, modes = arrays[2].shape
-        body = shards if dofs * nodes == modes else by_parts
+        blk_count, col_count = mesh.shape["blk"], mesh.shape["col"]
+        small = dofs * nodes == modes and modes % 3 == 0
+        body = shards if small and blk_count > 2 and col_count > 2 else by_parts
         return jax.shard_map(
             body, mesh=mesh, in_specs=placed, out_specs=P("groups", None), check_vma=False
         )(*arrays)

time: 52.7 us -> 51.2 us (0.972)
  Pallas kernels: 6.93 us -> 4.62 us
  starting transfers between devices: 22.8 us -> 24.7 us
  other arithmetic: 1.61 us -> 0.07 us
  waiting for transfers between devices: 15.2 us -> 16.4 us
  local copies, waits for them, and re-layouts: 5.62 us -> 4.98 us
    ppermute x13, starting transfers between devices: 22.8 us -> 24.7 us  [swap(): return lax.ppermute(value, axis, pairs)]
    unnamed x6 -> x12, local copies, waits for them, and re-layouts: 3.49 us -> 1.91 us
    pallas_call x1, Pallas kernels: 2.02 us -> 0.47 us  [shards(): pl.pallas_call(functools.partial(transfer_kernel, sub_rows), out_shape=[j...]
    ppermute x13, waiting for transfers between devices: 15.2 us -> 16.4 us  [swap(): return lax.ppermute(value, axis, pairs)]
    dynamic_slice x2 -> x3, local copies, waits for them, and re-layouts: 2.13 us -> 3.06 us  [columns(): return lax.dynamic_slice_in_dim(source, (blk ^ mask) * panels, panels, 1)]
    concatenate x1, other arithmetic: 0.78 us -> 0.02 us  [shards(): packs = jnp.concatenate([packs, swap(packs, 'col', 1)])]
    pallas_call x3 -> x5, Pallas kernels: 3.62 us -> 2.86 us  [the longest x1 1.06 us: shards(): pl.pallas_call(spline_kernel, out_shape=f32(folded(sub_rows) + folded(sha...]
    broadcast_in_dim x1 -> x0, other arithmetic: 0.75 us -> none  [shards(): packs = jnp.stack(packs)[None]]
  transfers between devices with their start and end apart: 13 -> 13, of which waited for: 7 -> 7; matrix products, arithmetic and copies ran while one was open for 5% -> 4% of each run, Pallas kernels for 10% -> 6%
where the time goes in v3:
time: 51.2 us; the launch traced here: 51 us
  starting transfers between devices  24.7 us (48%)
  waiting for transfers between devices  16.4 us (32%)
  local copies, waits for them, and re-layouts  4.98 us (10%)
  Pallas kernels  4.62 us (9%)
    ppermute x13, starting transfers between devices, swap(): return lax.ppermute(value, axis, pairs)  24.7 us
    ppermute x13, waiting for transfers between devices, swap(): return lax.ppermute(value, axis, pairs)  16.4 us
    dynamic_slice x3, local copies, waits for them, and re-layouts, columns(): return lax.dynamic_slice_in_dim(source, (blk ^ mask) * panels, panels, 1)  3.06 us
    unnamed x12, local copies, waits for them, and re-layouts  1.91 us
    pallas_call x1, Pallas kernels, shards(): pl.pallas_call(spline_kernel, out_shape=f32(folded(sub_rows) + folded(sha...  1.06 us
  transfers between devices with their start and end apart: 13, of which 7 were waited for; matrix products, arithmetic and copies ran while one was open for 4% of the time, Pallas kernels for 6%

profile of v3, /device:TPU:0, one launch (start us, length us, event | category | flops | bytes accessed | tf_op | source)
XLA Modules:
  0.0 51.0 jit_solution(4989083595707938376)
XLA Ops:
  0.0 1.0 %constant_dynamic-slice_fusion.3 = f32[32,2048]{1,0:T(8,128)S(1)} fusion(f32[32,8192]{1,0:T(8,128)} %param.7, s32[]{:T(128)S(6)} %select_n.12), kind=kLoop, calls=%fused_computation.5 | loop fusion | bytes 524292 | tf_op jit(solution)/shard_map/dynamic_slice | solution.py:339
  1.1 4.1 %collective-permute-start.5 = (f32[32,2048]{1,0:T(8,128)S(1)}, f32[32,2048]{1,0:T(8,128)S(1)}, u32[]{:S(2)}, u32[]{:S(2)}) collective-permute-start(f32[32,2048]{1,0:T(8,128)S(1)} %constant_dynamic-slice_fusion.3), channel_id=1, source_target_pairs={{0,8},{4,12},{8,0},{12,4},{1,9},{5,13},{9,1},{13,5},{2,10},{6,14},... | collective-permute-start | bytes 786440 | tf_op jit(solution)/shard_map/ppermute | solution.py:20
  5.2 1.1 %constant_dynamic-slice_fusion.1 = (f32[32,2048]{1,0:T(8,128)S(1)}, f32[32,2048]{1,0:T(8,128)S(1)}) fusion(f32[32,8192]{1,0:T(8,128)} %param.7, s32[]{:T(128)S(6)} %select_n.14, s32[]{:T(128)S(6)} %select_n.13), kind=kLoop, calls=%fused_computation.3 | loop fusion | bytes 1048584 | tf_op jit(solution)/shard_map/dynamic_slice | solution.py:339
  6.2 1.6 %collective-permute-start.4 = (f32[32,2048]{1,0:T(8,128)S(1)}, f32[32,2048]{1,0:T(8,128)S(1)}, u32[]{:S(2)}, u32[]{:S(2)}) collective-permute-start(f32[32,2048]{1,0:T(8,128)S(1)} %get-tuple-element.36), channel_id=1, source_target_pairs={{0,4},{4,0},{8,12},{12,8},{1,5},{5,1},{9,13},{13,9},{2,6},{6,2},{1... | collective-permute-start | bytes 786440 | tf_op jit(solution)/shard_map/ppermute | solution.py:20
  7.9 1.1 %shard_map.73.refs_0_ = f32[30,128]{1,0:T(8,128)S(1)} custom-call(s32[1,1,4,8]{3,2,1,0:T(4,128)S(1)} %copy-done.3, s32[1,1,4,8]{3,2,1,0:T(4,128)S(1)} %copy-done.4, s32[1,1,4]{2,1,0:T(1,128)S(1)} %copy-done.5, f32[1,1,6,4,8]{4,3,2,1,0:T(4,128)S(1)} %copy-done.2, f32[6,8,192]{2,1,0:T(8,128)S(1)} %copy-done.1), custom_call_target="tpu_custom_call" | custom-call | bytes 3500 | tf_op jit(solution)/shard_map/pallas_call | solution.py:352
  9.0 0.0 collective-permute-start.3
  9.0 1.9 %collective-permute-start.2 = (f32[30,128]{1,0:T(8,128)S(1)}, f32[30,128]{1,0:T(8,128)S(1)}, u32[]{:S(2)}, u32[]{:S(2)}) collective-permute-start(f32[30,128]{1,0:T(8,128)S(1)} %shard_map.73.refs_0_), channel_id=1, source_target_pairs={{0,8},{4,12},{8,0},{12,4},{1,9},{5,13},{9,1},{13,5},{2,10},{6,14},... | collective-permute-start | bytes 46088 | tf_op jit(solution)/shard_map/ppermute | solution.py:20
  10.9 2.5 %collective-permute-start.1 = (f32[30,128]{1,0:T(8,128)S(1)}, f32[30,128]{1,0:T(8,128)S(1)}, u32[]{:S(2)}, u32[]{:S(2)}) collective-permute-start(f32[30,128]{1,0:T(8,128)S(1)} %shard_map.73.refs_0_), channel_id=1, source_target_pairs={{0,4},{4,0},{8,12},{12,8},{1,5},{5,1},{9,13},{13,9},{2,6},{6,2},{1... | collective-permute-start | bytes 46088 | tf_op jit(solution)/shard_map/ppermute | solution.py:20
  13.4 5.6 %collective-permute-done.3.refs_3_ = f32[30,128]{1,0:T(8,128)S(1)} collective-permute-done((f32[30,128]{1,0:T(8,128)S(1)}, f32[30,128]{1,0:T(8,128)S(1)}, u32[]{:S(2)}, u32[]{:S(2)}) %collective-permute-start.3) | collective-permute-done | bytes 15392 | tf_op jit(solution)/shard_map/ppermute | solution.py:20
  19.0 2.5 %collective-permute-start = (f32[32,2048]{1,0:T(8,128)S(1)}, f32[32,2048]{1,0:T(8,128)S(1)}, u32[]{:S(2)}, u32[]{:S(2)}) collective-permute-start(f32[32,2048]{1,0:T(8,128)S(1)} %get-tuple-element.34), channel_id=1, source_target_pairs={{0,12},{4,8},{8,4},{12,0},{1,13},{5,9},{9,5},{13,1},{2,14},{6,10},... | collective-permute-start | bytes 786440 | tf_op jit(solution)/shard_map/ppermute | solution.py:20
  21.5 1.0 %constant_dynamic-slice_fusion.refs_0_ = f32[32,2048]{1,0:T(8,128)S(1)} fusion(f32[32,8192]{1,0:T(8,128)} %param.7, s32[]{:T(128)S(6)} %select_n.15), kind=kLoop, calls=%fused_computation.2 | loop fusion | bytes 524292 | tf_op jit(solution)/shard_map/dynamic_slice | solution.py:339
  22.5 0.0 collective-permute-done.2.refs_2_
  22.5 0.0 collective-permute-done.1.refs_1_
  22.5 0.0 collective-permute-done.4.refs_1_
  22.5 1.6 %collective-permute-start.6 = (f32[1,4,30,128]{3,2,1,0:T(8,128)S(1)}, f32[1,4,30,128]{3,2,1,0:T(8,128)S(1)}, u32[]{:S(2)}, u32[]{:S(2)}) collective-permute-start(f32[1,4,30,128]{3,2,1,0:T(8,128)S(1)} %bitcast.6), channel_id=1, source_target_pairs={{0,2},{1,3},{2,0},{3,1},{4,6},{5,7},{6,4},{7,5},{8,10},{9,11},{10,... | collective-permute-start | bytes 184328 | tf_op jit(solution)/shard_map/ppermute | solution.py:20
  24.1 1.9 %copy-done = f32[1,2048,384]{2,1,0:T(8,128)S(1)} copy-done((f32[1,2048,384]{2,1,0:T(8,128)S(1)}, f32[1,2048,384]{2,1,0:T(8,128)}, u32[]{:S(2)}) %copy-start) | copy-done | bytes 3145752
  26.0 0.7 %shard_map.76 = (bf16[2048,384]{1,0:T(8,128)(2,1)S(1)}, bf16[2048,384]{1,0:T(8,128)(2,1)S(1)}) custom-call(f32[2048,384]{1,0:T(8,128)S(1)} %bitcast.3), custom_call_target="tpu_custom_call" | custom-call | bytes 3500 | tf_op jit(solution)/shard_map/pallas_call | solution.py:236
  26.7 0.2 collective-permute-done.6.refs_1_
  26.9 0.8 %shard_map.77.refs_1_ = f32[96,384]{1,0:T(8,128)S(1)} custom-call(f32[32,2048]{1,0:T(8,128)S(1)} %constant_dynamic-slice_fusion.refs_0_, f32[32,2048]{1,0:T(8,128)S(1)} %collective-permute-done.4.refs_1_, f32[32,2048]{1,0:T(8,128)S(1)} %collective-permute-done.5.refs_2_, bf16[2048,384]{1,0:T(8,128)(2,1)S(1)} %get-tuple-element.47.refs_3_.refs_2_, ...), custom_call_target="tpu_custom_call" | custom-call | bytes 3500 | tf_op jit(solution)/shard_map/pallas_call | solution.py:284
  27.7 0.6 %shard_map.78 = (f32[64,384]{1,0:T(8,128)S(1)}, f32[64,384]{1,0:T(8,128)S(1)}) custom-call(f32[32,2048]{1,0:T(8,128)S(1)} %collective-permute-done.refs_0_, f32[96,384]{1,0:T(8,128)S(1)} %shard_map.77.refs_1_, bf16[2048,384]{1,0:T(8,128)(2,1)S(1)} %get-tuple-element.47.refs_3_.refs_2_, bf16[2048,384]{1,0:T(8,128)(2,1)S(1)} %get-tuple-element.48.refs_4_.refs_3_), custom_call_target="tpu_custom_call" | custom-call | bytes 3500 | tf_op jit(solution)/shard_map/pallas_call | solution.py:297
  28.3 0.1 collective-permute-start.7
  28.4 1.3 %collective-permute-done.7 = f32[64,384]{1,0:T(8,128)S(1)} collective-permute-done((f32[64,384]{1,0:T(8,128)S(1)}, f32[64,384]{1,0:T(8,128)S(1)}, u32[]{:S(2)}, u32[]{:S(2)}) %collective-permute-start.7) | collective-permute-done | bytes 98336 | tf_op jit(solution)/shard_map/ppermute | solution.py:20
  29.7 1.6 %collective-permute-start.8 = (f32[64,384]{1,0:T(8,128)S(1)}, f32[64,384]{1,0:T(8,128)S(1)}, u32[]{:S(2)}, u32[]{:S(2)}) collective-permute-start(f32[64,384]{1,0:T(8,128)S(1)} %add.28), channel_id=1, source_target_pairs={{0,2},{1,3},{2,0},{3,1},{4,6},{5,7},{6,4},{7,5},{8,10},{9,11},{10,... | collective-permute-start | bytes 294920 | tf_op jit(solution)/shard_map/ppermute | solution.py:20
  31.2 3.4 %collective-permute-done.8 = f32[64,384]{1,0:T(8,128)S(1)} collective-permute-done((f32[64,384]{1,0:T(8,128)S(1)}, f32[64,384]{1,0:T(8,128)S(1)}, u32[]{:S(2)}, u32[]{:S(2)}) %collective-permute-start.8) | collective-permute-done | bytes 98336 | tf_op jit(solution)/shard_map/ppermute | solution.py:20
  34.6 5.5 %collective-permute-start.9 = (f32[64,384]{1,0:T(8,128)S(1)}, f32[64,384]{1,0:T(8,128)S(1)}, u32[]{:S(2)}, u32[]{:S(2)}) collective-permute-start(f32[64,384]{1,0:T(8,128)S(1)} %add.29), channel_id=1, source_target_pairs={{0,4},{4,0},{8,12},{12,8},{1,5},{5,1},{9,13},{13,9},{2,6},{6,2},{1... | collective-permute-start | bytes 294920 | tf_op jit(solution)/shard_map/ppermute | solution.py:20
  40.1 2.6 %collective-permute-done.9 = f32[64,384]{1,0:T(8,128)S(1)} collective-permute-done((f32[64,384]{1,0:T(8,128)S(1)}, f32[64,384]{1,0:T(8,128)S(1)}, u32[]{:S(2)}, u32[]{:S(2)}) %collective-permute-start.9) | collective-permute-done | bytes 98336 | tf_op jit(solution)/shard_map/ppermute | solution.py:20
  42.7 3.3 %collective-permute-start.10 = (f32[64,384]{1,0:T(8,128)S(1)}, f32[64,384]{1,0:T(8,128)S(1)}, u32[]{:S(2)}, u32[]{:S(2)}) collective-permute-start(f32[64,384]{1,0:T(8,128)S(1)} %add.30), channel_id=1, source_target_pairs={{0,8},{4,12},{8,0},{12,4},{1,9},{5,13},{9,1},{13,5},{2,10},{6,14},... | collective-permute-start | bytes 294920 | tf_op jit(solution)/shard_map/ppermute | solution.py:20
  46.0 0.5 shard_map.79
  46.5 2.1 %collective-permute-done.10 = f32[64,384]{1,0:T(8,128)S(1)} collective-permute-done((f32[64,384]{1,0:T(8,128)S(1)}, f32[64,384]{1,0:T(8,128)S(1)}, u32[]{:S(2)}, u32[]{:S(2)}) %collective-permute-start.10) | collective-permute-done | bytes 98336 | tf_op jit(solution)/shard_map/ppermute | solution.py:20
  48.6 0.1 collective-permute-start.12
  48.7 1.3 %collective-permute-done.12.other = f32[64,384]{1,0:T(8,128)S(1)} collective-permute-done((f32[64,384]{1,0:T(8,128)S(1)}, f32[64,384]{1,0:T(8,128)S(1)}, u32[]{:S(2)}, u32[]{:S(2)}) %collective-permute-start.12) | collective-permute-done | bytes 98336 | tf_op jit(solution)/shard_map/ppermute | solution.py:20
  50.0 1.0 %shard_map.80 = f32[192,384]{1,0:T(8,128)} custom-call(bf16[192,128]{1,0:T(8,128)(2,1)S(1)} %get-tuple-element.54.high, bf16[192,128]{1,0:T(8,128)(2,1)S(1)} %get-tuple-element.55.low, f32[64,384]{1,0:T(8,128)S(1)} %maximum_add_fusion.total, f32[64,384]{1,0:T(8,128)S(1)} %collective-permute-done.12.other), custom_call_target="tpu_custom_call" | custom-call | tf_op jit(solution)/shard_map/pallas_call | solution.py:394
  (23 shorter events, 0.1 us)
Async XLA Ops:
  0.0 7.9 %copy-start.3 = (s32[1,1,4,8]{3,2,1,0:T(4,128)S(1)}, s32[1,1,4,8]{3,2,1,0:T(4,128)}, u32[]{:S(2)}) copy-start(s32[1,1,4,8]{3,2,1,0:T(4,128)} %src_rows) | copy-start | bytes 388
  0.0 7.9 %copy-start.2 = (f32[1,1,6,4,8]{4,3,2,1,0:T(4,128)S(1)}, f32[1,1,6,4,8]{4,3,2,1,0:T(4,128)}, u32[]{:S(2)}) copy-start(f32[1,1,6,4,8]{4,3,2,1,0:T(4,128)} %weights.1) | copy-start | bytes 2308
  0.0 7.9 %copy-start.5 = (s32[1,1,4]{2,1,0:T(1,128)S(1)}, s32[1,1,4]{2,1,0:T(1,128)}, u32[]{:S(2)}) copy-start(s32[1,1,4]{2,1,0:T(1,128)} %counts.1) | copy-start | bytes 52
  0.0 7.9 %copy-start.4 = (s32[1,1,4,8]{3,2,1,0:T(4,128)S(1)}, s32[1,1,4,8]{3,2,1,0:T(4,128)}, u32[]{:S(2)}) copy-start(s32[1,1,4,8]{3,2,1,0:T(4,128)} %dst_nodes.1) | copy-start | bytes 388
  0.0 7.9 %copy-start.1 = (f32[6,8,192]{2,1,0:T(8,128)S(1)}, f32[6,8,192]{2,1,0:T(8,128)}, u32[]{:S(2)}) copy-start(f32[6,8,192]{2,1,0:T(8,128)} %modes.1) | copy-start | bytes 110596
  1.1 21.4 %collective-permute-start.5 = (f32[32,2048]{1,0:T(8,128)S(1)}, f32[32,2048]{1,0:T(8,128)S(1)}, u32[]{:S(2)}, u32[]{:S(2)}) collective-permute-start(f32[32,2048]{1,0:T(8,128)S(1)} %constant_dynamic-slice_fusion.3), channel_id=1, source_target_pairs={{0,8},{4,12},{8,0},{12,4},{1,9},{5,13},{9,1},{13,5},{2,10},{6,14},... | collective-permute-start | bytes 786440 | tf_op jit(solution)/shard_map/ppermute | solution.py:20
  6.2 16.3 %collective-permute-start.4 = (f32[32,2048]{1,0:T(8,128)S(1)}, f32[32,2048]{1,0:T(8,128)S(1)}, u32[]{:S(2)}, u32[]{:S(2)}) collective-permute-start(f32[32,2048]{1,0:T(8,128)S(1)} %get-tuple-element.36), channel_id=1, source_target_pairs={{0,4},{4,0},{8,12},{12,8},{1,5},{5,1},{9,13},{13,9},{2,6},{6,2},{1... | collective-permute-start | bytes 786440 | tf_op jit(solution)/shard_map/ppermute | solution.py:20
  9.0 10.0 %collective-permute-start.3 = (f32[30,128]{1,0:T(8,128)S(1)}, f32[30,128]{1,0:T(8,128)S(1)}, u32[]{:S(2)}, u32[]{:S(2)}) collective-permute-start(f32[30,128]{1,0:T(8,128)S(1)} %shard_map.73.refs_0_), channel_id=1, source_target_pairs={{0,12},{4,8},{8,4},{12,0},{1,13},{5,9},{9,5},{13,1},{2,14},{6,10},... | collective-permute-start | bytes 46088 | tf_op jit(solution)/shard_map/ppermute | solution.py:20
  9.0 13.5 %collective-permute-start.2 = (f32[30,128]{1,0:T(8,128)S(1)}, f32[30,128]{1,0:T(8,128)S(1)}, u32[]{:S(2)}, u32[]{:S(2)}) collective-permute-start(f32[30,128]{1,0:T(8,128)S(1)} %shard_map.73.refs_0_), channel_id=1, source_target_pairs={{0,8},{4,12},{8,0},{12,4},{1,9},{5,13},{9,1},{13,5},{2,10},{6,14},... | collective-permute-start | bytes 46088 | tf_op jit(solution)/shard_map/ppermute | solution.py:20
  10.9 11.6 %collective-permute-start.1 = (f32[30,128]{1,0:T(8,128)S(1)}, f32[30,128]{1,0:T(8,128)S(1)}, u32[]{:S(2)}, u32[]{:S(2)}) collective-permute-start(f32[30,128]{1,0:T(8,128)S(1)} %shard_map.73.refs_0_), channel_id=1, source_target_pairs={{0,4},{4,0},{8,12},{12,8},{1,5},{5,1},{9,13},{13,9},{2,6},{6,2},{1... | collective-permute-start | bytes 46088 | tf_op jit(solution)/shard_map/ppermute | solution.py:20
  19.0 8.7 %collective-permute-start = (f32[32,2048]{1,0:T(8,128)S(1)}, f32[32,2048]{1,0:T(8,128)S(1)}, u32[]{:S(2)}, u32[]{:S(2)}) collective-permute-start(f32[32,2048]{1,0:T(8,128)S(1)} %get-tuple-element.34), channel_id=1, source_target_pairs={{0,12},{4,8},{8,4},{12,0},{1,13},{5,9},{9,5},{13,1},{2,14},{6,10},... | collective-permute-start | bytes 786440 | tf_op jit(solution)/shard_map/ppermute | solution.py:20
  22.5 4.3 %collective-permute-start.6 = (f32[1,4,30,128]{3,2,1,0:T(8,128)S(1)}, f32[1,4,30,128]{3,2,1,0:T(8,128)S(1)}, u32[]{:S(2)}, u32[]{:S(2)}) collective-permute-start(f32[1,4,30,128]{3,2,1,0:T(8,128)S(1)} %bitcast.6), channel_id=1, source_target_pairs={{0,2},{1,3},{2,0},{3,1},{4,6},{5,7},{6,4},{7,5},{8,10},{9,11},{10,... | collective-permute-start | bytes 184328 | tf_op jit(solution)/shard_map/ppermute | solution.py:20
  24.1 1.9 %copy-start = (f32[1,2048,384]{2,1,0:T(8,128)S(1)}, f32[1,2048,384]{2,1,0:T(8,128)}, u32[]{:S(2)}) copy-start(f32[1,2048,384]{2,1,0:T(8,128)} %param.8) | copy-start | bytes 9437188
  28.3 1.4 %collective-permute-start.7 = (f32[64,384]{1,0:T(8,128)S(1)}, f32[64,384]{1,0:T(8,128)S(1)}, u32[]{:S(2)}, u32[]{:S(2)}) collective-permute-start(f32[64,384]{1,0:T(8,128)S(1)} %get-tuple-element.50), channel_id=1, source_target_pairs={{0,1},{1,0},{2,3},{3,2},{4,5},{5,4},{6,7},{7,6},{8,9},{9,8},{10,11... | collective-permute-start | bytes 294920 | tf_op jit(solution)/shard_map/ppermute | solution.py:20
  29.7 4.9 %collective-permute-start.8 = (f32[64,384]{1,0:T(8,128)S(1)}, f32[64,384]{1,0:T(8,128)S(1)}, u32[]{:S(2)}, u32[]{:S(2)}) collective-permute-start(f32[64,384]{1,0:T(8,128)S(1)} %add.28), channel_id=1, source_target_pairs={{0,2},{1,3},{2,0},{3,1},{4,6},{5,7},{6,4},{7,5},{8,10},{9,11},{10,... | collective-permute-start | bytes 294920 | tf_op jit(solution)/shard_map/ppermute | solution.py:20
  31.2 14.8 %collective-permute-start.11 = (f32[2,4,30,128]{3,2,1,0:T(8,128)S(1)}, f32[2,4,30,128]{3,2,1,0:T(8,128)S(1)}, u32[]{:S(2)}, u32[]{:S(2)}) collective-permute-start(f32[2,4,30,128]{3,2,1,0:T(8,128)S(1)} %bitcast.4), channel_id=1, source_target_pairs={{0,1},{1,0},{2,3},{3,2},{4,5},{5,4},{6,7},{7,6},{8,9},{9,8},{10,11... | collective-permute-start | bytes 368648 | tf_op jit(solution)/shard_map/ppermute | solution.py:20
  34.6 8.1 %collective-permute-start.9 = (f32[64,384]{1,0:T(8,128)S(1)}, f32[64,384]{1,0:T(8,128)S(1)}, u32[]{:S(2)}, u32[]{:S(2)}) collective-permute-start(f32[64,384]{1,0:T(8,128)S(1)} %add.29), channel_id=1, source_target_pairs={{0,4},{4,0},{8,12},{12,8},{1,5},{5,1},{9,13},{13,9},{2,6},{6,2},{1... | collective-permute-start | bytes 294920 | tf_op jit(solution)/shard_map/ppermute | solution.py:20
  42.7 5.9 %collective-permute-start.10 = (f32[64,384]{1,0:T(8,128)S(1)}, f32[64,384]{1,0:T(8,128)S(1)}, u32[]{:S(2)}, u32[]{:S(2)}) collective-permute-start(f32[64,384]{1,0:T(8,128)S(1)} %add.30), channel_id=1, source_target_pairs={{0,8},{4,12},{8,0},{12,4},{1,9},{5,13},{9,1},{13,5},{2,10},{6,14},... | collective-permute-start | bytes 294920 | tf_op jit(solution)/shard_map/ppermute | solution.py:20
  48.6 1.4 %collective-permute-start.12 = (f32[64,384]{1,0:T(8,128)S(1)}, f32[64,384]{1,0:T(8,128)S(1)}, u32[]{:S(2)}, u32[]{:S(2)}) collective-permute-start(f32[64,384]{1,0:T(8,128)S(1)} %maximum_add_fusion.total), channel_id=1, source_target_pairs={{0,1},{1,0},{2,3},{3,2},{4,5},{5,4},{6,7},{7,6},{8,9},{9,8},{10,11... | collective-permute-start | bytes 294920 | tf_op jit(solution)/shard_map/ppermute | solution.py:20

commit v4 on v3

--- a/solution.py
+++ b/solution.py
@@ -357,10 +357,10 @@
         compiler_params=ROOM,
         cost_estimate=cost(0.001),
     )(lists, dst_nodes, counts, spline_weights, node_modes)
-    last = swap(after(last, pack), "blk", far_masks[-1])
+    last = swap(last, "blk", far_masks[-1])
     packs = [pack] + [swap(pack, "blk", mask) for mask in range(1, blk_count)]
-    waiting = lax.optimization_barrier((*packs, *near, *far))
-    packs, near, far = waiting[:blk_count], waiting[blk_count : blk_count + half], waiting[blk_count + half :]
+    waiting = lax.optimization_barrier((*packs[::-1], *near, *far))
+    packs, near, far = waiting[:blk_count][::-1], waiting[blk_count : blk_count + half], waiting[blk_count + half :]
     packs = joined(*packs)[None]
     for mask in masks("col")[:0:-1]:
         packs = joined(packs, swap(packs, "col", mask)).reshape(-1, *packs.shape[1:])

time: 51.2 us -> 49.8 us (0.973)
  starting transfers between devices: 24.7 us -> 22.2 us
  waiting for transfers between devices: 16.4 us -> 17.5 us
    ppermute x13, starting transfers between devices: 24.7 us -> 22.2 us  [swap(): return lax.ppermute(value, axis, pairs)]
    ppermute x13, waiting for transfers between devices: 16.4 us -> 17.5 us  [swap(): return lax.ppermute(value, axis, pairs)]
where the time goes in v4:
time: 49.8 us; the launch traced here: 49.6 us
  starting transfers between devices  22.2 us (45%)
  waiting for transfers between devices  17.5 us (35%)
  local copies, waits for them, and re-layouts  4.98 us (10%)
  Pallas kernels  4.62 us (9%)
    ppermute x13, starting transfers between devices, swap(): return lax.ppermute(value, axis, pairs)  22.2 us
    ppermute x13, waiting for transfers between devices, swap(): return lax.ppermute(value, axis, pairs)  17.5 us
    dynamic_slice x3, local copies, waits for them, and re-layouts, columns(): return lax.dynamic_slice_in_dim(source, (blk ^ mask) * panels, panels, 1)  3.06 us
    unnamed x12, local copies, waits for them, and re-layouts  1.91 us
    pallas_call x1, Pallas kernels, shards(): pl.pallas_call(spline_kernel, out_shape=f32(folded(sub_rows) + folded(sha...  1.06 us
  transfers between devices with their start and end apart: 13, of which 7 were waited for; matrix products, arithmetic and copies ran while one was open for 4% of the time, Pallas kernels for 6%

profile of v4, /device:TPU:0, one launch (start us, length us, event | category | flops | bytes accessed | tf_op | source)
XLA Modules:
  0.0 49.6 jit_solution(1310261705424111786)
XLA Ops:
  0.0 1.0 %constant_dynamic-slice_fusion.3 = f32[32,2048]{1,0:T(8,128)S(1)} fusion(f32[32,8192]{1,0:T(8,128)} %param.7, s32[]{:T(128)S(6)} %select_n.12), kind=kLoop, calls=%fused_computation.5 | loop fusion | bytes 524292 | tf_op jit(solution)/shard_map/dynamic_slice | solution.py:339
  1.1 4.1 %collective-permute-start.5 = (f32[32,2048]{1,0:T(8,128)S(1)}, f32[32,2048]{1,0:T(8,128)S(1)}, u32[]{:S(2)}, u32[]{:S(2)}) collective-permute-start(f32[32,2048]{1,0:T(8,128)S(1)} %constant_dynamic-slice_fusion.3), channel_id=1, source_target_pairs={{0,8},{4,12},{8,0},{12,4},{1,9},{5,13},{9,1},{13,5},{2,10},{6,14},... | collective-permute-start | bytes 786440 | tf_op jit(solution)/shard_map/ppermute | solution.py:20
  5.2 1.1 %constant_dynamic-slice_fusion.1 = (f32[32,2048]{1,0:T(8,128)S(1)}, f32[32,2048]{1,0:T(8,128)S(1)}) fusion(f32[32,8192]{1,0:T(8,128)} %param.7, s32[]{:T(128)S(6)} %select_n.14, s32[]{:T(128)S(6)} %select_n.13), kind=kLoop, calls=%fused_computation.3 | loop fusion | bytes 1048584 | tf_op jit(solution)/shard_map/dynamic_slice | solution.py:339
  6.2 1.6 %collective-permute-start.4 = (f32[32,2048]{1,0:T(8,128)S(1)}, f32[32,2048]{1,0:T(8,128)S(1)}, u32[]{:S(2)}, u32[]{:S(2)}) collective-permute-start(f32[32,2048]{1,0:T(8,128)S(1)} %get-tuple-element.34), channel_id=1, source_target_pairs={{0,4},{4,0},{8,12},{12,8},{1,5},{5,1},{9,13},{13,9},{2,6},{6,2},{1... | collective-permute-start | bytes 786440 | tf_op jit(solution)/shard_map/ppermute | solution.py:20
  7.9 1.1 %shard_map.73.refs_0_ = f32[30,128]{1,0:T(8,128)S(1)} custom-call(s32[1,1,4,8]{3,2,1,0:T(4,128)S(1)} %copy-done.3, s32[1,1,4,8]{3,2,1,0:T(4,128)S(1)} %copy-done.4, s32[1,1,4]{2,1,0:T(1,128)S(1)} %copy-done.5, f32[1,1,6,4,8]{4,3,2,1,0:T(4,128)S(1)} %copy-done.2, f32[6,8,192]{2,1,0:T(8,128)S(1)} %copy-done.1), custom_call_target="tpu_custom_call" | custom-call | bytes 3500 | tf_op jit(solution)/shard_map/pallas_call | solution.py:352
  9.0 0.5 collective-permute-start.3
  9.4 0.0 collective-permute-start.2
  9.5 3.9 %collective-permute-start.1 = (f32[30,128]{1,0:T(8,128)S(1)}, f32[30,128]{1,0:T(8,128)S(1)}, u32[]{:S(2)}, u32[]{:S(2)}) collective-permute-start(f32[30,128]{1,0:T(8,128)S(1)} %shard_map.73.refs_0_), channel_id=1, source_target_pairs={{0,12},{4,8},{8,4},{12,0},{1,13},{5,9},{9,5},{13,1},{2,14},{6,10},... | collective-permute-start | bytes 46088 | tf_op jit(solution)/shard_map/ppermute | solution.py:20
  13.4 6.2 %collective-permute-done.3.refs_1_ = f32[30,128]{1,0:T(8,128)S(1)} collective-permute-done((f32[30,128]{1,0:T(8,128)S(1)}, f32[30,128]{1,0:T(8,128)S(1)}, u32[]{:S(2)}, u32[]{:S(2)}) %collective-permute-start.3) | collective-permute-done | bytes 15392 | tf_op jit(solution)/shard_map/ppermute | solution.py:20
  19.6 2.5 %collective-permute-start = (f32[32,2048]{1,0:T(8,128)S(1)}, f32[32,2048]{1,0:T(8,128)S(1)}, u32[]{:S(2)}, u32[]{:S(2)}) collective-permute-start(f32[32,2048]{1,0:T(8,128)S(1)} %get-tuple-element.31), channel_id=1, source_target_pairs={{0,12},{4,8},{8,4},{12,0},{1,13},{5,9},{9,5},{13,1},{2,14},{6,10},... | collective-permute-start | bytes 786440 | tf_op jit(solution)/shard_map/ppermute | solution.py:20
  22.1 1.0 %constant_dynamic-slice_fusion.refs_0_ = f32[32,2048]{1,0:T(8,128)S(1)} fusion(f32[32,8192]{1,0:T(8,128)} %param.7, s32[]{:T(128)S(6)} %select_n.15), kind=kLoop, calls=%fused_computation.2 | loop fusion | bytes 524292 | tf_op jit(solution)/shard_map/dynamic_slice | solution.py:339
  23.0 0.0 collective-permute-done.2.refs_2_
  23.0 0.0 collective-permute-done.1.refs_3_
  23.0 0.0 collective-permute-done.5.refs_2_
  23.1 1.6 %collective-permute-start.6 = (f32[1,4,30,128]{3,2,1,0:T(8,128)S(1)}, f32[1,4,30,128]{3,2,1,0:T(8,128)S(1)}, u32[]{:S(2)}, u32[]{:S(2)}) collective-permute-start(f32[1,4,30,128]{3,2,1,0:T(8,128)S(1)} %bitcast.6), channel_id=1, source_target_pairs={{0,2},{1,3},{2,0},{3,1},{4,6},{5,7},{6,4},{7,5},{8,10},{9,11},{10,... | collective-permute-start | bytes 184328 | tf_op jit(solution)/shard_map/ppermute | solution.py:20
  24.6 1.9 %copy-done = f32[1,2048,384]{2,1,0:T(8,128)S(1)} copy-done((f32[1,2048,384]{2,1,0:T(8,128)S(1)}, f32[1,2048,384]{2,1,0:T(8,128)}, u32[]{:S(2)}) %copy-start) | copy-done | bytes 3145752
  26.5 0.7 %shard_map.76 = (bf16[2048,384]{1,0:T(8,128)(2,1)S(1)}, bf16[2048,384]{1,0:T(8,128)(2,1)S(1)}) custom-call(f32[2048,384]{1,0:T(8,128)S(1)} %bitcast.3), custom_call_target="tpu_custom_call" | custom-call | bytes 3500 | tf_op jit(solution)/shard_map/pallas_call | solution.py:236
  27.2 0.2 collective-permute-done.6.refs_1_
  27.4 0.8 %shard_map.77.refs_1_ = f32[96,384]{1,0:T(8,128)S(1)} custom-call(f32[32,2048]{1,0:T(8,128)S(1)} %constant_dynamic-slice_fusion.refs_0_, f32[32,2048]{1,0:T(8,128)S(1)} %collective-permute-done.4.refs_1_, f32[32,2048]{1,0:T(8,128)S(1)} %collective-permute-done.5.refs_2_, bf16[2048,384]{1,0:T(8,128)(2,1)S(1)} %get-tuple-element.45.refs_3_.refs_2_, ...), custom_call_target="tpu_custom_call" | custom-call | bytes 3500 | tf_op jit(solution)/shard_map/pallas_call | solution.py:284
  28.2 0.6 %shard_map.78 = (f32[64,384]{1,0:T(8,128)S(1)}, f32[64,384]{1,0:T(8,128)S(1)}) custom-call(f32[32,2048]{1,0:T(8,128)S(1)} %collective-permute-done.refs_0_, f32[96,384]{1,0:T(8,128)S(1)} %shard_map.77.refs_1_, bf16[2048,384]{1,0:T(8,128)(2,1)S(1)} %get-tuple-element.45.refs_3_.refs_2_, bf16[2048,384]{1,0:T(8,128)(2,1)S(1)} %get-tuple-element.46.refs_4_.refs_3_), custom_call_target="tpu_custom_call" | custom-call | bytes 3500 | tf_op jit(solution)/shard_map/pallas_call | solution.py:297
  28.8 0.1 collective-permute-start.7
  28.9 1.3 %collective-permute-done.7 = f32[64,384]{1,0:T(8,128)S(1)} collective-permute-done((f32[64,384]{1,0:T(8,128)S(1)}, f32[64,384]{1,0:T(8,128)S(1)}, u32[]{:S(2)}, u32[]{:S(2)}) %collective-permute-start.7) | collective-permute-done | bytes 98336 | tf_op jit(solution)/shard_map/ppermute | solution.py:20
  30.2 1.6 %collective-permute-start.8 = (f32[64,384]{1,0:T(8,128)S(1)}, f32[64,384]{1,0:T(8,128)S(1)}, u32[]{:S(2)}, u32[]{:S(2)}) collective-permute-start(f32[64,384]{1,0:T(8,128)S(1)} %add.28), channel_id=1, source_target_pairs={{0,2},{1,3},{2,0},{3,1},{4,6},{5,7},{6,4},{7,5},{8,10},{9,11},{10,... | collective-permute-start | bytes 294920 | tf_op jit(solution)/shard_map/ppermute | solution.py:20
  31.8 3.4 %collective-permute-done.8 = f32[64,384]{1,0:T(8,128)S(1)} collective-permute-done((f32[64,384]{1,0:T(8,128)S(1)}, f32[64,384]{1,0:T(8,128)S(1)}, u32[]{:S(2)}, u32[]{:S(2)}) %collective-permute-start.8) | collective-permute-done | bytes 98336 | tf_op jit(solution)/shard_map/ppermute | solution.py:20
  35.2 3.8 %collective-permute-start.9 = (f32[64,384]{1,0:T(8,128)S(1)}, f32[64,384]{1,0:T(8,128)S(1)}, u32[]{:S(2)}, u32[]{:S(2)}) collective-permute-start(f32[64,384]{1,0:T(8,128)S(1)} %add.29), channel_id=1, source_target_pairs={{0,4},{4,0},{8,12},{12,8},{1,5},{5,1},{9,13},{13,9},{2,6},{6,2},{1... | collective-permute-start | bytes 294920 | tf_op jit(solution)/shard_map/ppermute | solution.py:20
  39.0 2.6 %collective-permute-done.9 = f32[64,384]{1,0:T(8,128)S(1)} collective-permute-done((f32[64,384]{1,0:T(8,128)S(1)}, f32[64,384]{1,0:T(8,128)S(1)}, u32[]{:S(2)}, u32[]{:S(2)}) %collective-permute-start.9) | collective-permute-done | bytes 98336 | tf_op jit(solution)/shard_map/ppermute | solution.py:20
  41.6 2.5 %collective-permute-start.10 = (f32[64,384]{1,0:T(8,128)S(1)}, f32[64,384]{1,0:T(8,128)S(1)}, u32[]{:S(2)}, u32[]{:S(2)}) collective-permute-start(f32[64,384]{1,0:T(8,128)S(1)} %add.30), channel_id=1, source_target_pairs={{0,8},{4,12},{8,0},{12,4},{1,9},{5,13},{9,1},{13,5},{2,10},{6,14},... | collective-permute-start | bytes 294920 | tf_op jit(solution)/shard_map/ppermute | solution.py:20
  44.1 0.5 shard_map.79
  44.6 2.6 %collective-permute-done.10 = f32[64,384]{1,0:T(8,128)S(1)} collective-permute-done((f32[64,384]{1,0:T(8,128)S(1)}, f32[64,384]{1,0:T(8,128)S(1)}, u32[]{:S(2)}, u32[]{:S(2)}) %collective-permute-start.10) | collective-permute-done | bytes 98336 | tf_op jit(solution)/shard_map/ppermute | solution.py:20
  47.2 0.1 collective-permute-start.12
  47.3 1.3 %collective-permute-done.12.other = f32[64,384]{1,0:T(8,128)S(1)} collective-permute-done((f32[64,384]{1,0:T(8,128)S(1)}, f32[64,384]{1,0:T(8,128)S(1)}, u32[]{:S(2)}, u32[]{:S(2)}) %collective-permute-start.12) | collective-permute-done | bytes 98336 | tf_op jit(solution)/shard_map/ppermute | solution.py:20
  48.6 1.0 %shard_map.80 = f32[192,384]{1,0:T(8,128)} custom-call(bf16[192,128]{1,0:T(8,128)(2,1)S(1)} %get-tuple-element.52.high, bf16[192,128]{1,0:T(8,128)(2,1)S(1)} %get-tuple-element.53.low, f32[64,384]{1,0:T(8,128)S(1)} %maximum_add_fusion.total, f32[64,384]{1,0:T(8,128)S(1)} %collective-permute-done.12.other), custom_call_target="tpu_custom_call" | custom-call | tf_op jit(solution)/shard_map/pallas_call | solution.py:394
  (23 shorter events, 0.1 us)
Async XLA Ops:
  0.0 7.9 %copy-start.3 = (s32[1,1,4,8]{3,2,1,0:T(4,128)S(1)}, s32[1,1,4,8]{3,2,1,0:T(4,128)}, u32[]{:S(2)}) copy-start(s32[1,1,4,8]{3,2,1,0:T(4,128)} %src_rows) | copy-start | bytes 388
  0.0 7.9 %copy-start.2 = (f32[1,1,6,4,8]{4,3,2,1,0:T(4,128)S(1)}, f32[1,1,6,4,8]{4,3,2,1,0:T(4,128)}, u32[]{:S(2)}) copy-start(f32[1,1,6,4,8]{4,3,2,1,0:T(4,128)} %weights.1) | copy-start | bytes 2308
  0.0 7.9 %copy-start.5 = (s32[1,1,4]{2,1,0:T(1,128)S(1)}, s32[1,1,4]{2,1,0:T(1,128)}, u32[]{:S(2)}) copy-start(s32[1,1,4]{2,1,0:T(1,128)} %counts.1) | copy-start | bytes 52
  0.0 7.9 %copy-start.4 = (s32[1,1,4,8]{3,2,1,0:T(4,128)S(1)}, s32[1,1,4,8]{3,2,1,0:T(4,128)}, u32[]{:S(2)}) copy-start(s32[1,1,4,8]{3,2,1,0:T(4,128)} %dst_nodes.1) | copy-start | bytes 388
  0.0 7.9 %copy-start.1 = (f32[6,8,192]{2,1,0:T(8,128)S(1)}, f32[6,8,192]{2,1,0:T(8,128)}, u32[]{:S(2)}) copy-start(f32[6,8,192]{2,1,0:T(8,128)} %modes.1) | copy-start | bytes 110596
  1.1 22.0 %collective-permute-start.5 = (f32[32,2048]{1,0:T(8,128)S(1)}, f32[32,2048]{1,0:T(8,128)S(1)}, u32[]{:S(2)}, u32[]{:S(2)}) collective-permute-start(f32[32,2048]{1,0:T(8,128)S(1)} %constant_dynamic-slice_fusion.3), channel_id=1, source_target_pairs={{0,8},{4,12},{8,0},{12,4},{1,9},{5,13},{9,1},{13,5},{2,10},{6,14},... | collective-permute-start | bytes 786440 | tf_op jit(solution)/shard_map/ppermute | solution.py:20
  6.2 16.8 %collective-permute-start.4 = (f32[32,2048]{1,0:T(8,128)S(1)}, f32[32,2048]{1,0:T(8,128)S(1)}, u32[]{:S(2)}, u32[]{:S(2)}) collective-permute-start(f32[32,2048]{1,0:T(8,128)S(1)} %get-tuple-element.34), channel_id=1, source_target_pairs={{0,4},{4,0},{8,12},{12,8},{1,5},{5,1},{9,13},{13,9},{2,6},{6,2},{1... | collective-permute-start | bytes 786440 | tf_op jit(solution)/shard_map/ppermute | solution.py:20
  9.0 10.6 %collective-permute-start.3 = (f32[30,128]{1,0:T(8,128)S(1)}, f32[30,128]{1,0:T(8,128)S(1)}, u32[]{:S(2)}, u32[]{:S(2)}) collective-permute-start(f32[30,128]{1,0:T(8,128)S(1)} %shard_map.73.refs_0_), channel_id=1, source_target_pairs={{0,4},{4,0},{8,12},{12,8},{1,5},{5,1},{9,13},{13,9},{2,6},{6,2},{1... | collective-permute-start | bytes 46088 | tf_op jit(solution)/shard_map/ppermute | solution.py:20
  9.4 13.6 %collective-permute-start.2 = (f32[30,128]{1,0:T(8,128)S(1)}, f32[30,128]{1,0:T(8,128)S(1)}, u32[]{:S(2)}, u32[]{:S(2)}) collective-permute-start(f32[30,128]{1,0:T(8,128)S(1)} %shard_map.73.refs_0_), channel_id=1, source_target_pairs={{0,8},{4,12},{8,0},{12,4},{1,9},{5,13},{9,1},{13,5},{2,10},{6,14},... | collective-permute-start | bytes 46088 | tf_op jit(solution)/shard_map/ppermute | solution.py:20
  9.5 13.6 %collective-permute-start.1 = (f32[30,128]{1,0:T(8,128)S(1)}, f32[30,128]{1,0:T(8,128)S(1)}, u32[]{:S(2)}, u32[]{:S(2)}) collective-permute-start(f32[30,128]{1,0:T(8,128)S(1)} %shard_map.73.refs_0_), channel_id=1, source_target_pairs={{0,12},{4,8},{8,4},{12,0},{1,13},{5,9},{9,5},{13,1},{2,14},{6,10},... | collective-permute-start | bytes 46088 | tf_op jit(solution)/shard_map/ppermute | solution.py:20
  19.6 8.7 %collective-permute-start = (f32[32,2048]{1,0:T(8,128)S(1)}, f32[32,2048]{1,0:T(8,128)S(1)}, u32[]{:S(2)}, u32[]{:S(2)}) collective-permute-start(f32[32,2048]{1,0:T(8,128)S(1)} %get-tuple-element.31), channel_id=1, source_target_pairs={{0,12},{4,8},{8,4},{12,0},{1,13},{5,9},{9,5},{13,1},{2,14},{6,10},... | collective-permute-start | bytes 786440 | tf_op jit(solution)/shard_map/ppermute | solution.py:20
  23.1 4.3 %collective-permute-start.6 = (f32[1,4,30,128]{3,2,1,0:T(8,128)S(1)}, f32[1,4,30,128]{3,2,1,0:T(8,128)S(1)}, u32[]{:S(2)}, u32[]{:S(2)}) collective-permute-start(f32[1,4,30,128]{3,2,1,0:T(8,128)S(1)} %bitcast.6), channel_id=1, source_target_pairs={{0,2},{1,3},{2,0},{3,1},{4,6},{5,7},{6,4},{7,5},{8,10},{9,11},{10,... | collective-permute-start | bytes 184328 | tf_op jit(solution)/shard_map/ppermute | solution.py:20
  24.6 1.9 %copy-start = (f32[1,2048,384]{2,1,0:T(8,128)S(1)}, f32[1,2048,384]{2,1,0:T(8,128)}, u32[]{:S(2)}) copy-start(f32[1,2048,384]{2,1,0:T(8,128)} %param.8) | copy-start | bytes 9437188
  28.8 1.4 %collective-permute-start.7 = (f32[64,384]{1,0:T(8,128)S(1)}, f32[64,384]{1,0:T(8,128)S(1)}, u32[]{:S(2)}, u32[]{:S(2)}) collective-permute-start(f32[64,384]{1,0:T(8,128)S(1)} %get-tuple-element.48), channel_id=1, source_target_pairs={{0,1},{1,0},{2,3},{3,2},{4,5},{5,4},{6,7},{7,6},{8,9},{9,8},{10,11... | collective-permute-start | bytes 294920 | tf_op jit(solution)/shard_map/ppermute | solution.py:20
  30.2 4.9 %collective-permute-start.8 = (f32[64,384]{1,0:T(8,128)S(1)}, f32[64,384]{1,0:T(8,128)S(1)}, u32[]{:S(2)}, u32[]{:S(2)}) collective-permute-start(f32[64,384]{1,0:T(8,128)S(1)} %add.28), channel_id=1, source_target_pairs={{0,2},{1,3},{2,0},{3,1},{4,6},{5,7},{6,4},{7,5},{8,10},{9,11},{10,... | collective-permute-start | bytes 294920 | tf_op jit(solution)/shard_map/ppermute | solution.py:20
  31.8 12.3 %collective-permute-start.11 = (f32[2,4,30,128]{3,2,1,0:T(8,128)S(1)}, f32[2,4,30,128]{3,2,1,0:T(8,128)S(1)}, u32[]{:S(2)}, u32[]{:S(2)}) collective-permute-start(f32[2,4,30,128]{3,2,1,0:T(8,128)S(1)} %bitcast.4), channel_id=1, source_target_pairs={{0,1},{1,0},{2,3},{3,2},{4,5},{5,4},{6,7},{7,6},{8,9},{9,8},{10,11... | collective-permute-start | bytes 368648 | tf_op jit(solution)/shard_map/ppermute | solution.py:20
  35.2 6.4 %collective-permute-start.9 = (f32[64,384]{1,0:T(8,128)S(1)}, f32[64,384]{1,0:T(8,128)S(1)}, u32[]{:S(2)}, u32[]{:S(2)}) collective-permute-start(f32[64,384]{1,0:T(8,128)S(1)} %add.29), channel_id=1, source_target_pairs={{0,4},{4,0},{8,12},{12,8},{1,5},{5,1},{9,13},{13,9},{2,6},{6,2},{1... | collective-permute-start | bytes 294920 | tf_op jit(solution)/shard_map/ppermute | solution.py:20
  41.6 5.6 %collective-permute-start.10 = (f32[64,384]{1,0:T(8,128)S(1)}, f32[64,384]{1,0:T(8,128)S(1)}, u32[]{:S(2)}, u32[]{:S(2)}) collective-permute-start(f32[64,384]{1,0:T(8,128)S(1)} %add.30), channel_id=1, source_target_pairs={{0,8},{4,12},{8,0},{12,4},{1,9},{5,13},{9,1},{13,5},{2,10},{6,14},... | collective-permute-start | bytes 294920 | tf_op jit(solution)/shard_map/ppermute | solution.py:20
  47.2 1.4 %collective-permute-start.12 = (f32[64,384]{1,0:T(8,128)S(1)}, f32[64,384]{1,0:T(8,128)S(1)}, u32[]{:S(2)}, u32[]{:S(2)}) collective-permute-start(f32[64,384]{1,0:T(8,128)S(1)} %maximum_add_fusion.total), channel_id=1, source_target_pairs={{0,1},{1,0},{2,3},{3,2},{4,5},{5,4},{6,7},{7,6},{8,9},{9,8},{10,11... | collective-permute-start | bytes 294920 | tf_op jit(solution)/shard_map/ppermute | solution.py:20

commit v5 on v4

--- a/solution.py
+++ b/solution.py
@@ -202,9 +202,19 @@
     high[...], low[...] = split(whole)
 
 
-def last_kernel(high, low, total, other, out):
-    right_high, right_low = split(jnp.concatenate([total[...], other[...]]))
-    out[...] = mxu(high[...], right_high) + (mxu(high[...], right_low) + mxu(low[...], right_high))
+def modal(high, low, rows):
+    right_high, right_low = split(rows[...])
+    return mxu(high, right_high) + (mxu(high, right_low) + mxu(low, right_high))
+
+
+def base_kernel(high, low, total, out):
+    count = total.shape[0]
+    out[...] = modal(high[:, :count], low[:, :count], total)
+
+
+def last_kernel(high, low, base, other, out):
+    count = other.shape[0]
+    out[...] = base[...] + modal(high[:, count:], low[:, count:], other)
 
 
 def split(value):
@@ -391,11 +401,20 @@
     rows = total.shape[0] // 2
     total = total + jnp.concatenate([there[rows:], there[:rows]])
     other = swap(total, "col", 1)
+    base = pl.pallas_call(
+        base_kernel,
+        out_shape=f32(modes, width),
+        in_specs=[VMEM] * 3,
+        out_specs=VMEM,
+        compiler_params=ROOM,
+        cost_estimate=cost(1),
+    )(*transfer, total)
     return pl.pallas_call(
         last_kernel,
         out_shape=f32(modes, width),
-        compiler_params=ROOM,
-    )(*transfer, total, other)
+        in_specs=[VMEM] * 4,
+        compiler_params=ROOM,
+    )(*transfer, base, other)
 
 
 def solution(mesh):

time: 49.8 us -> 49.8 us (level)
    pallas_call x1 -> x2, Pallas kernels: 0.98 us -> 1.28 us  [the longest x1 1.03 us: shards(): pl.pallas_call(last_kernel, out_shape=f32(modes, width), in_specs=[VMEM]...]
  transfers between devices with their start and end apart: 13 -> 13, of which waited for: 7 -> 7; matrix products, arithmetic and copies ran while one was open for 4% -> 4% of each run, Pallas kernels for 6% -> 7%
where the time goes in v5:
time: 49.8 us; the launch traced here: 49.6 us
  starting transfers between devices  22.2 us (45%)
  waiting for transfers between devices  17.3 us (35%)
  local copies, waits for them, and re-layouts  4.98 us (10%)
  Pallas kernels  4.91 us (10%)
    ppermute x13, starting transfers between devices, swap(): return lax.ppermute(value, axis, pairs)  22.2 us
    ppermute x13, waiting for transfers between devices, swap(): return lax.ppermute(value, axis, pairs)  17.3 us
    dynamic_slice x3, local copies, waits for them, and re-layouts, columns(): return lax.dynamic_slice_in_dim(source, (blk ^ mask) * panels, panels, 1)  3.06 us
    unnamed x12, local copies, waits for them, and re-layouts  1.91 us
    pallas_call x1, Pallas kernels, shards(): pl.pallas_call(spline_kernel, out_shape=f32(folded(sub_rows) + folded(sha...  1.06 us
    pallas_call x1, Pallas kernels, shards(): pl.pallas_call(last_kernel, out_shape=f32(modes, width), in_specs=[VMEM]...  1.03 us
  transfers between devices with their start and end apart: 13, of which 7 were waited for; matrix products, arithmetic and copies ran while one was open for 4% of the time, Pallas kernels for 7%

profile of v5, /device:TPU:0, one launch (start us, length us, event | category | flops | bytes accessed | tf_op | source)
XLA Modules:
  0.0 49.6 jit_solution(15703835315190654463)
XLA Ops:
  0.0 1.0 %constant_dynamic-slice_fusion.3 = f32[32,2048]{1,0:T(8,128)S(1)} fusion(f32[32,8192]{1,0:T(8,128)} %param.7, s32[]{:T(128)S(6)} %select_n.12), kind=kLoop, calls=%fused_computation.5 | loop fusion | bytes 524292 | tf_op jit(solution)/shard_map/dynamic_slice | solution.py:349
  1.1 4.1 %collective-permute-start.5 = (f32[32,2048]{1,0:T(8,128)S(1)}, f32[32,2048]{1,0:T(8,128)S(1)}, u32[]{:S(2)}, u32[]{:S(2)}) collective-permute-start(f32[32,2048]{1,0:T(8,128)S(1)} %constant_dynamic-slice_fusion.3), channel_id=1, source_target_pairs={{0,8},{4,12},{8,0},{12,4},{1,9},{5,13},{9,1},{13,5},{2,10},{6,14},... | collective-permute-start | bytes 786440 | tf_op jit(solution)/shard_map/ppermute | solution.py:20
  5.2 1.1 %constant_dynamic-slice_fusion.1 = (f32[32,2048]{1,0:T(8,128)S(1)}, f32[32,2048]{1,0:T(8,128)S(1)}) fusion(f32[32,8192]{1,0:T(8,128)} %param.7, s32[]{:T(128)S(6)} %select_n.14, s32[]{:T(128)S(6)} %select_n.13), kind=kLoop, calls=%fused_computation.3 | loop fusion | bytes 1048584 | tf_op jit(solution)/shard_map/dynamic_slice | solution.py:349
  6.2 1.6 %collective-permute-start.4 = (f32[32,2048]{1,0:T(8,128)S(1)}, f32[32,2048]{1,0:T(8,128)S(1)}, u32[]{:S(2)}, u32[]{:S(2)}) collective-permute-start(f32[32,2048]{1,0:T(8,128)S(1)} %get-tuple-element.34), channel_id=1, source_target_pairs={{0,4},{4,0},{8,12},{12,8},{1,5},{5,1},{9,13},{13,9},{2,6},{6,2},{1... | collective-permute-start | bytes 786440 | tf_op jit(solution)/shard_map/ppermute | solution.py:20
  7.9 1.1 %shard_map.73.refs_0_ = f32[30,128]{1,0:T(8,128)S(1)} custom-call(s32[1,1,4,8]{3,2,1,0:T(4,128)S(1)} %copy-done.3, s32[1,1,4,8]{3,2,1,0:T(4,128)S(1)} %copy-done.4, s32[1,1,4]{2,1,0:T(1,128)S(1)} %copy-done.5, f32[1,1,6,4,8]{4,3,2,1,0:T(4,128)S(1)} %copy-done.2, f32[6,8,192]{2,1,0:T(8,128)S(1)} %copy-done.1), custom_call_target="tpu_custom_call" | custom-call | bytes 3500 | tf_op jit(solution)/shard_map/pallas_call | solution.py:362
  9.0 0.5 collective-permute-start.3
  9.4 0.0 collective-permute-start.2
  9.5 3.9 %collective-permute-start.1 = (f32[30,128]{1,0:T(8,128)S(1)}, f32[30,128]{1,0:T(8,128)S(1)}, u32[]{:S(2)}, u32[]{:S(2)}) collective-permute-start(f32[30,128]{1,0:T(8,128)S(1)} %shard_map.73.refs_0_), channel_id=1, source_target_pairs={{0,12},{4,8},{8,4},{12,0},{1,13},{5,9},{9,5},{13,1},{2,14},{6,10},... | collective-permute-start | bytes 46088 | tf_op jit(solution)/shard_map/ppermute | solution.py:20
  13.4 6.2 %collective-permute-done.3.refs_1_ = f32[30,128]{1,0:T(8,128)S(1)} collective-permute-done((f32[30,128]{1,0:T(8,128)S(1)}, f32[30,128]{1,0:T(8,128)S(1)}, u32[]{:S(2)}, u32[]{:S(2)}) %collective-permute-start.3) | collective-permute-done | bytes 15392 | tf_op jit(solution)/shard_map/ppermute | solution.py:20
  19.6 2.5 %collective-permute-start = (f32[32,2048]{1,0:T(8,128)S(1)}, f32[32,2048]{1,0:T(8,128)S(1)}, u32[]{:S(2)}, u32[]{:S(2)}) collective-permute-start(f32[32,2048]{1,0:T(8,128)S(1)} %get-tuple-element.31), channel_id=1, source_target_pairs={{0,12},{4,8},{8,4},{12,0},{1,13},{5,9},{9,5},{13,1},{2,14},{6,10},... | collective-permute-start | bytes 786440 | tf_op jit(solution)/shard_map/ppermute | solution.py:20
  22.1 1.0 %constant_dynamic-slice_fusion.refs_0_ = f32[32,2048]{1,0:T(8,128)S(1)} fusion(f32[32,8192]{1,0:T(8,128)} %param.7, s32[]{:T(128)S(6)} %select_n.15), kind=kLoop, calls=%fused_computation.2 | loop fusion | bytes 524292 | tf_op jit(solution)/shard_map/dynamic_slice | solution.py:349
  23.0 0.0 collective-permute-done.2.refs_2_
  23.0 0.0 collective-permute-done.1.refs_3_
  23.1 1.6 %collective-permute-start.6 = (f32[1,4,30,128]{3,2,1,0:T(8,128)S(1)}, f32[1,4,30,128]{3,2,1,0:T(8,128)S(1)}, u32[]{:S(2)}, u32[]{:S(2)}) collective-permute-start(f32[1,4,30,128]{3,2,1,0:T(8,128)S(1)} %bitcast.6), channel_id=1, source_target_pairs={{0,2},{1,3},{2,0},{3,1},{4,6},{5,7},{6,4},{7,5},{8,10},{9,11},{10,... | collective-permute-start | bytes 184328 | tf_op jit(solution)/shard_map/ppermute | solution.py:20
  24.6 1.9 %copy-done = f32[1,2048,384]{2,1,0:T(8,128)S(1)} copy-done((f32[1,2048,384]{2,1,0:T(8,128)S(1)}, f32[1,2048,384]{2,1,0:T(8,128)}, u32[]{:S(2)}) %copy-start) | copy-done | bytes 3145752
  26.5 0.7 %shard_map.76 = (bf16[2048,384]{1,0:T(8,128)(2,1)S(1)}, bf16[2048,384]{1,0:T(8,128)(2,1)S(1)}) custom-call(f32[2048,384]{1,0:T(8,128)S(1)} %bitcast.3), custom_call_target="tpu_custom_call" | custom-call | bytes 3500 | tf_op jit(solution)/shard_map/pallas_call | solution.py:246
  27.2 0.2 collective-permute-done.6.refs_1_
  27.4 0.8 %shard_map.77.refs_1_ = f32[96,384]{1,0:T(8,128)S(1)} custom-call(f32[32,2048]{1,0:T(8,128)S(1)} %constant_dynamic-slice_fusion.refs_0_, f32[32,2048]{1,0:T(8,128)S(1)} %collective-permute-done.4.refs_1_, f32[32,2048]{1,0:T(8,128)S(1)} %collective-permute-done.5.refs_2_, bf16[2048,384]{1,0:T(8,128)(2,1)S(1)} %get-tuple-element.45.refs_3_.refs_2_, ...), custom_call_target="tpu_custom_call" | custom-call | bytes 3500 | tf_op jit(solution)/shard_map/pallas_call | solution.py:294
  28.2 0.6 %shard_map.78 = (f32[64,384]{1,0:T(8,128)S(1)}, f32[64,384]{1,0:T(8,128)S(1)}) custom-call(f32[32,2048]{1,0:T(8,128)S(1)} %collective-permute-done.refs_0_, f32[96,384]{1,0:T(8,128)S(1)} %shard_map.77.refs_1_, bf16[2048,384]{1,0:T(8,128)(2,1)S(1)} %get-tuple-element.45.refs_3_.refs_2_, bf16[2048,384]{1,0:T(8,128)(2,1)S(1)} %get-tuple-element.46.refs_4_.refs_3_), custom_call_target="tpu_custom_call" | custom-call | bytes 3500 | tf_op jit(solution)/shard_map/pallas_call | solution.py:307
  28.8 0.1 collective-permute-start.7
  28.9 1.3 %collective-permute-done.7 = f32[64,384]{1,0:T(8,128)S(1)} collective-permute-done((f32[64,384]{1,0:T(8,128)S(1)}, f32[64,384]{1,0:T(8,128)S(1)}, u32[]{:S(2)}, u32[]{:S(2)}) %collective-permute-start.7) | collective-permute-done | bytes 98336 | tf_op jit(solution)/shard_map/ppermute | solution.py:20
  30.2 1.6 %collective-permute-start.8 = (f32[64,384]{1,0:T(8,128)S(1)}, f32[64,384]{1,0:T(8,128)S(1)}, u32[]{:S(2)}, u32[]{:S(2)}) collective-permute-start(f32[64,384]{1,0:T(8,128)S(1)} %add.28), channel_id=1, source_target_pairs={{0,2},{1,3},{2,0},{3,1},{4,6},{5,7},{6,4},{7,5},{8,10},{9,11},{10,... | collective-permute-start | bytes 294920 | tf_op jit(solution)/shard_map/ppermute | solution.py:20
  31.8 3.4 %collective-permute-done.8 = f32[64,384]{1,0:T(8,128)S(1)} collective-permute-done((f32[64,384]{1,0:T(8,128)S(1)}, f32[64,384]{1,0:T(8,128)S(1)}, u32[]{:S(2)}, u32[]{:S(2)}) %collective-permute-start.8) | collective-permute-done | bytes 98336 | tf_op jit(solution)/shard_map/ppermute | solution.py:20
  35.2 3.8 %collective-permute-start.9 = (f32[64,384]{1,0:T(8,128)S(1)}, f32[64,384]{1,0:T(8,128)S(1)}, u32[]{:S(2)}, u32[]{:S(2)}) collective-permute-start(f32[64,384]{1,0:T(8,128)S(1)} %add.29), channel_id=1, source_target_pairs={{0,4},{4,0},{8,12},{12,8},{1,5},{5,1},{9,13},{13,9},{2,6},{6,2},{1... | collective-permute-start | bytes 294920 | tf_op jit(solution)/shard_map/ppermute | solution.py:20
  39.0 2.6 %collective-permute-done.9 = f32[64,384]{1,0:T(8,128)S(1)} collective-permute-done((f32[64,384]{1,0:T(8,128)S(1)}, f32[64,384]{1,0:T(8,128)S(1)}, u32[]{:S(2)}, u32[]{:S(2)}) %collective-permute-start.9) | collective-permute-done | bytes 98336 | tf_op jit(solution)/shard_map/ppermute | solution.py:20
  41.6 2.5 %collective-permute-start.10 = (f32[64,384]{1,0:T(8,128)S(1)}, f32[64,384]{1,0:T(8,128)S(1)}, u32[]{:S(2)}, u32[]{:S(2)}) collective-permute-start(f32[64,384]{1,0:T(8,128)S(1)} %add.30), channel_id=1, source_target_pairs={{0,8},{4,12},{8,0},{12,4},{1,9},{5,13},{9,1},{13,5},{2,10},{6,14},... | collective-permute-start | bytes 294920 | tf_op jit(solution)/shard_map/ppermute | solution.py:20
  44.1 0.5 shard_map.79
  44.6 2.6 %collective-permute-done.10 = f32[64,384]{1,0:T(8,128)S(1)} collective-permute-done((f32[64,384]{1,0:T(8,128)S(1)}, f32[64,384]{1,0:T(8,128)S(1)}, u32[]{:S(2)}, u32[]{:S(2)}) %collective-permute-start.10) | collective-permute-done | bytes 98336 | tf_op jit(solution)/shard_map/ppermute | solution.py:20
  47.2 0.1 collective-permute-start.12
  47.3 0.2 shard_map.80.base
  47.6 1.0 %collective-permute-done.12.other = f32[64,384]{1,0:T(8,128)S(1)} collective-permute-done((f32[64,384]{1,0:T(8,128)S(1)}, f32[64,384]{1,0:T(8,128)S(1)}, u32[]{:S(2)}, u32[]{:S(2)}) %collective-permute-start.12) | collective-permute-done | bytes 98336 | tf_op jit(solution)/shard_map/ppermute | solution.py:20
  48.6 1.0 %shard_map.81 = f32[192,384]{1,0:T(8,128)} custom-call(bf16[192,128]{1,0:T(8,128)(2,1)S(1)} %get-tuple-element.52.high, bf16[192,128]{1,0:T(8,128)(2,1)S(1)} %get-tuple-element.53.low, f32[192,384]{1,0:T(8,128)S(1)} %shard_map.80.base, f32[64,384]{1,0:T(8,128)S(1)} %collective-permute-done.12.other), custom_call_target="tpu_custom_call" | custom-call | tf_op jit(solution)/shard_map/pallas_call | solution.py:412
  (24 shorter events, 0.1 us)
Async XLA Ops:
  0.0 7.9 %copy-start.3 = (s32[1,1,4,8]{3,2,1,0:T(4,128)S(1)}, s32[1,1,4,8]{3,2,1,0:T(4,128)}, u32[]{:S(2)}) copy-start(s32[1,1,4,8]{3,2,1,0:T(4,128)} %src_rows) | copy-start | bytes 388
  0.0 7.9 %copy-start.2 = (f32[1,1,6,4,8]{4,3,2,1,0:T(4,128)S(1)}, f32[1,1,6,4,8]{4,3,2,1,0:T(4,128)}, u32[]{:S(2)}) copy-start(f32[1,1,6,4,8]{4,3,2,1,0:T(4,128)} %weights.1) | copy-start | bytes 2308
  0.0 7.9 %copy-start.5 = (s32[1,1,4]{2,1,0:T(1,128)S(1)}, s32[1,1,4]{2,1,0:T(1,128)}, u32[]{:S(2)}) copy-start(s32[1,1,4]{2,1,0:T(1,128)} %counts.1) | copy-start | bytes 52
  0.0 7.9 %copy-start.4 = (s32[1,1,4,8]{3,2,1,0:T(4,128)S(1)}, s32[1,1,4,8]{3,2,1,0:T(4,128)}, u32[]{:S(2)}) copy-start(s32[1,1,4,8]{3,2,1,0:T(4,128)} %dst_nodes.1) | copy-start | bytes 388
  0.0 7.9 %copy-start.1 = (f32[6,8,192]{2,1,0:T(8,128)S(1)}, f32[6,8,192]{2,1,0:T(8,128)}, u32[]{:S(2)}) copy-start(f32[6,8,192]{2,1,0:T(8,128)} %modes.1) | copy-start | bytes 110596
  1.1 22.0 %collective-permute-start.5 = (f32[32,2048]{1,0:T(8,128)S(1)}, f32[32,2048]{1,0:T(8,128)S(1)}, u32[]{:S(2)}, u32[]{:S(2)}) collective-permute-start(f32[32,2048]{1,0:T(8,128)S(1)} %constant_dynamic-slice_fusion.3), channel_id=1, source_target_pairs={{0,8},{4,12},{8,0},{12,4},{1,9},{5,13},{9,1},{13,5},{2,10},{6,14},... | collective-permute-start | bytes 786440 | tf_op jit(solution)/shard_map/ppermute | solution.py:20
  6.2 16.8 %collective-permute-start.4 = (f32[32,2048]{1,0:T(8,128)S(1)}, f32[32,2048]{1,0:T(8,128)S(1)}, u32[]{:S(2)}, u32[]{:S(2)}) collective-permute-start(f32[32,2048]{1,0:T(8,128)S(1)} %get-tuple-element.34), channel_id=1, source_target_pairs={{0,4},{4,0},{8,12},{12,8},{1,5},{5,1},{9,13},{13,9},{2,6},{6,2},{1... | collective-permute-start | bytes 786440 | tf_op jit(solution)/shard_map/ppermute | solution.py:20
  9.0 10.6 %collective-permute-start.3 = (f32[30,128]{1,0:T(8,128)S(1)}, f32[30,128]{1,0:T(8,128)S(1)}, u32[]{:S(2)}, u32[]{:S(2)}) collective-permute-start(f32[30,128]{1,0:T(8,128)S(1)} %shard_map.73.refs_0_), channel_id=1, source_target_pairs={{0,4},{4,0},{8,12},{12,8},{1,5},{5,1},{9,13},{13,9},{2,6},{6,2},{1... | collective-permute-start | bytes 46088 | tf_op jit(solution)/shard_map/ppermute | solution.py:20
  9.4 13.6 %collective-permute-start.2 = (f32[30,128]{1,0:T(8,128)S(1)}, f32[30,128]{1,0:T(8,128)S(1)}, u32[]{:S(2)}, u32[]{:S(2)}) collective-permute-start(f32[30,128]{1,0:T(8,128)S(1)} %shard_map.73.refs_0_), channel_id=1, source_target_pairs={{0,8},{4,12},{8,0},{12,4},{1,9},{5,13},{9,1},{13,5},{2,10},{6,14},... | collective-permute-start | bytes 46088 | tf_op jit(solution)/shard_map/ppermute | solution.py:20
  9.5 13.6 %collective-permute-start.1 = (f32[30,128]{1,0:T(8,128)S(1)}, f32[30,128]{1,0:T(8,128)S(1)}, u32[]{:S(2)}, u32[]{:S(2)}) collective-permute-start(f32[30,128]{1,0:T(8,128)S(1)} %shard_map.73.refs_0_), channel_id=1, source_target_pairs={{0,12},{4,8},{8,4},{12,0},{1,13},{5,9},{9,5},{13,1},{2,14},{6,10},... | collective-permute-start | bytes 46088 | tf_op jit(solution)/shard_map/ppermute | solution.py:20
  19.6 8.7 %collective-permute-start = (f32[32,2048]{1,0:T(8,128)S(1)}, f32[32,2048]{1,0:T(8,128)S(1)}, u32[]{:S(2)}, u32[]{:S(2)}) collective-permute-start(f32[32,2048]{1,0:T(8,128)S(1)} %get-tuple-element.31), channel_id=1, source_target_pairs={{0,12},{4,8},{8,4},{12,0},{1,13},{5,9},{9,5},{13,1},{2,14},{6,10},... | collective-permute-start | bytes 786440 | tf_op jit(solution)/shard_map/ppermute | solution.py:20
  23.1 4.3 %collective-permute-start.6 = (f32[1,4,30,128]{3,2,1,0:T(8,128)S(1)}, f32[1,4,30,128]{3,2,1,0:T(8,128)S(1)}, u32[]{:S(2)}, u32[]{:S(2)}) collective-permute-start(f32[1,4,30,128]{3,2,1,0:T(8,128)S(1)} %bitcast.6), channel_id=1, source_target_pairs={{0,2},{1,3},{2,0},{3,1},{4,6},{5,7},{6,4},{7,5},{8,10},{9,11},{10,... | collective-permute-start | bytes 184328 | tf_op jit(solution)/shard_map/ppermute | solution.py:20
  24.6 1.9 %copy-start = (f32[1,2048,384]{2,1,0:T(8,128)S(1)}, f32[1,2048,384]{2,1,0:T(8,128)}, u32[]{:S(2)}) copy-start(f32[1,2048,384]{2,1,0:T(8,128)} %param.8) | copy-start | bytes 9437188
  28.8 1.4 %collective-permute-start.7 = (f32[64,384]{1,0:T(8,128)S(1)}, f32[64,384]{1,0:T(8,128)S(1)}, u32[]{:S(2)}, u32[]{:S(2)}) collective-permute-start(f32[64,384]{1,0:T(8,128)S(1)} %get-tuple-element.48), channel_id=1, source_target_pairs={{0,1},{1,0},{2,3},{3,2},{4,5},{5,4},{6,7},{7,6},{8,9},{9,8},{10,11... | collective-permute-start | bytes 294920 | tf_op jit(solution)/shard_map/ppermute | solution.py:20
  30.2 4.9 %collective-permute-start.8 = (f32[64,384]{1,0:T(8,128)S(1)}, f32[64,384]{1,0:T(8,128)S(1)}, u32[]{:S(2)}, u32[]{:S(2)}) collective-permute-start(f32[64,384]{1,0:T(8,128)S(1)} %add.28), channel_id=1, source_target_pairs={{0,2},{1,3},{2,0},{3,1},{4,6},{5,7},{6,4},{7,5},{8,10},{9,11},{10,... | collective-permute-start | bytes 294920 | tf_op jit(solution)/shard_map/ppermute | solution.py:20
  31.8 12.3 %collective-permute-start.11 = (f32[2,4,30,128]{3,2,1,0:T(8,128)S(1)}, f32[2,4,30,128]{3,2,1,0:T(8,128)S(1)}, u32[]{:S(2)}, u32[]{:S(2)}) collective-permute-start(f32[2,4,30,128]{3,2,1,0:T(8,128)S(1)} %bitcast.4), channel_id=1, source_target_pairs={{0,1},{1,0},{2,3},{3,2},{4,5},{5,4},{6,7},{7,6},{8,9},{9,8},{10,11... | collective-permute-start | bytes 368648 | tf_op jit(solution)/shard_map/ppermute | solution.py:20
  35.2 6.4 %collective-permute-start.9 = (f32[64,384]{1,0:T(8,128)S(1)}, f32[64,384]{1,0:T(8,128)S(1)}, u32[]{:S(2)}, u32[]{:S(2)}) collective-permute-start(f32[64,384]{1,0:T(8,128)S(1)} %add.29), channel_id=1, source_target_pairs={{0,4},{4,0},{8,12},{12,8},{1,5},{5,1},{9,13},{13,9},{2,6},{6,2},{1... | collective-permute-start | bytes 294920 | tf_op jit(solution)/shard_map/ppermute | solution.py:20
  41.6 5.6 %collective-permute-start.10 = (f32[64,384]{1,0:T(8,128)S(1)}, f32[64,384]{1,0:T(8,128)S(1)}, u32[]{:S(2)}, u32[]{:S(2)}) collective-permute-start(f32[64,384]{1,0:T(8,128)S(1)} %add.30), channel_id=1, source_target_pairs={{0,8},{4,12},{8,0},{12,4},{1,9},{5,13},{9,1},{13,5},{2,10},{6,14},... | collective-permute-start | bytes 294920 | tf_op jit(solution)/shard_map/ppermute | solution.py:20
  47.2 1.4 %collective-permute-start.12 = (f32[64,384]{1,0:T(8,128)S(1)}, f32[64,384]{1,0:T(8,128)S(1)}, u32[]{:S(2)}, u32[]{:S(2)}) collective-permute-start(f32[64,384]{1,0:T(8,128)S(1)} %maximum_add_fusion.total), channel_id=1, source_target_pairs={{0,1},{1,0},{2,3},{3,2},{4,5},{5,4},{6,7},{7,6},{8,9},{9,8},{10,11... | collective-permute-start | bytes 294920 | tf_op jit(solution)/shard_map/ppermute | solution.py:20

commit v6 on v4

--- a/solution.py
+++ b/solution.py
@@ -359,8 +359,10 @@
     )(lists, dst_nodes, counts, spline_weights, node_modes)
     last = swap(last, "blk", far_masks[-1])
     packs = [pack] + [swap(pack, "blk", mask) for mask in range(1, blk_count)]
-    waiting = lax.optimization_barrier((*packs[::-1], *near, *far))
-    packs, near, far = waiting[:blk_count][::-1], waiting[blk_count : blk_count + half], waiting[blk_count + half :]
+    order = [2, 3, 1, 0]
+    waiting = lax.optimization_barrier((*[packs[mask] for mask in order], *near, *far))
+    packs = [waiting[order.index(mask)] for mask in range(blk_count)]
+    near, far = waiting[blk_count : blk_count + half], waiting[blk_count + half :]
     packs = joined(*packs)[None]
     for mask in masks("col")[:0:-1]:
         packs = joined(packs, swap(packs, "col", mask)).reshape(-1, *packs.shape[1:])

time: 49.8 us -> 49.8 us (level)
  starting transfers between devices: 22.2 us -> 21.3 us
  waiting for transfers between devices: 17.5 us -> 18.4 us
    ppermute x13, waiting for transfers between devices: 17.5 us -> 18.4 us  [swap(): return lax.ppermute(value, axis, pairs)]
    ppermute x13, starting transfers between devices: 22.2 us -> 21.3 us  [swap(): return lax.ppermute(value, axis, pairs)]
where the time goes in v6:
time: 49.8 us; the launch traced here: 49.6 us
  starting transfers between devices  21.3 us (43%)
  waiting for transfers between devices  18.4 us (37%)
  local copies, waits for them, and re-layouts  4.98 us (10%)
  Pallas kernels  4.62 us (9%)
    ppermute x13, starting transfers between devices, swap(): return lax.ppermute(value, axis, pairs)  21.3 us
    ppermute x13, waiting for transfers between devices, swap(): return lax.ppermute(value, axis, pairs)  18.4 us
    dynamic_slice x3, local copies, waits for them, and re-layouts, columns(): return lax.dynamic_slice_in_dim(source, (blk ^ mask) * panels, panels, 1)  3.06 us
    unnamed x12, local copies, waits for them, and re-layouts  1.91 us
    pallas_call x1, Pallas kernels, shards(): pl.pallas_call(spline_kernel, out_shape=f32(folded(sub_rows) + folded(sha...  1.06 us
  transfers between devices with their start and end apart: 13, of which 7 were waited for; matrix products, arithmetic and copies ran while one was open for 4% of the time, Pallas kernels for 6%

profile of v6, /device:TPU:0, one launch (start us, length us, event | category | flops | bytes accessed | tf_op | source)
XLA Modules:
  0.0 49.6 jit_solution(15812243355023830511)
XLA Ops:
  0.0 1.0 %constant_dynamic-slice_fusion.3 = f32[32,2048]{1,0:T(8,128)S(1)} fusion(f32[32,8192]{1,0:T(8,128)} %param.7, s32[]{:T(128)S(6)} %select_n.12), kind=kLoop, calls=%fused_computation.5 | loop fusion | bytes 524292 | tf_op jit(solution)/shard_map/dynamic_slice | solution.py:339
  1.1 4.1 %collective-permute-start.5 = (f32[32,2048]{1,0:T(8,128)S(1)}, f32[32,2048]{1,0:T(8,128)S(1)}, u32[]{:S(2)}, u32[]{:S(2)}) collective-permute-start(f32[32,2048]{1,0:T(8,128)S(1)} %constant_dynamic-slice_fusion.3), channel_id=1, source_target_pairs={{0,8},{4,12},{8,0},{12,4},{1,9},{5,13},{9,1},{13,5},{2,10},{6,14},... | collective-permute-start | bytes 786440 | tf_op jit(solution)/shard_map/ppermute | solution.py:20
  5.2 1.1 %constant_dynamic-slice_fusion.1 = (f32[32,2048]{1,0:T(8,128)S(1)}, f32[32,2048]{1,0:T(8,128)S(1)}) fusion(f32[32,8192]{1,0:T(8,128)} %param.7, s32[]{:T(128)S(6)} %select_n.14, s32[]{:T(128)S(6)} %select_n.13), kind=kLoop, calls=%fused_computation.3 | loop fusion | bytes 1048584 | tf_op jit(solution)/shard_map/dynamic_slice | solution.py:339
  6.2 1.6 %collective-permute-start.4 = (f32[32,2048]{1,0:T(8,128)S(1)}, f32[32,2048]{1,0:T(8,128)S(1)}, u32[]{:S(2)}, u32[]{:S(2)}) collective-permute-start(f32[32,2048]{1,0:T(8,128)S(1)} %get-tuple-element.34), channel_id=1, source_target_pairs={{0,4},{4,0},{8,12},{12,8},{1,5},{5,1},{9,13},{13,9},{2,6},{6,2},{1... | collective-permute-start | bytes 786440 | tf_op jit(solution)/shard_map/ppermute | solution.py:20
  7.9 1.1 %shard_map.73.refs_0_ = f32[30,128]{1,0:T(8,128)S(1)} custom-call(s32[1,1,4,8]{3,2,1,0:T(4,128)S(1)} %copy-done.3, s32[1,1,4,8]{3,2,1,0:T(4,128)S(1)} %copy-done.4, s32[1,1,4]{2,1,0:T(1,128)S(1)} %copy-done.5, f32[1,1,6,4,8]{4,3,2,1,0:T(4,128)S(1)} %copy-done.2, f32[6,8,192]{2,1,0:T(8,128)S(1)} %copy-done.1), custom_call_target="tpu_custom_call" | custom-call | bytes 3500 | tf_op jit(solution)/shard_map/pallas_call | solution.py:352
  9.0 0.5 collective-permute-start.3
  9.4 1.3 %collective-permute-start.2 = (f32[30,128]{1,0:T(8,128)S(1)}, f32[30,128]{1,0:T(8,128)S(1)}, u32[]{:S(2)}, u32[]{:S(2)}) collective-permute-start(f32[30,128]{1,0:T(8,128)S(1)} %shard_map.73.refs_0_), channel_id=1, source_target_pairs={{0,12},{4,8},{8,4},{12,0},{1,13},{5,9},{9,5},{13,1},{2,14},{6,10},... | collective-permute-start | bytes 46088 | tf_op jit(solution)/shard_map/ppermute | solution.py:20
  10.8 1.7 %collective-permute-start.1 = (f32[30,128]{1,0:T(8,128)S(1)}, f32[30,128]{1,0:T(8,128)S(1)}, u32[]{:S(2)}, u32[]{:S(2)}) collective-permute-start(f32[30,128]{1,0:T(8,128)S(1)} %shard_map.73.refs_0_), channel_id=1, source_target_pairs={{0,8},{4,12},{8,0},{12,4},{1,9},{5,13},{9,1},{13,5},{2,10},{6,14},... | collective-permute-start | bytes 46088 | tf_op jit(solution)/shard_map/ppermute | solution.py:20
  12.5 7.1 %collective-permute-done.3.refs_1_ = f32[30,128]{1,0:T(8,128)S(1)} collective-permute-done((f32[30,128]{1,0:T(8,128)S(1)}, f32[30,128]{1,0:T(8,128)S(1)}, u32[]{:S(2)}, u32[]{:S(2)}) %collective-permute-start.3) | collective-permute-done | bytes 15392 | tf_op jit(solution)/shard_map/ppermute | solution.py:20
  19.6 2.2 %collective-permute-start = (f32[32,2048]{1,0:T(8,128)S(1)}, f32[32,2048]{1,0:T(8,128)S(1)}, u32[]{:S(2)}, u32[]{:S(2)}) collective-permute-start(f32[32,2048]{1,0:T(8,128)S(1)} %get-tuple-element.31), channel_id=1, source_target_pairs={{0,12},{4,8},{8,4},{12,0},{1,13},{5,9},{9,5},{13,1},{2,14},{6,10},... | collective-permute-start | bytes 786440 | tf_op jit(solution)/shard_map/ppermute | solution.py:20
  21.8 1.0 %constant_dynamic-slice_fusion.refs_0_ = f32[32,2048]{1,0:T(8,128)S(1)} fusion(f32[32,8192]{1,0:T(8,128)} %param.7, s32[]{:T(128)S(6)} %select_n.15), kind=kLoop, calls=%fused_computation.2 | loop fusion | bytes 524292 | tf_op jit(solution)/shard_map/dynamic_slice | solution.py:339
  22.8 0.0 collective-permute-done.2.refs_3_
  22.8 0.0 collective-permute-done.5.refs_2_
  22.8 0.0 collective-permute-done.4.refs_1_
  22.8 1.6 %collective-permute-start.6 = (f32[1,4,30,128]{3,2,1,0:T(8,128)S(1)}, f32[1,4,30,128]{3,2,1,0:T(8,128)S(1)}, u32[]{:S(2)}, u32[]{:S(2)}) collective-permute-start(f32[1,4,30,128]{3,2,1,0:T(8,128)S(1)} %bitcast.6), channel_id=1, source_target_pairs={{0,2},{1,3},{2,0},{3,1},{4,6},{5,7},{6,4},{7,5},{8,10},{9,11},{10,... | collective-permute-start | bytes 184328 | tf_op jit(solution)/shard_map/ppermute | solution.py:20
  24.4 1.9 %copy-done = f32[1,2048,384]{2,1,0:T(8,128)S(1)} copy-done((f32[1,2048,384]{2,1,0:T(8,128)S(1)}, f32[1,2048,384]{2,1,0:T(8,128)}, u32[]{:S(2)}) %copy-start) | copy-done | bytes 3145752
  26.3 0.7 %shard_map.76 = (bf16[2048,384]{1,0:T(8,128)(2,1)S(1)}, bf16[2048,384]{1,0:T(8,128)(2,1)S(1)}) custom-call(f32[2048,384]{1,0:T(8,128)S(1)} %bitcast.3), custom_call_target="tpu_custom_call" | custom-call | bytes 3500 | tf_op jit(solution)/shard_map/pallas_call | solution.py:236
  27.0 0.2 collective-permute-done.6.refs_1_
  27.2 0.8 %shard_map.77.refs_1_ = f32[96,384]{1,0:T(8,128)S(1)} custom-call(f32[32,2048]{1,0:T(8,128)S(1)} %constant_dynamic-slice_fusion.refs_0_, f32[32,2048]{1,0:T(8,128)S(1)} %collective-permute-done.4.refs_1_, f32[32,2048]{1,0:T(8,128)S(1)} %collective-permute-done.5.refs_2_, bf16[2048,384]{1,0:T(8,128)(2,1)S(1)} %get-tuple-element.45.refs_3_.refs_2_, ...), custom_call_target="tpu_custom_call" | custom-call | bytes 3500 | tf_op jit(solution)/shard_map/pallas_call | solution.py:284
  28.0 0.6 %shard_map.78 = (f32[64,384]{1,0:T(8,128)S(1)}, f32[64,384]{1,0:T(8,128)S(1)}) custom-call(f32[32,2048]{1,0:T(8,128)S(1)} %collective-permute-done.refs_0_, f32[96,384]{1,0:T(8,128)S(1)} %shard_map.77.refs_1_, bf16[2048,384]{1,0:T(8,128)(2,1)S(1)} %get-tuple-element.45.refs_3_.refs_2_, bf16[2048,384]{1,0:T(8,128)(2,1)S(1)} %get-tuple-element.46.refs_4_.refs_3_), custom_call_target="tpu_custom_call" | custom-call | bytes 3500 | tf_op jit(solution)/shard_map/pallas_call | solution.py:297
  28.6 0.1 collective-permute-start.7
  28.7 1.3 %collective-permute-done.7 = f32[64,384]{1,0:T(8,128)S(1)} collective-permute-done((f32[64,384]{1,0:T(8,128)S(1)}, f32[64,384]{1,0:T(8,128)S(1)}, u32[]{:S(2)}, u32[]{:S(2)}) %collective-permute-start.7) | collective-permute-done | bytes 98336 | tf_op jit(solution)/shard_map/ppermute | solution.py:20
  30.0 1.6 %collective-permute-start.8 = (f32[64,384]{1,0:T(8,128)S(1)}, f32[64,384]{1,0:T(8,128)S(1)}, u32[]{:S(2)}, u32[]{:S(2)}) collective-permute-start(f32[64,384]{1,0:T(8,128)S(1)} %add.28), channel_id=1, source_target_pairs={{0,2},{1,3},{2,0},{3,1},{4,6},{5,7},{6,4},{7,5},{8,10},{9,11},{10,... | collective-permute-start | bytes 294920 | tf_op jit(solution)/shard_map/ppermute | solution.py:20
  31.6 3.3 %collective-permute-done.8 = f32[64,384]{1,0:T(8,128)S(1)} collective-permute-done((f32[64,384]{1,0:T(8,128)S(1)}, f32[64,384]{1,0:T(8,128)S(1)}, u32[]{:S(2)}, u32[]{:S(2)}) %collective-permute-start.8) | collective-permute-done | bytes 98336 | tf_op jit(solution)/shard_map/ppermute | solution.py:20
  34.9 4.1 %collective-permute-start.9 = (f32[64,384]{1,0:T(8,128)S(1)}, f32[64,384]{1,0:T(8,128)S(1)}, u32[]{:S(2)}, u32[]{:S(2)}) collective-permute-start(f32[64,384]{1,0:T(8,128)S(1)} %add.29), channel_id=1, source_target_pairs={{0,4},{4,0},{8,12},{12,8},{1,5},{5,1},{9,13},{13,9},{2,6},{6,2},{1... | collective-permute-start | bytes 294920 | tf_op jit(solution)/shard_map/ppermute | solution.py:20
  39.0 2.6 %collective-permute-done.9 = f32[64,384]{1,0:T(8,128)S(1)} collective-permute-done((f32[64,384]{1,0:T(8,128)S(1)}, f32[64,384]{1,0:T(8,128)S(1)}, u32[]{:S(2)}, u32[]{:S(2)}) %collective-permute-start.9) | collective-permute-done | bytes 98336 | tf_op jit(solution)/shard_map/ppermute | solution.py:20
  41.6 2.5 %collective-permute-start.10 = (f32[64,384]{1,0:T(8,128)S(1)}, f32[64,384]{1,0:T(8,128)S(1)}, u32[]{:S(2)}, u32[]{:S(2)}) collective-permute-start(f32[64,384]{1,0:T(8,128)S(1)} %add.30), channel_id=1, source_target_pairs={{0,8},{4,12},{8,0},{12,4},{1,9},{5,13},{9,1},{13,5},{2,10},{6,14},... | collective-permute-start | bytes 294920 | tf_op jit(solution)/shard_map/ppermute | solution.py:20
  44.1 0.5 shard_map.79
  44.6 2.6 %collective-permute-done.10 = f32[64,384]{1,0:T(8,128)S(1)} collective-permute-done((f32[64,384]{1,0:T(8,128)S(1)}, f32[64,384]{1,0:T(8,128)S(1)}, u32[]{:S(2)}, u32[]{:S(2)}) %collective-permute-start.10) | collective-permute-done | bytes 98336 | tf_op jit(solution)/shard_map/ppermute | solution.py:20
  47.2 0.1 collective-permute-start.12
  47.3 1.3 %collective-permute-done.12.other = f32[64,384]{1,0:T(8,128)S(1)} collective-permute-done((f32[64,384]{1,0:T(8,128)S(1)}, f32[64,384]{1,0:T(8,128)S(1)}, u32[]{:S(2)}, u32[]{:S(2)}) %collective-permute-start.12) | collective-permute-done | bytes 98336 | tf_op jit(solution)/shard_map/ppermute | solution.py:20
  48.6 1.0 %shard_map.80 = f32[192,384]{1,0:T(8,128)} custom-call(bf16[192,128]{1,0:T(8,128)(2,1)S(1)} %get-tuple-element.52.high, bf16[192,128]{1,0:T(8,128)(2,1)S(1)} %get-tuple-element.53.low, f32[64,384]{1,0:T(8,128)S(1)} %maximum_add_fusion.total, f32[64,384]{1,0:T(8,128)S(1)} %collective-permute-done.12.other), custom_call_target="tpu_custom_call" | custom-call | tf_op jit(solution)/shard_map/pallas_call | solution.py:396
  (23 shorter events, 0.1 us)
Async XLA Ops:
  0.0 7.9 %copy-start.3 = (s32[1,1,4,8]{3,2,1,0:T(4,128)S(1)}, s32[1,1,4,8]{3,2,1,0:T(4,128)}, u32[]{:S(2)}) copy-start(s32[1,1,4,8]{3,2,1,0:T(4,128)} %src_rows) | copy-start | bytes 388
  0.0 7.9 %copy-start.2 = (f32[1,1,6,4,8]{4,3,2,1,0:T(4,128)S(1)}, f32[1,1,6,4,8]{4,3,2,1,0:T(4,128)}, u32[]{:S(2)}) copy-start(f32[1,1,6,4,8]{4,3,2,1,0:T(4,128)} %weights.1) | copy-start | bytes 2308
  0.0 7.9 %copy-start.5 = (s32[1,1,4]{2,1,0:T(1,128)S(1)}, s32[1,1,4]{2,1,0:T(1,128)}, u32[]{:S(2)}) copy-start(s32[1,1,4]{2,1,0:T(1,128)} %counts.1) | copy-start | bytes 52
  0.0 7.9 %copy-start.4 = (s32[1,1,4,8]{3,2,1,0:T(4,128)S(1)}, s32[1,1,4,8]{3,2,1,0:T(4,128)}, u32[]{:S(2)}) copy-start(s32[1,1,4,8]{3,2,1,0:T(4,128)} %dst_nodes.1) | copy-start | bytes 388
  0.0 7.9 %copy-start.1 = (f32[6,8,192]{2,1,0:T(8,128)S(1)}, f32[6,8,192]{2,1,0:T(8,128)}, u32[]{:S(2)}) copy-start(f32[6,8,192]{2,1,0:T(8,128)} %modes.1) | copy-start | bytes 110596
  1.1 21.7 %collective-permute-start.5 = (f32[32,2048]{1,0:T(8,128)S(1)}, f32[32,2048]{1,0:T(8,128)S(1)}, u32[]{:S(2)}, u32[]{:S(2)}) collective-permute-start(f32[32,2048]{1,0:T(8,128)S(1)} %constant_dynamic-slice_fusion.3), channel_id=1, source_target_pairs={{0,8},{4,12},{8,0},{12,4},{1,9},{5,13},{9,1},{13,5},{2,10},{6,14},... | collective-permute-start | bytes 786440 | tf_op jit(solution)/shard_map/ppermute | solution.py:20
  6.2 16.6 %collective-permute-start.4 = (f32[32,2048]{1,0:T(8,128)S(1)}, f32[32,2048]{1,0:T(8,128)S(1)}, u32[]{:S(2)}, u32[]{:S(2)}) collective-permute-start(f32[32,2048]{1,0:T(8,128)S(1)} %get-tuple-element.34), channel_id=1, source_target_pairs={{0,4},{4,0},{8,12},{12,8},{1,5},{5,1},{9,13},{13,9},{2,6},{6,2},{1... | collective-permute-start | bytes 786440 | tf_op jit(solution)/shard_map/ppermute | solution.py:20
  9.0 10.6 %collective-permute-start.3 = (f32[30,128]{1,0:T(8,128)S(1)}, f32[30,128]{1,0:T(8,128)S(1)}, u32[]{:S(2)}, u32[]{:S(2)}) collective-permute-start(f32[30,128]{1,0:T(8,128)S(1)} %shard_map.73.refs_0_), channel_id=1, source_target_pairs={{0,4},{4,0},{8,12},{12,8},{1,5},{5,1},{9,13},{13,9},{2,6},{6,2},{1... | collective-permute-start | bytes 46088 | tf_op jit(solution)/shard_map/ppermute | solution.py:20
  9.4 13.3 %collective-permute-start.2 = (f32[30,128]{1,0:T(8,128)S(1)}, f32[30,128]{1,0:T(8,128)S(1)}, u32[]{:S(2)}, u32[]{:S(2)}) collective-permute-start(f32[30,128]{1,0:T(8,128)S(1)} %shard_map.73.refs_0_), channel_id=1, source_target_pairs={{0,12},{4,8},{8,4},{12,0},{1,13},{5,9},{9,5},{13,1},{2,14},{6,10},... | collective-permute-start | bytes 46088 | tf_op jit(solution)/shard_map/ppermute | solution.py:20
  10.8 12.0 %collective-permute-start.1 = (f32[30,128]{1,0:T(8,128)S(1)}, f32[30,128]{1,0:T(8,128)S(1)}, u32[]{:S(2)}, u32[]{:S(2)}) collective-permute-start(f32[30,128]{1,0:T(8,128)S(1)} %shard_map.73.refs_0_), channel_id=1, source_target_pairs={{0,8},{4,12},{8,0},{12,4},{1,9},{5,13},{9,1},{13,5},{2,10},{6,14},... | collective-permute-start | bytes 46088 | tf_op jit(solution)/shard_map/ppermute | solution.py:20
  19.6 8.4 %collective-permute-start = (f32[32,2048]{1,0:T(8,128)S(1)}, f32[32,2048]{1,0:T(8,128)S(1)}, u32[]{:S(2)}, u32[]{:S(2)}) collective-permute-start(f32[32,2048]{1,0:T(8,128)S(1)} %get-tuple-element.31), channel_id=1, source_target_pairs={{0,12},{4,8},{8,4},{12,0},{1,13},{5,9},{9,5},{13,1},{2,14},{6,10},... | collective-permute-start | bytes 786440 | tf_op jit(solution)/shard_map/ppermute | solution.py:20
  22.8 4.3 %collective-permute-start.6 = (f32[1,4,30,128]{3,2,1,0:T(8,128)S(1)}, f32[1,4,30,128]{3,2,1,0:T(8,128)S(1)}, u32[]{:S(2)}, u32[]{:S(2)}) collective-permute-start(f32[1,4,30,128]{3,2,1,0:T(8,128)S(1)} %bitcast.6), channel_id=1, source_target_pairs={{0,2},{1,3},{2,0},{3,1},{4,6},{5,7},{6,4},{7,5},{8,10},{9,11},{10,... | collective-permute-start | bytes 184328 | tf_op jit(solution)/shard_map/ppermute | solution.py:20
  24.4 1.9 %copy-start = (f32[1,2048,384]{2,1,0:T(8,128)S(1)}, f32[1,2048,384]{2,1,0:T(8,128)}, u32[]{:S(2)}) copy-start(f32[1,2048,384]{2,1,0:T(8,128)} %param.8) | copy-start | bytes 9437188
  28.6 1.4 %collective-permute-start.7 = (f32[64,384]{1,0:T(8,128)S(1)}, f32[64,384]{1,0:T(8,128)S(1)}, u32[]{:S(2)}, u32[]{:S(2)}) collective-permute-start(f32[64,384]{1,0:T(8,128)S(1)} %get-tuple-element.48), channel_id=1, source_target_pairs={{0,1},{1,0},{2,3},{3,2},{4,5},{5,4},{6,7},{7,6},{8,9},{9,8},{10,11... | collective-permute-start | bytes 294920 | tf_op jit(solution)/shard_map/ppermute | solution.py:20
  30.0 4.9 %collective-permute-start.8 = (f32[64,384]{1,0:T(8,128)S(1)}, f32[64,384]{1,0:T(8,128)S(1)}, u32[]{:S(2)}, u32[]{:S(2)}) collective-permute-start(f32[64,384]{1,0:T(8,128)S(1)} %add.28), channel_id=1, source_target_pairs={{0,2},{1,3},{2,0},{3,1},{4,6},{5,7},{6,4},{7,5},{8,10},{9,11},{10,... | collective-permute-start | bytes 294920 | tf_op jit(solution)/shard_map/ppermute | solution.py:20
  31.6 12.5 %collective-permute-start.11 = (f32[2,4,30,128]{3,2,1,0:T(8,128)S(1)}, f32[2,4,30,128]{3,2,1,0:T(8,128)S(1)}, u32[]{:S(2)}, u32[]{:S(2)}) collective-permute-start(f32[2,4,30,128]{3,2,1,0:T(8,128)S(1)} %bitcast.4), channel_id=1, source_target_pairs={{0,1},{1,0},{2,3},{3,2},{4,5},{5,4},{6,7},{7,6},{8,9},{9,8},{10,11... | collective-permute-start | bytes 368648 | tf_op jit(solution)/shard_map/ppermute | solution.py:20
  34.9 6.7 %collective-permute-start.9 = (f32[64,384]{1,0:T(8,128)S(1)}, f32[64,384]{1,0:T(8,128)S(1)}, u32[]{:S(2)}, u32[]{:S(2)}) collective-permute-start(f32[64,384]{1,0:T(8,128)S(1)} %add.29), channel_id=1, source_target_pairs={{0,4},{4,0},{8,12},{12,8},{1,5},{5,1},{9,13},{13,9},{2,6},{6,2},{1... | collective-permute-start | bytes 294920 | tf_op jit(solution)/shard_map/ppermute | solution.py:20
  41.6 5.6 %collective-permute-start.10 = (f32[64,384]{1,0:T(8,128)S(1)}, f32[64,384]{1,0:T(8,128)S(1)}, u32[]{:S(2)}, u32[]{:S(2)}) collective-permute-start(f32[64,384]{1,0:T(8,128)S(1)} %add.30), channel_id=1, source_target_pairs={{0,8},{4,12},{8,0},{12,4},{1,9},{5,13},{9,1},{13,5},{2,10},{6,14},... | collective-permute-start | bytes 294920 | tf_op jit(solution)/shard_map/ppermute | solution.py:20
  47.2 1.4 %collective-permute-start.12 = (f32[64,384]{1,0:T(8,128)S(1)}, f32[64,384]{1,0:T(8,128)S(1)}, u32[]{:S(2)}, u32[]{:S(2)}) collective-permute-start(f32[64,384]{1,0:T(8,128)S(1)} %maximum_add_fusion.total), channel_id=1, source_target_pairs={{0,1},{1,0},{2,3},{3,2},{4,5},{5,4},{6,7},{7,6},{8,9},{9,8},{10,11... | collective-permute-start | bytes 294920 | tf_op jit(solution)/shard_map/ppermute | solution.py:20
